TPU v7x, 256 devices: a whole 4x4x8 slice. The times are simulated.
256 devices in a mesh: dp: 32 (over z, x), cent: 8 (over y, core).
Axes of the slice: x: 4, y: 4, z: 8, core: 2. Of those that a mesh axis runs over, the one named last changes fastest.
Arguments:
- embeddings: bfloat16 [32768, 768], P('dp'), may hold values from -2 to 2
- centroids: float32 [8192, 768], P(('dp', 'cent')), may hold values from -1 to 1
Outputs:
- new_centroids: float32 [8192, 768], P(('dp', 'cent'))
- counts: float32 [8192], P(('dp', 'cent'))
- row_lse: float32 [32768], P('dp')
All inputs are finite; a program needn't handle non-finite values.
Results may differ from a plain program's by a relative error of at most 0.02.
Values may be sent and summed in bfloat16 or wider, within the bound.
No kernel may reach another device: no remote copies, remote signals or barrier semaphores. Data moves between devices by JAX's collectives and lax.ppermute only.
A program may use at most 64 MiB of HBM per device.

v0:
```python
import jax
import jax.numpy as jnp
from jax import lax
from jax.sharding import PartitionSpec as P

ITERS = 2


sharpness = 50.0


def expect(embeddings, copy):
    squares = jnp.sum(jnp.square(copy.astype(jnp.float32)), axis=1)
    logits = (
        jnp.dot(embeddings, copy.T, preferred_element_type=jnp.float32) - 0.5 * squares
    ) * sharpness
    local_peak = jnp.max(logits, axis=1)
    global_peak = lax.pmax(local_peak, "cent")
    total = lax.psum(jnp.sum(jnp.exp(logits - global_peak[:, None]), axis=1), "cent")
    log_total = global_peak + jnp.log(total)
    resp = jnp.exp(logits - log_total[:, None]).astype(jnp.bfloat16)
    sums = lax.dot_general(
        resp, embeddings, (((0,), (0,)), ((), ())), preferred_element_type=jnp.float32
    )
    weights = jnp.sum(resp.astype(jnp.float32), axis=0)
    return (sums, weights, log_total)


def on_device(embeddings, centroids):
    own_rows = centroids.shape[0]
    whole = lax.all_gather(centroids, "dp", axis=0, tiled=True)
    for step in range(ITERS):
        copy = whole.astype(jnp.bfloat16)
        sums, weights, row_lse = expect(embeddings, copy)
        all_sums, all_counts = lax.psum((sums, weights), "dp")
        whole = (all_sums + whole) / (all_counts[:, None] + 1.0)
    start = lax.axis_index("dp") * own_rows
    current = lax.dynamic_slice_in_dim(whole, start, own_rows, 0)
    counts = lax.dynamic_slice_in_dim(all_counts, start, own_rows, 0)
    return (current, counts, row_lse)


def solution(mesh):
    in_specs = (P("dp", None), P(("dp", "cent"), None))
    out_specs = (P(("dp", "cent"), None), P(("dp", "cent")), P("dp"))
    return jax.shard_map(
        on_device, mesh=mesh, in_specs=in_specs, out_specs=out_specs, check_vma=False
    )
```

profile of v0, /device:TPU:2, one launch (start us, length us, event | category | flops | bytes accessed | tf_op | source)
XLA Modules:
  0.0 489.2 jit_solution(13829581031727526043)
XLA Ops:
  7.2 0.0 copy-start
  7.2 0.0 all-gather.2.cloned.1.call-start
  7.2 0.7 all-gather.2.cloned.1.call-update
  7.9 0.0 all-reduce.3.cloned.1.call-start
  8.0 84.3 %all-gather.2.cloned.1.call-done = f32[1024,768]{1,0:T(8,128)} async-done(((f32[32,768]{1,0:T(8,128)}), f32[1024,768]{1,0:T(8,128)}) %all-gather.2.cloned.1.call-update) | async-done | bytes 3145744 | tf_op jit(solution)/shard_map/all_gather | solution.py:31
  92.3 2.2 multiply_reduce_fusion.1
  94.4 0.0 copy-done
  94.4 5.6 %fusion = (f32[1024]{0:T(1024)S(1)}, f32[1024,1024]{0,1:T(8,128)}) fusion(f32[1024]{0:T(1024)S(1)} %broadcast_multiply_fusion.1, bf16[1024,768]{1,0:T(8,128)(2,1)S(1)} %copy-done, f32[1024,768]{1,0:T(8,128)} %all-gather.2.cloned.1.call-done), kind=kOutput, calls=%fused_computation.8 | convolution fusion | flops 1614543872 | bytes 8921088 | tf_op jit(solution)/shard_map/dot_general | solution.py:15
  100.1 12.4 %pmax.14 = f32[1024]{0:T(1024)S(1)} all-reduce(f32[1024]{0:T(1024)S(1)} %get-tuple-element.5), channel_id=1, replica_groups=mesh['dp'=32,'cent'=8] {'cent'}, use_global_device_ids=true, to_apply=%region_2.0 | all-reduce | flops 1024 | bytes 8192 | tf_op jit(solution)/shard_map/pmax | solution.py:18
  112.5 3.1 exponential_reduce_fusion.1
  115.6 12.4 %psum.42 = f32[1024]{0:T(1024)S(1)} all-reduce(f32[1024]{0:T(1024)S(1)} %exponential_reduce_fusion.1), channel_id=1, replica_groups=mesh['dp'=32,'cent'=8] {'cent'}, use_global_device_ids=true, to_apply=%region_4.0 | all-reduce | flops 1024 | bytes 8192 | tf_op jit(solution)/shard_map/psum | solution.py:19
  128.0 6.0 %fusion.7 = f32[1024,768]{1,0:T(8,128)} fusion(bf16[1024,768]{1,0:T(8,128)(2,1)S(1)} %copy-done, f32[1024,1024]{0,1:T(8,128)} %get-tuple-element.6, f32[1024]{0:T(1024)S(1)} %log_add_fusion.1, f32[1024]{0:T(1024)S(1)} %broadcast_multiply_fusion.1), kind=kOutput, calls=%fused_computation.25 | convolution fusion | flops 1614807040 | bytes 8921088 | tf_op jit(solution)/shard_map/dot_general | solution.py:22
  134.0 0.0 all-reduce.3.cloned.1.call-update
  134.1 0.0 all-reduce.5.cloned.1.call-start
  134.1 3.3 convert_reduce_fusion.1
  137.4 71.6 %psum.44 = f32[1024]{0:T(1024)S(1)} all-reduce(f32[1024]{0:T(1024)S(1)} %convert_reduce_fusion.1), channel_id=1, replica_groups=mesh['dp'=32,'cent'=8] {'dp'}, use_global_device_ids=true, to_apply=%region_7.0 | all-reduce | flops 1024 | bytes 8192 | tf_op jit(solution)/shard_map/psum | solution.py:35
  208.9 77.8 %all-reduce.3.cloned.1.call-done = f32[1024,768]{1,0:T(8,128)} async-done(((f32[1024,768]{1,0:T(8,128)}), f32[1024,768]{1,0:T(8,128)}) %all-reduce.3.cloned.1.call-update) | async-done | bytes 3145744 | tf_op jit(solution)/shard_map/psum | solution.py:35
  286.8 3.4 multiply_reduce_fusion
  290.2 3.8 fusion.1
  294.0 12.4 %pmax.15 = f32[1024]{0:T(1024)S(1)} all-reduce(f32[1024]{0:T(1024)S(1)} %get-tuple-element.7), channel_id=1, replica_groups=mesh['dp'=32,'cent'=8] {'cent'}, use_global_device_ids=true, to_apply=%region_10.0 | all-reduce | flops 1024 | bytes 8192 | tf_op jit(solution)/shard_map/pmax | solution.py:18
  306.4 3.2 exponential_reduce_fusion
  309.5 12.6 %psum.45 = f32[1024]{0:T(1024)S(1)} all-reduce(f32[1024]{0:T(1024)S(1)} %exponential_reduce_fusion), channel_id=1, replica_groups=mesh['dp'=32,'cent'=8] {'cent'}, use_global_device_ids=true, to_apply=%region_12.0 | all-reduce | flops 1024 | bytes 8192 | tf_op jit(solution)/shard_map/psum | solution.py:19
  322.1 0.0 copy-start.2
  322.2 6.0 %fusion.8 = f32[1024,768]{1,0:T(8,128)} fusion(bf16[1024,768]{1,0:T(8,128)(2,1)S(1)} %copy-done, f32[1024,1024]{0,1:T(8,128)} %get-tuple-element.8, f32[1024]{0:T(1024)S(1)} %log_add_fusion, f32[1024]{0:T(1024)S(1)} %broadcast_multiply_fusion), kind=kOutput, calls=%fused_computation.26 | convolution fusion | flops 1614807040 | bytes 8921088 | tf_op jit(solution)/shard_map/dot_general | solution.py:22
  328.2 0.0 all-reduce.5.cloned.1.call-update
  328.2 0.0 copy-done.2
  328.2 3.0 convert_reduce_fusion
  331.2 71.5 %psum.47 = f32[1024]{0:T(1024)S(1)} all-reduce(f32[1024]{0:T(1024)S(1)} %convert_reduce_fusion), channel_id=1, replica_groups=mesh['dp'=32,'cent'=8] {'dp'}, use_global_device_ids=true, to_apply=%region_15.0 | all-reduce | flops 1024 | bytes 8192 | tf_op jit(solution)/shard_map/psum | solution.py:35
  402.8 0.6 dynamic_slice.7
  403.4 0.1 dynamic-slice
  403.4 77.5 %all-reduce.5.cloned.1.call-done = f32[1024,768]{1,0:T(8,128)} async-done(((f32[1024,768]{1,0:T(8,128)}), f32[1024,768]{1,0:T(8,128)}) %all-reduce.5.cloned.1.call-update) | async-done | bytes 3145744 | tf_op jit(solution)/shard_map/psum | solution.py:35
  481.0 1.7 fusion.6
  (8 shorter events, 0.0 us)
Async XLA Ops:
  7.2 87.3 %copy-start = (bf16[1024,768]{1,0:T(8,128)(2,1)S(1)}, bf16[1024,768]{1,0:T(8,128)(2,1)}, u32[]{:S(2)}) copy-start(bf16[1024,768]{1,0:T(8,128)(2,1)} %param.2) | copy-start | bytes 4718596
  7.2 85.1 %all-gather.2.cloned.1.call-start = ((), (), s32[]{:S(2)}) async-start(), calls=%async_computation | async-start | bytes 3244032 | tf_op jit(solution)/shard_map/all_gather | solution.py:31
  7.9 278.9 %all-reduce.3.cloned.1.call-start = ((), (), s32[]{:S(2)}) async-start(), calls=%async_computation.1 | async-start | bytes 6291456 | tf_op jit(solution)/shard_map/psum | solution.py:35
  134.1 346.9 %all-reduce.5.cloned.1.call-start = ((), (), s32[]{:S(2)}) async-start(), calls=%async_computation.2 | async-start | bytes 6291456 | tf_op jit(solution)/shard_map/psum | solution.py:35
  290.2 3.8 copy-start.1
  322.1 6.0 %copy-start.2 = (f32[1024]{0:T(1024)}, f32[1024]{0:T(1024)S(1)}, u32[]{:S(2)}) copy-start(f32[1024]{0:T(1024)S(1)} %log_add_fusion) | copy-start | bytes 12292
Sparse Core Ops, SparseCore 0:
  10.6 81.6 all-gather.1
  134.2 152.5 all-reduce.2
  328.3 152.6 all-reduce.4
where the time goes:
time: 491 us; the launch traced here: 489 us
  waiting for transfers between devices  240 us (49%)
  blocking collectives  193 us (39%)
  matrix products  21.4 us (4%)
  other arithmetic  19.8 us (4%)
  between operations  13.9 us (3%)
    psum x2, waiting for transfers between devices, on_device(): all_sums, all_counts = lax.psum((sums, weights), 'dp')  155 us
    psum x2, blocking collectives, on_device(): all_sums, all_counts = lax.psum((sums, weights), 'dp')  143 us
    all_gather x1, waiting for transfers between devices, on_device(): whole = lax.all_gather(centroids, 'dp', axis=0, tiled=True)  84.3 us
    psum x2, blocking collectives, expect(): lax.psum(jnp.sum(jnp.exp(logits - global_peak[:, None]), axis=1), 'cent')  25 us
    pmax x2, blocking collectives, expect(): global_peak = lax.pmax(local_peak, 'cent')  24.8 us
    dot_general x2, matrix products, expect(): lax.dot_general(resp, embeddings, (((0,), (0,)), ((), ())), preferred_ele...  12 us
  transfers between devices with their start and end apart: 3, of which 3 were waited for; matrix products, arithmetic and copies ran while one was open for 1% of the time, Pallas kernels for 0%

commit v1 on v0

v1 whole, which is shorter than its diff:
```python
import functools
import math

import jax
import jax.numpy as jnp
from jax import lax
from jax.experimental import pallas as pl
from jax.experimental.pallas import tpu as pltpu
from jax.sharding import Mesh
from jax.sharding import PartitionSpec as P

ITERS = 2
D = 768
Z, X, Y, C = 8, 4, 4, 2
OWN = 32
K = Z * OWN
COL = 1024
HALF = COL // 2
CHUNK = 512
WIDE = D + 128
F32, BF16 = jnp.float32, jnp.bfloat16
SCALE = 50.0 * math.log2(math.e)
VMEM = pl.BlockSpec(memory_space=pltpu.VMEM)
ANY = pl.BlockSpec(memory_space=pl.ANY)
SMEM = pl.BlockSpec(memory_space=pltpu.SMEM)


def rows_to_tile(v):
    return jnp.concatenate([v[:, i * 128 : (i + 1) * 128] for i in range(v.shape[1] // 128)], axis=0)


def tile_to_rows(v):
    return jnp.concatenate([v[i : i + 1] for i in range(v.shape[0])], axis=1)


def swap_halves(v, c):
    h = v.shape[0] // 2
    return jnp.where(c == 0, v, jnp.concatenate([v[h:], v[:h]], axis=0))


def load_all(pieces, emb, sems):
    waits, at = [], 0
    for piece in pieces:
        for i in range(piece.shape[0] // CHUNK):
            copy = pltpu.make_async_copy(
                piece.at[pl.ds(i * CHUNK, CHUNK)], emb.at[pl.ds(at, CHUNK)], sems.at[len(waits)]
            )
            copy.start()
            waits.append(copy)
            at += CHUNK
    return waits


def score_kernel(n, first, merge, *refs):
    idx, cent_ref = refs[:2]
    refs = refs[2:]
    if merge:
        own_ref, refs = refs[0], refs[1:]
    pieces, (p_ref, m_ref, l_ref, emb, sems) = refs[:n], refs[n:]
    waits = load_all(pieces, emb, sems)
    cent = cent_ref[...]
    wide = cent.astype(F32)
    half_squares = (0.5 * SCALE) * jnp.sum(wide * wide, axis=1, keepdims=True)
    x, c = idx[0], idx[1]
    lse = []
    for i, wait in enumerate(waits):
        wait.wait()
        rows = pl.ds(i * CHUNK, CHUNK)
        dots = lax.dot_general(
            cent, emb[rows, :], (((1,), (1,)), ((), ())), preferred_element_type=F32
        )
        logits = dots * SCALE - half_squares
        peak = jnp.max(logits, axis=0, keepdims=True)
        p = jnp.exp2(logits - peak)
        total = jnp.sum(p, axis=0, keepdims=True)
        p_ref[:, rows] = p.astype(BF16)
        m_ref[pl.ds(i * 4, 4), :] = rows_to_tile(peak)
        lse.append(rows_to_tile(peak + jnp.log2(total)))
    if merge:
        l_ref[pl.ds(8 * x, 8), :] = own_ref[...]
    for j in range(len(lse) // 2):
        column = jnp.concatenate(lse[2 * j : 2 * j + 2], axis=0)
        k = first + j
        if k == 0:
            if l_ref.shape[0] == 8:
                l_ref[...] = column
            else:
                l_ref[pl.ds(8 * x, 8), :] = column
        else:
            l_ref[pl.ds(8 * lax.rem(x + (X - k), X), 8), :] = swap_halves(column, c)


def score(idx, cent, pieces, first, own=None):
    rows = sum(p.shape[0] for p in pieces)
    out = 8 if (first == 0 and rows == COL) else X * 8
    merge = own is not None
    return pl.pallas_call(
        functools.partial(score_kernel, len(pieces), first, merge),
        out_shape=(
            jax.ShapeDtypeStruct((K, rows), BF16),
            jax.ShapeDtypeStruct((rows // 128, 128), F32),
            jax.ShapeDtypeStruct((out, 128), F32),
        ),
        in_specs=[SMEM, VMEM] + [VMEM] * merge + [ANY] * len(pieces),
        out_specs=(VMEM, VMEM, VMEM),
        scratch_shapes=[
            pltpu.VMEM((rows, D), BF16),
            pltpu.SemaphoreType.DMA((rows // CHUNK,)),
        ],
        compiler_params=pltpu.CompilerParams(vmem_limit_bytes=24 << 20),
        name="score",
    )(idx, cent, *([own] if merge else []), *pieces)


def sum_kernel(n, np_, *refs):
    idx, parts_ref = refs[:2]
    refs = refs[2:]
    ps, ms, pieces = refs[:np_], refs[np_ : 2 * np_], refs[2 * np_ : 2 * np_ + n]
    out_ref, lse_ref, emb, sems = refs[2 * np_ + n :]
    waits = load_all(pieces, emb, sems)
    x, c = idx[0], idx[1]
    parts = [parts_ref[pl.ds(i * 32, 32), :] for i in range(X * Y)]
    peak = functools.reduce(jnp.maximum, parts)
    total = sum(jnp.exp2(v - peak) for v in parts)
    lse_ref[...] = peak + jnp.log2(total)
    acc = jnp.zeros((K, D), F32)
    weights = jnp.zeros((K, 128), F32)
    at = 0
    for p_ref, m_ref in zip(ps, ms):
        for j in range(p_ref.shape[1] // COL):
            k = at // 2
            lse = lse_ref[pl.ds(8 * lax.rem(x + (X - k), X), 8), :]
            if k > 0:
                lse = swap_halves(lse, c)
            factor = jnp.exp2(m_ref[pl.ds(j * 8, 8), :] - lse)
            for h in range(2):
                f = tile_to_rows(factor[4 * h : 4 * h + 4])
                p = p_ref[:, pl.ds((2 * j + h) * CHUNK, CHUNK)].astype(F32)
                resp = (p * f).astype(BF16)
                waits[at].wait()
                acc += jnp.dot(resp, emb[pl.ds(at * CHUNK, CHUNK), :], preferred_element_type=F32)
                wide = resp.astype(F32)
                for i in range(CHUNK // 128):
                    weights += wide[:, i * 128 : (i + 1) * 128]
                at += 1
    counts = jnp.sum(weights, axis=1, keepdims=True)
    high = counts.astype(BF16).astype(F32)
    lane = lax.broadcasted_iota(jnp.int32, (K, 128), 1)
    tail = jnp.where(lane == 0, high, jnp.where(lane == 1, counts - high, 0.0))
    out_ref[:, :D] = acc.astype(BF16)
    out_ref[:, D:] = tail.astype(BF16)


def sums_of(idx, parts, ps, ms, pieces):
    rows = X * COL
    return pl.pallas_call(
        functools.partial(sum_kernel, len(pieces), len(ps)),
        out_shape=(
            jax.ShapeDtypeStruct((K, WIDE), BF16),
            jax.ShapeDtypeStruct((X * 8, 128), F32),
        ),
        in_specs=[SMEM, VMEM] + [VMEM] * (2 * len(ps)) + [ANY] * len(pieces),
        out_specs=(VMEM, VMEM),
        scratch_shapes=[
            pltpu.VMEM((rows, D), BF16),
            pltpu.SemaphoreType.DMA((rows // CHUNK,)),
        ],
        compiler_params=pltpu.CompilerParams(vmem_limit_bytes=24 << 20),
        name="sums",
    )(idx, parts, *ps, *ms, *pieces)


def update_kernel(got_ref, cur_ref, new_ref, copies_ref, counts_ref):
    total = got_ref[pl.ds(0, OWN), :].astype(F32)
    for i in range(1, Z):
        total += got_ref[pl.ds(i * OWN, OWN), :].astype(F32)
    counts = total[:, D : D + 1] + total[:, D + 1 : D + 2]
    new = (total[:, :D] + cur_ref[...]) / (counts + 1.0)
    new_ref[...] = new
    for i in range(Z):
        copies_ref[pl.ds(i * OWN, OWN), :] = new.astype(BF16)
    counts_ref[...] = jnp.broadcast_to(counts, (OWN, 128))


def update(got, current):
    return pl.pallas_call(
        update_kernel,
        out_shape=(
            jax.ShapeDtypeStruct((OWN, D), F32),
            jax.ShapeDtypeStruct((K, D), BF16),
            jax.ShapeDtypeStruct((OWN, 128), F32),
        ),
        in_specs=[VMEM, VMEM],
        out_specs=(VMEM, VMEM, VMEM),
        name="update",
    )(got, current)


def shift(v, axis, size, k):
    return lax.ppermute(v, axis, [(i, (i + k) % size) for i in range(size)])


def on_device(embeddings, centroids):
    x, c = lax.axis_index("x"), lax.axis_index("c")
    idx = jnp.stack([x, c]).astype(jnp.int32)
    mine = lax.dynamic_slice_in_dim(embeddings, c * HALF, HALF, 0)
    near = {k: shift(mine, "x", X, k) for k in (1, 3, 2)}
    pieces = [embeddings]
    for k in (1, 2, 3):
        pieces += [near[k], shift(near[k], "c", C, 1)]
    copies = jnp.tile(centroids.astype(BF16), (Z, 1))
    current = centroids
    for step in range(ITERS):
        cent = lax.all_to_all(copies, "z", 0, 0, tiled=True)
        if step == 0:
            p0, m0, l0 = score(idx, cent, pieces[:1], 0)
            p1, m1, lse = score(idx, cent, pieces[1:], 1, l0)
            ps, ms = [p0, p1], [m0, m1]
        else:
            p, m, lse = score(idx, cent, pieces, 0)
            ps, ms = [p], [m]
        lse = jnp.logaddexp2(lse, shift(lse, "c", C, 1))
        parts = lax.all_to_all(jnp.tile(lse, (X * Y, 1)), ("x", "y"), 0, 0, tiled=True)
        out, total = sums_of(idx, parts, ps, ms, pieces)
        got = lax.all_to_all(out, "z", 0, 0, tiled=True)
        current, copies, counts = update(got, current)
    row_lse = lax.dynamic_slice_in_dim(total, x * 8, 8, 0).reshape(COL) * math.log(2.0)
    return current, counts[:, 0], row_lse


def solution(mesh):
    split = Mesh(mesh.devices.reshape(Z, X, Y, C), ("z", "x", "y", "c"))
    dp, every = ("z", "x"), ("z", "x", "y", "c")
    return jax.shard_map(
        on_device,
        mesh=split,
        in_specs=(P(dp, None), P(every, None)),
        out_specs=(P(every, None), P(every), P(dp)),
        check_vma=False,
    )
```

time: 491 us -> 177 us (0.36)
  waiting for transfers between devices: 240 us -> 65.5 us
  blocking collectives: 193 us -> 61.3 us
  Pallas kernels: 0 us -> 24.9 us
  matrix products: 21.4 us -> 0 us
  other arithmetic: 19.8 us -> 1.62 us
  starting transfers between devices: 0.12 us -> 17 us
  between operations: 13.9 us -> 0.79 us
    psum x4 -> x0, blocking collectives: 168 us -> none  [the longest x2 143 us: on_device(): all_sums, all_counts = lax.psum((sums, weights), 'dp')]
    psum x2 -> x0, waiting for transfers between devices: 155 us -> none  [on_device(): all_sums, all_counts = lax.psum((sums, weights), 'dp')]
    all_gather x1 -> x0, waiting for transfers between devices: 84.3 us -> none  [on_device(): whole = lax.all_gather(centroids, 'dp', axis=0, tiled=True)]
    all_to_all x0 -> x4, blocking collectives: none -> 61.3 us  [the longest x2 27.2 us: on_device(): lax.all_to_all(jnp.tile(lse, (X * Y, 1)), ('x', 'y'), 0, 0, tiled=True)]
    ppermute x0 -> x8, waiting for transfers between devices: none -> 35.7 us  [shift(): return lax.ppermute(v, axis, [(i, (i + k) % size) for i in range(size)])]
    all_to_all x0 -> x2, waiting for transfers between devices: none -> 29.8 us  [the longest x1 15.3 us: on_device(): cent = lax.all_to_all(copies, 'z', 0, 0, tiled=True)]
    pallas_call x0 -> x7, Pallas kernels: none -> 24.9 us  [the longest x3 12.1 us: score(): pl.pallas_call(functools.partial(score_kernel, len(pieces), first, merge)...]
    pmax x2 -> x0, blocking collectives: 24.8 us -> none  [expect(): global_peak = lax.pmax(local_peak, 'cent')]
  transfers between devices with their start and end apart: 3 -> 10, of which waited for: 3 -> 7; matrix products, arithmetic and copies ran while one was open for 1% -> 1% of each run, Pallas kernels for 0% -> 1%
where the time goes in v1:
time: 177 us; the launch traced here: 176 us
  waiting for transfers between devices  65.5 us (37%)
  blocking collectives  61.3 us (35%)
  Pallas kernels  24.9 us (14%)
  starting transfers between devices  17 us (10%)
  local copies, waits for them, and re-layouts  5.02 us (3%)
    ppermute x8, waiting for transfers between devices, shift(): return lax.ppermute(v, axis, [(i, (i + k) % size) for i in range(size)])  35.7 us
    all_to_all x2, blocking collectives, on_device(): lax.all_to_all(jnp.tile(lse, (X * Y, 1)), ('x', 'y'), 0, 0, tiled=True)  27.2 us
    all_to_all x1, blocking collectives, on_device(): got = lax.all_to_all(out, 'z', 0, 0, tiled=True)  18.3 us
    all_to_all x1, blocking collectives, on_device(): cent = lax.all_to_all(copies, 'z', 0, 0, tiled=True)  15.8 us
    all_to_all x1, waiting for transfers between devices, on_device(): cent = lax.all_to_all(copies, 'z', 0, 0, tiled=True)  15.3 us
    all_to_all x1, waiting for transfers between devices, on_device(): got = lax.all_to_all(out, 'z', 0, 0, tiled=True)  14.6 us
    pallas_call x3, Pallas kernels, score(): pl.pallas_call(functools.partial(score_kernel, len(pieces), first, merge)...  12.1 us
    pallas_call x2, Pallas kernels, sums_of(): pl.pallas_call(functools.partial(sum_kernel, len(pieces), len(ps)), out_s...  8.8 us
  transfers between devices with their start and end apart: 10, of which 7 were waited for; matrix products, arithmetic and copies ran while one was open for 1% of the time, Pallas kernels for 1%

profile of v1, /device:TPU:2, one launch (start us, length us, event | category | flops | bytes accessed | tf_op | source)
XLA Modules:
  0.0 176.1 jit_solution(1164479913095791781)
XLA Ops:
  0.6 1.3 constant_dynamic-slice_fusion
  2.0 2.3 %collective-permute-start.4 = (bf16[512,768]{1,0:T(8,128)(2,1)S(1)}, bf16[512,768]{1,0:T(8,128)(2,1)S(1)}, u32[]{:S(2)}, u32[]{:S(2)}) collective-permute-start(bf16[512,768]{1,0:T(8,128)(2,1)S(1)} %constant_dynamic-slice_fusion), channel_id=1, source_target_pairs={{0,24},{8,0},{16,8},{24,16},{1,25},{9,1},{17,9},{25,17},{2,26},{10... | collective-permute-start | bytes 2359304 | tf_op jit(solution)/shard_map/ppermute | solution.py:200
  4.3 0.7 collective-permute-start.2
  5.0 1.8 %collective-permute-start = (bf16[512,768]{1,0:T(8,128)(2,1)S(1)}, bf16[512,768]{1,0:T(8,128)(2,1)}, u32[]{:S(2)}, u32[]{:S(2)}) collective-permute-start(bf16[512,768]{1,0:T(8,128)(2,1)S(1)} %constant_dynamic-slice_fusion), channel_id=1, source_target_pairs={{0,8},{8,16},{16,24},{24,0},{1,9},{9,17},{17,25},{25,1},{2,10},{10... | collective-permute-start | bytes 2359304 | tf_op jit(solution)/shard_map/ppermute | solution.py:200
  6.8 15.5 %collective-permute-done.4.refs_7_.refs_11_.refs_9_ = bf16[512,768]{1,0:T(8,128)(2,1)S(1)} collective-permute-done((bf16[512,768]{1,0:T(8,128)(2,1)S(1)}, bf16[512,768]{1,0:T(8,128)(2,1)S(1)}, u32[]{:S(2)}, u32[]{:S(2)}) %collective-permute-start.4) | collective-permute-done | bytes 786464 | tf_op jit(solution)/shard_map/ppermute | solution.py:200
  22.3 16.8 %collective-permute-done.2.refs_5_.refs_9_.refs_7_ = bf16[512,768]{1,0:T(8,128)(2,1)S(1)} collective-permute-done((bf16[512,768]{1,0:T(8,128)(2,1)S(1)}, bf16[512,768]{1,0:T(8,128)(2,1)S(1)}, u32[]{:S(2)}, u32[]{:S(2)}) %collective-permute-start.2) | collective-permute-done | bytes 786464 | tf_op jit(solution)/shard_map/ppermute | solution.py:200
  39.1 1.0 collective-permute-done.refs_3_.refs_7_.refs_5_
  40.1 0.9 convert_element_type.3
  41.0 0.8 tile.6
  41.8 8.5 %all-to-all-start = ((bf16[8,32,768]{2,1,0:T(8,128)(2,1)}), bf16[8,32,768]{2,1,0:T(8,128)(2,1)S(1)}, u32[]{:S(2)}, u32[]{:S(2)}) async-start(bf16[8,32,768]{2,1,0:T(8,128)(2,1)} %tile.6), calls=%async_computation | async-start | bytes 786432 | tf_op jit(solution)/shard_map/all_to_all | solution.py:214
  50.4 15.3 %all-to-all-done = bf16[8,32,768]{2,1,0:T(8,128)(2,1)S(1)} async-done(((bf16[8,32,768]{2,1,0:T(8,128)(2,1)}), bf16[8,32,768]{2,1,0:T(8,128)(2,1)S(1)}, u32[]{:S(2)}, u32[]{:S(2)}) %all-to-all-start) | async-done | bytes 393248 | tf_op jit(solution)/shard_map/all_to_all | solution.py:214
  65.6 1.9 %score.3 = (bf16[256,1024]{1,0:T(8,128)(2,1)S(1)}, f32[8,128]{1,0:T(8,128)S(1)}, f32[8,128]{1,0:T(8,128)S(1)}) custom-call(s32[2]{0:T(128)S(1)} %pad_add_fusion.refs_0_, bf16[256,768]{1,0:T(8,128)(2,1)S(1)} %bitcast.13, bf16[1024,768]{1,0:T(8,128)(2,1)S(1)} %copy-done), custom_call_target="tpu_custom_call" | custom-call | tf_op jit(solution)/shard_map/score/pallas_call | solution.py:97
  67.6 5.0 %score.4 = (bf16[256,3072]{1,0:T(8,128)(2,1)S(1)}, f32[24,128]{1,0:T(8,128)S(1)}, f32[32,128]{1,0:T(8,128)S(1)}) custom-call(s32[2]{0:T(128)S(1)} %pad_add_fusion.refs_0_, bf16[256,768]{1,0:T(8,128)(2,1)S(1)} %bitcast.14, f32[8,128]{1,0:T(8,128)S(1)} %get-tuple-element.19.refs_2_, bf16[512,768]{1,0:T(8,128)(2,1)} %collective-permute-done.refs_3_.refs_7_.refs_5_, ...), custom_call_target="tpu_custom_call" | custom-call | tf_op jit(solution)/shard_map/score/pallas_call | solution.py:97
  72.6 0.1 collective-permute-start.6
  72.7 1.2 collective-permute-done.6
  73.9 14.3 %all_to_all.57 = f32[16,32,128]{2,1,0:T(8,128)S(1)} all-to-all(f32[16,32,128]{2,1,0:T(8,128)S(1)} %tile.7), channel_id=1, replica_groups=mesh['z'=8,'x'=4,'y'=4,'c'=2] {'x','y'}, dimensions={0} | all-to-all | bytes 524288 | tf_op jit(solution)/shard_map/all_to_all | solution.py:223
  88.2 4.5 %sums.2 = (bf16[256,896]{1,0:T(8,128)(2,1)S(1)}, f32[32,128]{1,0:T(8,128)}) custom-call(s32[2]{0:T(128)S(1)} %pad_add_fusion.refs_0_, f32[512,128]{1,0:T(8,128)S(1)} %bitcast.17, bf16[256,1024]{1,0:T(8,128)(2,1)S(1)} %get-tuple-element.21.refs_2_, bf16[256,3072]{1,0:T(8,128)(2,1)S(1)} %get-tuple-element.22.refs_3_, f32[8,128]{1,0:T(8,128)S(1)} %get-tuple-element.23.refs_4_, ...), custom_call_target="tpu_custom_call" | custom-call | tf_op jit(solution)/shard_map/sums/pallas_call | solution.py:156
  92.7 18.3 %all_to_all.58 = bf16[8,32,896]{2,1,0:T(8,128)(2,1)} all-to-all(bf16[8,32,896]{2,1,0:T(8,128)(2,1)S(1)} %bitcast.19), channel_id=1, replica_groups=mesh['z'=8,'x'=4,'y'=4,'c'=2] {'z'}, dimensions={0} | all-to-all | bytes 917504 | tf_op jit(solution)/shard_map/all_to_all | solution.py:225
  111.0 2.0 %update.2 = (f32[32,768]{1,0:T(8,128)}, bf16[256,768]{1,0:T(8,128)(2,1)}, f32[32,128]{1,0:T(8,128)}) custom-call(bf16[256,896]{1,0:T(8,128)(2,1)} %bitcast.21, f32[32,768]{1,0:T(8,128)} %cur_ref.1), custom_call_target="tpu_custom_call" | custom-call | tf_op jit(solution)/shard_map/update/pallas_call | solution.py:186
  113.0 15.8 %all_to_all.59 = bf16[8,32,768]{2,1,0:T(8,128)(2,1)S(1)} all-to-all(bf16[8,32,768]{2,1,0:T(8,128)(2,1)} %bitcast.22), channel_id=1, replica_groups=mesh['z'=8,'x'=4,'y'=4,'c'=2] {'z'}, dimensions={0} | all-to-all | bytes 786432 | tf_op jit(solution)/shard_map/all_to_all | solution.py:214
  128.8 5.3 %score.5 = (bf16[256,4096]{1,0:T(8,128)(2,1)S(1)}, f32[32,128]{1,0:T(8,128)S(1)}, f32[32,128]{1,0:T(8,128)S(1)}) custom-call(s32[2]{0:T(128)S(1)} %pad_add_fusion.refs_0_, bf16[256,768]{1,0:T(8,128)(2,1)S(1)} %bitcast.15, bf16[1024,768]{1,0:T(8,128)(2,1)S(1)} %copy-done, bf16[512,768]{1,0:T(8,128)(2,1)} %collective-permute-done.refs_3_.refs_7_.refs_5_, ...), custom_call_target="tpu_custom_call" | custom-call | tf_op jit(solution)/shard_map/score/pallas_call | solution.py:97
  134.1 0.1 collective-permute-start.7
  134.2 1.2 collective-permute-done.7
  135.4 12.9 %all_to_all.60 = f32[16,32,128]{2,1,0:T(8,128)S(1)} all-to-all(f32[16,32,128]{2,1,0:T(8,128)S(1)} %tile.8), channel_id=1, replica_groups=mesh['z'=8,'x'=4,'y'=4,'c'=2] {'x','y'}, dimensions={0} | all-to-all | bytes 524288 | tf_op jit(solution)/shard_map/all_to_all | solution.py:223
  148.3 4.3 %sums.3 = (bf16[256,896]{1,0:T(8,128)(2,1)S(1)}, f32[32,128]{1,0:T(8,128)S(1)}) custom-call(s32[2]{0:T(128)S(1)} %pad_add_fusion.refs_0_, f32[512,128]{1,0:T(8,128)S(1)} %bitcast.16, bf16[256,4096]{1,0:T(8,128)(2,1)S(1)} %get-tuple-element.28.refs_2_, f32[32,128]{1,0:T(8,128)S(1)} %get-tuple-element.29.refs_3_, bf16[1024,768]{1,0:T(8,128)(2,1)S(1)} %copy-done, ...), custom_call_target="tpu_custom_call" | custom-call | tf_op jit(solution)/shard_map/sums/pallas_call | solution.py:156
  152.6 0.8 copy-done.1
  153.4 3.5 %all-to-all-start.5 = ((bf16[8,32,896]{2,1,0:T(8,128)(2,1)}), bf16[8,32,896]{2,1,0:T(8,128)(2,1)S(1)}, u32[]{:S(2)}, u32[]{:S(2)}) async-start(bf16[8,32,896]{2,1,0:T(8,128)(2,1)} %bitcast.18), calls=%async_computation.5 | async-start | bytes 917504 | tf_op jit(solution)/shard_map/all_to_all | solution.py:225
  156.9 0.6 multiply_bitcast_fusion
  157.5 14.6 %all-to-all-done.5 = bf16[8,32,896]{2,1,0:T(8,128)(2,1)S(1)} async-done(((bf16[8,32,896]{2,1,0:T(8,128)(2,1)}), bf16[8,32,896]{2,1,0:T(8,128)(2,1)S(1)}, u32[]{:S(2)}, u32[]{:S(2)}) %all-to-all-start.5) | async-done | bytes 458784 | tf_op jit(solution)/shard_map/all_to_all | solution.py:225
  172.0 0.8 copy-done.2
  172.8 2.0 %update.3 = (f32[32,768]{1,0:T(8,128)}, bf16[256,768]{1,0:T(8,128)(2,1)}, f32[32,128]{1,0:T(8,128)}) custom-call(bf16[256,896]{1,0:T(8,128)(2,1)} %bitcast.20, f32[32,768]{1,0:T(8,128)} %get-tuple-element.31.cur_ref), custom_call_target="tpu_custom_call" | custom-call | tf_op jit(solution)/shard_map/update/pallas_call | solution.py:186
  174.8 1.3 slice_reduce_fusion
  (15 shorter events, 0.2 us)
Async XLA Ops:
  0.6 65.0 %copy-start = (bf16[1024,768]{1,0:T(8,128)(2,1)S(1)}, bf16[1024,768]{1,0:T(8,128)(2,1)}, u32[]{:S(2)}) copy-start(bf16[1024,768]{1,0:T(8,128)(2,1)} %refs_4_.1) | copy-start | bytes 4718596
  2.0 20.3 %collective-permute-start.4 = (bf16[512,768]{1,0:T(8,128)(2,1)S(1)}, bf16[512,768]{1,0:T(8,128)(2,1)S(1)}, u32[]{:S(2)}, u32[]{:S(2)}) collective-permute-start(bf16[512,768]{1,0:T(8,128)(2,1)S(1)} %constant_dynamic-slice_fusion), channel_id=1, source_target_pairs={{0,24},{8,0},{16,8},{24,16},{1,25},{9,1},{17,9},{25,17},{2,26},{10... | collective-permute-start | bytes 2359304 | tf_op jit(solution)/shard_map/ppermute | solution.py:200
  4.3 34.8 %collective-permute-start.2 = (bf16[512,768]{1,0:T(8,128)(2,1)S(1)}, bf16[512,768]{1,0:T(8,128)(2,1)S(1)}, u32[]{:S(2)}, u32[]{:S(2)}) collective-permute-start(bf16[512,768]{1,0:T(8,128)(2,1)S(1)} %constant_dynamic-slice_fusion), channel_id=1, source_target_pairs={{0,16},{8,24},{16,0},{24,8},{1,17},{9,25},{17,1},{25,9},{2,18},{10... | collective-permute-start | bytes 2359304 | tf_op jit(solution)/shard_map/ppermute | solution.py:200
  5.0 35.1 %collective-permute-start = (bf16[512,768]{1,0:T(8,128)(2,1)S(1)}, bf16[512,768]{1,0:T(8,128)(2,1)}, u32[]{:S(2)}, u32[]{:S(2)}) collective-permute-start(bf16[512,768]{1,0:T(8,128)(2,1)S(1)} %constant_dynamic-slice_fusion), channel_id=1, source_target_pairs={{0,8},{8,16},{16,24},{24,0},{1,9},{9,17},{17,25},{25,1},{2,10},{10... | collective-permute-start | bytes 2359304 | tf_op jit(solution)/shard_map/ppermute | solution.py:200
  22.3 45.2 %collective-permute-start.5 = (bf16[512,768]{1,0:T(8,128)(2,1)S(1)}, bf16[512,768]{1,0:T(8,128)(2,1)}, u32[]{:S(2)}, u32[]{:S(2)}) collective-permute-start(bf16[512,768]{1,0:T(8,128)(2,1)S(1)} %collective-permute-done.4.refs_7_.refs_11_.refs_9_), channel_id=1, source_target_pairs={{0,1},{1,0},{2,3},{3,2},{4,5},{5,4},{6,7},{7,6},{8,9},{9,8},{10,11... | collective-permute-start | bytes 2359304 | tf_op jit(solution)/shard_map/ppermute | solution.py:200
  39.1 28.5 %collective-permute-start.3 = (bf16[512,768]{1,0:T(8,128)(2,1)S(1)}, bf16[512,768]{1,0:T(8,128)(2,1)}, u32[]{:S(2)}, u32[]{:S(2)}) collective-permute-start(bf16[512,768]{1,0:T(8,128)(2,1)S(1)} %collective-permute-done.2.refs_5_.refs_9_.refs_7_), channel_id=1, source_target_pairs={{0,1},{1,0},{2,3},{3,2},{4,5},{5,4},{6,7},{7,6},{8,9},{9,8},{10,11... | collective-permute-start | bytes 2359304 | tf_op jit(solution)/shard_map/ppermute | solution.py:200
  40.1 27.5 %collective-permute-start.1 = (bf16[512,768]{1,0:T(8,128)(2,1)}, bf16[512,768]{1,0:T(8,128)(2,1)}, u32[]{:S(2)}, u32[]{:S(2)}) collective-permute-start(bf16[512,768]{1,0:T(8,128)(2,1)} %collective-permute-done.refs_3_.refs_7_.refs_5_), channel_id=1, source_target_pairs={{0,1},{1,0},{2,3},{3,2},{4,5},{5,4},{6,7},{7,6},{8,9},{9,8},{10,11... | collective-permute-start | bytes 2359304 | tf_op jit(solution)/shard_map/ppermute | solution.py:200
  41.8 23.8 %all-to-all-start = ((bf16[8,32,768]{2,1,0:T(8,128)(2,1)}), bf16[8,32,768]{2,1,0:T(8,128)(2,1)S(1)}, u32[]{:S(2)}, u32[]{:S(2)}) async-start(bf16[8,32,768]{2,1,0:T(8,128)(2,1)} %tile.6), calls=%async_computation | async-start | bytes 786432 | tf_op jit(solution)/shard_map/all_to_all | solution.py:214
  72.6 1.3 collective-permute-start.6
  134.1 1.3 collective-permute-start.7
  152.6 0.8 copy-start.1
  153.4 18.6 %all-to-all-start.5 = ((bf16[8,32,896]{2,1,0:T(8,128)(2,1)}), bf16[8,32,896]{2,1,0:T(8,128)(2,1)S(1)}, u32[]{:S(2)}, u32[]{:S(2)}) async-start(bf16[8,32,896]{2,1,0:T(8,128)(2,1)} %bitcast.18), calls=%async_computation.5 | async-start | bytes 917504 | tf_op jit(solution)/shard_map/all_to_all | solution.py:225
  172.0 0.8 copy-start.2

commit v2 on v1

--- a/solution.py
+++ b/solution.py
@@ -63,9 +63,11 @@
     half_squares = (0.5 * SCALE) * jnp.sum(wide * wide, axis=1, keepdims=True)
     x, c = idx[0], idx[1]
     lse = []
-    for i, wait in enumerate(waits):
-        wait.wait()
-        rows = pl.ds(i * CHUNK, CHUNK)
+    step = emb.shape[0] // (1 if emb.shape[0] == COL else 2)
+    for at in range(0, emb.shape[0], step):
+        for wait in waits[at // CHUNK : (at + step) // CHUNK]:
+            wait.wait()
+        rows = pl.ds(at, step)
         dots = lax.dot_general(
             cent, emb[rows, :], (((1,), (1,)), ((), ())), preferred_element_type=F32
         )
@@ -74,12 +76,13 @@
         p = jnp.exp2(logits - peak)
         total = jnp.sum(p, axis=0, keepdims=True)
         p_ref[:, rows] = p.astype(BF16)
-        m_ref[pl.ds(i * 4, 4), :] = rows_to_tile(peak)
+        m_ref[pl.ds(at // 128, step // 128), :] = rows_to_tile(peak)
         lse.append(rows_to_tile(peak + jnp.log2(total)))
+    lse = jnp.concatenate(lse, axis=0)
     if merge:
         l_ref[pl.ds(8 * x, 8), :] = own_ref[...]
-    for j in range(len(lse) // 2):
-        column = jnp.concatenate(lse[2 * j : 2 * j + 2], axis=0)
+    for j in range(emb.shape[0] // COL):
+        column = lse[8 * j : 8 * j + 8]
         k = first + j
         if k == 0:
             if l_ref.shape[0] == 8:
@@ -123,8 +126,8 @@
     peak = functools.reduce(jnp.maximum, parts)
     total = sum(jnp.exp2(v - peak) for v in parts)
     lse_ref[...] = peak + jnp.log2(total)
-    acc = jnp.zeros((K, D), F32)
     weights = jnp.zeros((K, 128), F32)
+    resps = []
     at = 0
     for p_ref, m_ref in zip(ps, ms):
         for j in range(p_ref.shape[1] // COL):
@@ -137,12 +140,14 @@
                 f = tile_to_rows(factor[4 * h : 4 * h + 4])
                 p = p_ref[:, pl.ds((2 * j + h) * CHUNK, CHUNK)].astype(F32)
                 resp = (p * f).astype(BF16)
-                waits[at].wait()
-                acc += jnp.dot(resp, emb[pl.ds(at * CHUNK, CHUNK), :], preferred_element_type=F32)
                 wide = resp.astype(F32)
                 for i in range(CHUNK // 128):
                     weights += wide[:, i * 128 : (i + 1) * 128]
+                resps.append(resp)
                 at += 1
+    for wait in waits:
+        wait.wait()
+    acc = jnp.dot(jnp.concatenate(resps, axis=1), emb[...], preferred_element_type=F32)
     counts = jnp.sum(weights, axis=1, keepdims=True)
     high = counts.astype(BF16).astype(F32)
     lane = lax.broadcasted_iota(jnp.int32, (K, 128), 1)
@@ -179,7 +184,9 @@
     new_ref[...] = new
     for i in range(Z):
         copies_ref[pl.ds(i * OWN, OWN), :] = new.astype(BF16)
-    counts_ref[...] = jnp.broadcast_to(counts, (OWN, 128))
+    row = lax.broadcasted_iota(jnp.int32, (OWN, OWN), 0)
+    lane = lax.broadcasted_iota(jnp.int32, (OWN, OWN), 1)
+    counts_ref[...] = jnp.sum(jnp.where(row == lane, counts, 0.0), axis=0, keepdims=True)
 
 
 def update(got, current):
@@ -188,7 +195,7 @@
         out_shape=(
             jax.ShapeDtypeStruct((OWN, D), F32),
             jax.ShapeDtypeStruct((K, D), BF16),
-            jax.ShapeDtypeStruct((OWN, 128), F32),
+            jax.ShapeDtypeStruct((1, OWN), F32),
         ),
         in_specs=[VMEM, VMEM],
         out_specs=(VMEM, VMEM, VMEM),
@@ -205,15 +212,16 @@
     idx = jnp.stack([x, c]).astype(jnp.int32)
     mine = lax.dynamic_slice_in_dim(embeddings, c * HALF, HALF, 0)
     near = {k: shift(mine, "x", X, k) for k in (1, 3, 2)}
-    pieces = [embeddings]
-    for k in (1, 2, 3):
-        pieces += [near[k], shift(near[k], "c", C, 1)]
     copies = jnp.tile(centroids.astype(BF16), (Z, 1))
     current = centroids
     for step in range(ITERS):
         cent = lax.all_to_all(copies, "z", 0, 0, tiled=True)
         if step == 0:
-            p0, m0, l0 = score(idx, cent, pieces[:1], 0)
+            p0, m0, l0 = score(idx, cent, [embeddings], 0)
+            near, l0 = lax.optimization_barrier((near, l0))
+            pieces = [embeddings]
+            for k in (1, 2, 3):
+                pieces += [near[k], shift(near[k], "c", C, 1)]
             p1, m1, lse = score(idx, cent, pieces[1:], 1, l0)
             ps, ms = [p0, p1], [m0, m1]
         else:
@@ -225,7 +233,7 @@
         got = lax.all_to_all(out, "z", 0, 0, tiled=True)
         current, copies, counts = update(got, current)
     row_lse = lax.dynamic_slice_in_dim(total, x * 8, 8, 0).reshape(COL) * math.log(2.0)
-    return current, counts[:, 0], row_lse
+    return current, counts.reshape(OWN), row_lse
 
 
 def solution(mesh):

time: 177 us -> 159 us (0.90)
  waiting for transfers between devices: 65.5 us -> 42.4 us
  blocking collectives: 61.3 us -> 66.2 us
  Pallas kernels: 24.9 us -> 21 us
  local copies, waits for them, and re-layouts: 5.02 us -> 8.06 us
    ppermute x8, waiting for transfers between devices: 35.7 us -> 14.1 us  [shift(): return lax.ppermute(v, axis, [(i, (i + k) % size) for i in range(size)])]
    all_to_all x1, blocking collectives: 18.3 us -> 23.3 us  [on_device(): got = lax.all_to_all(out, 'z', 0, 0, tiled=True)]
    unnamed x6 -> x18, local copies, waits for them, and re-layouts: 1.53 us -> 4.97 us
    pallas_call x3, Pallas kernels: 12.1 us -> 9.61 us  [score(): pl.pallas_call(functools.partial(score_kernel, len(pieces), first, merge)...]
  transfers between devices with their start and end apart: 10 -> 10, of which waited for: 7 -> 8; matrix products, arithmetic and copies ran while one was open for 1% -> 2% of each run, Pallas kernels for 1% -> 1%
where the time goes in v2:
time: 159 us; the launch traced here: 158 us
  blocking collectives  66.2 us (42%)
  waiting for transfers between devices  42.4 us (27%)
  Pallas kernels  21 us (13%)
  starting transfers between devices  17.5 us (11%)
  local copies, waits for them, and re-layouts  8.06 us (5%)
  other arithmetic  1.61 us (1%)
    all_to_all x2, blocking collectives, on_device(): lax.all_to_all(jnp.tile(lse, (X * Y, 1)), ('x', 'y'), 0, 0, tiled=True)  27.4 us
    all_to_all x1, blocking collectives, on_device(): got = lax.all_to_all(out, 'z', 0, 0, tiled=True)  23.3 us
    all_to_all x1, blocking collectives, on_device(): cent = lax.all_to_all(copies, 'z', 0, 0, tiled=True)  15.4 us
    all_to_all x1, waiting for transfers between devices, on_device(): got = lax.all_to_all(out, 'z', 0, 0, tiled=True)  14.5 us
    ppermute x8, waiting for transfers between devices, shift(): return lax.ppermute(v, axis, [(i, (i + k) % size) for i in range(size)])  14.1 us
    all_to_all x1, waiting for transfers between devices, on_device(): cent = lax.all_to_all(copies, 'z', 0, 0, tiled=True)  13.8 us
    pallas_call x3, Pallas kernels, score(): pl.pallas_call(functools.partial(score_kernel, len(pieces), first, merge)...  9.61 us
    all_to_all x1, starting transfers between devices, on_device(): cent = lax.all_to_all(copies, 'z', 0, 0, tiled=True)  8.47 us
  transfers between devices with their start and end apart: 10, of which 8 were waited for; matrix products, arithmetic and copies ran while one was open for 2% of the time, Pallas kernels for 1%

profile of v2, /device:TPU:2, one launch (start us, length us, event | category | flops | bytes accessed | tf_op | source)
XLA Modules:
  0.0 157.6 jit_solution(7019155223724927320)
XLA Ops:
  0.6 2.2 %constant_dynamic-slice_fusion = bf16[512,768]{1,0:T(8,128)(2,1)} fusion(bf16[1024,768]{1,0:T(8,128)(2,1)} %refs_4_.1, s32[]{:T(128)S(6)} %select_n.12), kind=kLoop, calls=%fused_computation.4 | loop fusion | bytes 1572868 | tf_op jit(solution)/shard_map/dynamic_slice | solution.py:213
  2.9 2.3 %collective-permute-start.2 = (bf16[512,768]{1,0:T(8,128)(2,1)}, bf16[512,768]{1,0:T(8,128)(2,1)S(1)}, u32[]{:S(2)}, u32[]{:S(2)}) collective-permute-start(bf16[512,768]{1,0:T(8,128)(2,1)} %constant_dynamic-slice_fusion), channel_id=1, source_target_pairs={{0,24},{8,0},{16,8},{24,16},{1,25},{9,1},{17,9},{25,17},{2,26},{10... | collective-permute-start | bytes 2359304 | tf_op jit(solution)/shard_map/ppermute | solution.py:207
  5.1 0.7 collective-permute-start.1
  5.8 1.8 %collective-permute-start = (bf16[512,768]{1,0:T(8,128)(2,1)}, bf16[512,768]{1,0:T(8,128)(2,1)}, u32[]{:S(2)}, u32[]{:S(2)}) collective-permute-start(bf16[512,768]{1,0:T(8,128)(2,1)} %constant_dynamic-slice_fusion), channel_id=1, source_target_pairs={{0,8},{8,16},{16,24},{24,0},{1,9},{9,17},{17,25},{25,1},{2,10},{10... | collective-permute-start | bytes 2359304 | tf_op jit(solution)/shard_map/ppermute | solution.py:207
  7.6 0.9 convert_element_type.3
  8.5 0.8 tile.6
  9.4 8.5 %all-to-all-start = ((bf16[8,32,768]{2,1,0:T(8,128)(2,1)}), bf16[8,32,768]{2,1,0:T(8,128)(2,1)S(1)}, u32[]{:S(2)}, u32[]{:S(2)}) async-start(bf16[8,32,768]{2,1,0:T(8,128)(2,1)} %tile.6), calls=%async_computation | async-start | bytes 786432 | tf_op jit(solution)/shard_map/all_to_all | solution.py:218
  17.9 13.8 %all-to-all-done = bf16[8,32,768]{2,1,0:T(8,128)(2,1)S(1)} async-done(((bf16[8,32,768]{2,1,0:T(8,128)(2,1)}), bf16[8,32,768]{2,1,0:T(8,128)(2,1)S(1)}, u32[]{:S(2)}, u32[]{:S(2)}) %all-to-all-start) | async-done | bytes 393248 | tf_op jit(solution)/shard_map/all_to_all | solution.py:218
  31.7 1.6 score.3
  33.3 6.9 %collective-permute-done.1.refs_5_.refs_9_.refs_7_ = bf16[512,768]{1,0:T(8,128)(2,1)S(1)} collective-permute-done((bf16[512,768]{1,0:T(8,128)(2,1)}, bf16[512,768]{1,0:T(8,128)(2,1)S(1)}, u32[]{:S(2)}, u32[]{:S(2)}) %collective-permute-start.1) | collective-permute-done | bytes 786464 | tf_op jit(solution)/shard_map/ppermute | solution.py:207
  40.1 1.0 collective-permute-done.refs_3_.refs_7_.refs_5_
  41.7 3.1 %collective-permute-done.3.refs_4_.refs_8_.refs_6_ = bf16[512,768]{1,0:T(8,128)(2,1)S(1)} collective-permute-done((bf16[512,768]{1,0:T(8,128)(2,1)}, bf16[512,768]{1,0:T(8,128)(2,1)S(1)}, u32[]{:S(2)}, u32[]{:S(2)}) %collective-permute-start.3) | collective-permute-done | bytes 786464 | tf_op jit(solution)/shard_map/ppermute | solution.py:207
  44.7 0.9 collective-permute-done.5.refs_8_.refs_12_.refs_10_
  45.7 3.7 %score.4 = (bf16[256,3072]{1,0:T(8,128)(2,1)S(1)}, f32[24,128]{1,0:T(8,128)S(1)}, f32[32,128]{1,0:T(8,128)S(1)}) custom-call(s32[2]{0:T(128)S(1)} %pad_add_fusion.refs_0_, bf16[256,768]{1,0:T(8,128)(2,1)S(1)} %bitcast.15, f32[8,128]{1,0:T(8,128)S(1)} %get-tuple-element.24.refs_2_, bf16[512,768]{1,0:T(8,128)(2,1)} %collective-permute-done.refs_3_.refs_7_.refs_5_, ...), custom_call_target="tpu_custom_call" | custom-call | tf_op jit(solution)/shard_map/score/pallas_call | solution.py:100
  49.7 1.0 collective-permute-done.6
  50.8 14.4 %all_to_all.57 = f32[16,32,128]{2,1,0:T(8,128)S(1)} all-to-all(f32[16,32,128]{2,1,0:T(8,128)S(1)} %tile.7), channel_id=1, replica_groups=mesh['z'=8,'x'=4,'y'=4,'c'=2] {'x','y'}, dimensions={0} | all-to-all | bytes 524288 | tf_op jit(solution)/shard_map/all_to_all | solution.py:231
  65.1 3.7 %sums.2 = (bf16[256,896]{1,0:T(8,128)(2,1)S(1)}, f32[32,128]{1,0:T(8,128)}) custom-call(s32[2]{0:T(128)S(1)} %pad_add_fusion.refs_0_, f32[512,128]{1,0:T(8,128)S(1)} %bitcast.18, bf16[256,1024]{1,0:T(8,128)(2,1)S(1)} %get-tuple-element.29.refs_2_, bf16[256,3072]{1,0:T(8,128)(2,1)S(1)} %get-tuple-element.30.refs_3_, f32[8,128]{1,0:T(8,128)S(1)} %get-tuple-element.31.refs_4_, ...), custom_call_target="tpu_custom_call" | custom-call | tf_op jit(solution)/shard_map/sums/pallas_call | solution.py:161
  68.8 23.3 %all_to_all.58 = bf16[8,32,896]{2,1,0:T(8,128)(2,1)} all-to-all(bf16[8,32,896]{2,1,0:T(8,128)(2,1)S(1)} %bitcast.20), channel_id=1, replica_groups=mesh['z'=8,'x'=4,'y'=4,'c'=2] {'z'}, dimensions={0} | all-to-all | bytes 917504 | tf_op jit(solution)/shard_map/all_to_all | solution.py:233
  92.1 2.0 %update.2 = (f32[32,768]{1,0:T(8,128)}, bf16[256,768]{1,0:T(8,128)(2,1)}, f32[1,32]{1,0:T(1,128)}) custom-call(bf16[256,896]{1,0:T(8,128)(2,1)} %bitcast.22, f32[32,768]{1,0:T(8,128)} %cur_ref.1), custom_call_target="tpu_custom_call" | custom-call | tf_op jit(solution)/shard_map/update/pallas_call | solution.py:193
  94.1 15.4 %all_to_all.59 = bf16[8,32,768]{2,1,0:T(8,128)(2,1)S(1)} all-to-all(bf16[8,32,768]{2,1,0:T(8,128)(2,1)} %bitcast.23), channel_id=1, replica_groups=mesh['z'=8,'x'=4,'y'=4,'c'=2] {'z'}, dimensions={0} | all-to-all | bytes 786432 | tf_op jit(solution)/shard_map/all_to_all | solution.py:218
  109.5 1.1 copy-done.2
  110.7 1.1 copy-done.4
  111.8 1.1 copy-done.6
  112.9 4.3 %score.5 = (bf16[256,4096]{1,0:T(8,128)(2,1)S(1)}, f32[32,128]{1,0:T(8,128)S(1)}, f32[32,128]{1,0:T(8,128)S(1)}) custom-call(s32[2]{0:T(128)S(1)} %pad_add_fusion.refs_0_, bf16[256,768]{1,0:T(8,128)(2,1)S(1)} %bitcast.16, bf16[1024,768]{1,0:T(8,128)(2,1)S(1)} %copy-done, bf16[512,768]{1,0:T(8,128)(2,1)} %collective-permute-done.refs_3_.refs_7_.refs_5_, ...), custom_call_target="tpu_custom_call" | custom-call | tf_op jit(solution)/shard_map/score/pallas_call | solution.py:100
  117.4 1.2 collective-permute-done.7
  118.6 13.1 %all_to_all.60 = f32[16,32,128]{2,1,0:T(8,128)S(1)} all-to-all(f32[16,32,128]{2,1,0:T(8,128)S(1)} %tile.8), channel_id=1, replica_groups=mesh['z'=8,'x'=4,'y'=4,'c'=2] {'x','y'}, dimensions={0} | all-to-all | bytes 524288 | tf_op jit(solution)/shard_map/all_to_all | solution.py:231
  131.7 3.7 %sums.3 = (bf16[256,896]{1,0:T(8,128)(2,1)S(1)}, f32[32,128]{1,0:T(8,128)S(1)}) custom-call(s32[2]{0:T(128)S(1)} %pad_add_fusion.refs_0_, f32[512,128]{1,0:T(8,128)S(1)} %bitcast.17, bf16[256,4096]{1,0:T(8,128)(2,1)S(1)} %get-tuple-element.36.refs_2_, f32[32,128]{1,0:T(8,128)S(1)} %get-tuple-element.37.refs_3_, bf16[1024,768]{1,0:T(8,128)(2,1)S(1)} %copy-done, ...), custom_call_target="tpu_custom_call" | custom-call | tf_op jit(solution)/shard_map/sums/pallas_call | solution.py:161
  135.4 0.8 copy-done.7
  136.1 3.5 %all-to-all-start.5 = ((bf16[8,32,896]{2,1,0:T(8,128)(2,1)}), bf16[8,32,896]{2,1,0:T(8,128)(2,1)S(1)}, u32[]{:S(2)}, u32[]{:S(2)}) async-start(bf16[8,32,896]{2,1,0:T(8,128)(2,1)} %bitcast.19), calls=%async_computation.5 | async-start | bytes 917504 | tf_op jit(solution)/shard_map/all_to_all | solution.py:233
  140.2 14.5 %all-to-all-done.5 = bf16[8,32,896]{2,1,0:T(8,128)(2,1)S(1)} async-done(((bf16[8,32,896]{2,1,0:T(8,128)(2,1)}), bf16[8,32,896]{2,1,0:T(8,128)(2,1)S(1)}, u32[]{:S(2)}, u32[]{:S(2)}) %all-to-all-start.5) | async-done | bytes 458784 | tf_op jit(solution)/shard_map/all_to_all | solution.py:233
  154.8 0.8 copy-done.8
  155.5 2.0 %update.3 = (f32[32,768]{1,0:T(8,128)}, bf16[256,768]{1,0:T(8,128)(2,1)}, f32[1,32]{1,0:T(1,128)}) custom-call(bf16[256,896]{1,0:T(8,128)(2,1)} %bitcast.21, f32[32,768]{1,0:T(8,128)} %get-tuple-element.39.cur_ref), custom_call_target="tpu_custom_call" | custom-call | tf_op jit(solution)/shard_map/update/pallas_call | solution.py:193
  (26 shorter events, 1.6 us)
Async XLA Ops:
  0.6 31.0 %copy-start = (bf16[1024,768]{1,0:T(8,128)(2,1)S(1)}, bf16[1024,768]{1,0:T(8,128)(2,1)}, u32[]{:S(2)}) copy-start(bf16[1024,768]{1,0:T(8,128)(2,1)} %refs_4_.1) | copy-start | bytes 4718596
  2.9 30.4 %collective-permute-start.2 = (bf16[512,768]{1,0:T(8,128)(2,1)}, bf16[512,768]{1,0:T(8,128)(2,1)S(1)}, u32[]{:S(2)}, u32[]{:S(2)}) collective-permute-start(bf16[512,768]{1,0:T(8,128)(2,1)} %constant_dynamic-slice_fusion), channel_id=1, source_target_pairs={{0,24},{8,0},{16,8},{24,16},{1,25},{9,1},{17,9},{25,17},{2,26},{10... | collective-permute-start | bytes 2359304 | tf_op jit(solution)/shard_map/ppermute | solution.py:207
  5.1 35.0 %collective-permute-start.1 = (bf16[512,768]{1,0:T(8,128)(2,1)}, bf16[512,768]{1,0:T(8,128)(2,1)S(1)}, u32[]{:S(2)}, u32[]{:S(2)}) collective-permute-start(bf16[512,768]{1,0:T(8,128)(2,1)} %constant_dynamic-slice_fusion), channel_id=1, source_target_pairs={{0,16},{8,24},{16,0},{24,8},{1,17},{9,25},{17,1},{25,9},{2,18},{10... | collective-permute-start | bytes 2359304 | tf_op jit(solution)/shard_map/ppermute | solution.py:207
  5.8 35.3 %collective-permute-start = (bf16[512,768]{1,0:T(8,128)(2,1)}, bf16[512,768]{1,0:T(8,128)(2,1)}, u32[]{:S(2)}, u32[]{:S(2)}) collective-permute-start(bf16[512,768]{1,0:T(8,128)(2,1)} %constant_dynamic-slice_fusion), channel_id=1, source_target_pairs={{0,8},{8,16},{16,24},{24,0},{1,9},{9,17},{17,25},{25,1},{2,10},{10... | collective-permute-start | bytes 2359304 | tf_op jit(solution)/shard_map/ppermute | solution.py:207
  9.4 22.3 %all-to-all-start = ((bf16[8,32,768]{2,1,0:T(8,128)(2,1)}), bf16[8,32,768]{2,1,0:T(8,128)(2,1)S(1)}, u32[]{:S(2)}, u32[]{:S(2)}) async-start(bf16[8,32,768]{2,1,0:T(8,128)(2,1)} %tile.6), calls=%async_computation | async-start | bytes 786432 | tf_op jit(solution)/shard_map/all_to_all | solution.py:218
  41.2 3.6 %collective-permute-start.3 = (bf16[512,768]{1,0:T(8,128)(2,1)}, bf16[512,768]{1,0:T(8,128)(2,1)S(1)}, u32[]{:S(2)}, u32[]{:S(2)}) collective-permute-start(bf16[512,768]{1,0:T(8,128)(2,1)} %collective-permute-done.refs_3_.refs_7_.refs_5_), channel_id=1, source_target_pairs={{0,1},{1,0},{2,3},{3,2},{4,5},{5,4},{6,7},{7,6},{8,9},{9,8},{10,11... | collective-permute-start | bytes 2359304 | tf_op jit(solution)/shard_map/ppermute | solution.py:207
  41.2 3.6 %collective-permute-start.4 = (bf16[512,768]{1,0:T(8,128)(2,1)S(1)}, bf16[512,768]{1,0:T(8,128)(2,1)S(1)}, u32[]{:S(2)}, u32[]{:S(2)}) collective-permute-start(bf16[512,768]{1,0:T(8,128)(2,1)S(1)} %collective-permute-done.1.refs_5_.refs_9_.refs_7_), channel_id=1, source_target_pairs={{0,1},{1,0},{2,3},{3,2},{4,5},{5,4},{6,7},{7,6},{8,9},{9,8},{10,11... | collective-permute-start | bytes 2359304 | tf_op jit(solution)/shard_map/ppermute | solution.py:207
  41.7 4.0 %collective-permute-start.5 = (bf16[512,768]{1,0:T(8,128)(2,1)S(1)}, bf16[512,768]{1,0:T(8,128)(2,1)S(1)}, u32[]{:S(2)}, u32[]{:S(2)}) collective-permute-start(bf16[512,768]{1,0:T(8,128)(2,1)S(1)} %collective-permute-done.2.refs_7_.refs_11_.refs_9_), channel_id=1, source_target_pairs={{0,1},{1,0},{2,3},{3,2},{4,5},{5,4},{6,7},{7,6},{8,9},{9,8},{10,11... | collective-permute-start | bytes 2359304 | tf_op jit(solution)/shard_map/ppermute | solution.py:207
  44.7 20.4 %copy-start.1 = (bf16[512,768]{1,0:T(8,128)(2,1)}, bf16[512,768]{1,0:T(8,128)(2,1)S(1)}, u32[]{:S(2)}) copy-start(bf16[512,768]{1,0:T(8,128)(2,1)S(1)} %collective-permute-done.3.refs_4_.refs_8_.refs_6_) | copy-start | bytes 2359300
  44.7 20.4 %copy-start.3 = (bf16[512,768]{1,0:T(8,128)(2,1)}, bf16[512,768]{1,0:T(8,128)(2,1)S(1)}, u32[]{:S(2)}) copy-start(bf16[512,768]{1,0:T(8,128)(2,1)S(1)} %collective-permute-done.4.refs_6_.refs_10_.refs_8_) | copy-start | bytes 2359300
  45.7 19.4 %copy-start.5 = (bf16[512,768]{1,0:T(8,128)(2,1)}, bf16[512,768]{1,0:T(8,128)(2,1)S(1)}, u32[]{:S(2)}) copy-start(bf16[512,768]{1,0:T(8,128)(2,1)S(1)} %collective-permute-done.5.refs_8_.refs_12_.refs_10_) | copy-start | bytes 2359300
  49.4 1.3 collective-permute-start.6
  109.5 1.1 copy-start.2
  110.7 1.1 copy-start.4
  111.8 1.1 copy-start.6
  117.3 1.3 collective-permute-start.7
  135.4 0.8 copy-start.7
  136.1 18.6 %all-to-all-start.5 = ((bf16[8,32,896]{2,1,0:T(8,128)(2,1)}), bf16[8,32,896]{2,1,0:T(8,128)(2,1)S(1)}, u32[]{:S(2)}, u32[]{:S(2)}) async-start(bf16[8,32,896]{2,1,0:T(8,128)(2,1)} %bitcast.19), calls=%async_computation.5 | async-start | bytes 917504 | tf_op jit(solution)/shard_map/all_to_all | solution.py:233
  154.8 0.8 copy-start.8

commit v3 on v0

v3 whole, which is shorter than its diff:
```python
import functools
import math

import jax
import jax.numpy as jnp
from jax import lax
from jax.experimental import pallas as pl
from jax.experimental.pallas import tpu as pltpu
from jax.sharding import Mesh
from jax.sharding import PartitionSpec as P

ITERS = 2
D = 768
Z, X, Y, C = 8, 4, 4, 2
OWN = 32
K = Z * OWN
COL = 1024
HALF, QUARTER = COL // 2, COL // 4
PACK = OWN * D // 128 + 16
F32, BF16 = jnp.float32, jnp.bfloat16
SCALE = 50.0 * math.log2(math.e)
VMEM = pl.BlockSpec(memory_space=pltpu.VMEM)
ANY = pl.BlockSpec(memory_space=pl.ANY)
PARTS = ((0,), (1, 3), (2,))
ROWS = tuple(COL * len(part) for part in PARTS)


def in_hbm(v):
    return pltpu.with_memory_space_constraint(v, pltpu.HBM)


def limit(mib):
    return pltpu.CompilerParams(vmem_limit_bytes=mib << 20)


def shape(*dims, dtype=F32):
    return jax.ShapeDtypeStruct(dims, dtype)


def rows_to_tile(v):
    return jnp.concatenate([v[:, i * 128 : (i + 1) * 128] for i in range(v.shape[1] // 128)], axis=0)


def tile_to_rows(v):
    return jnp.concatenate([v[i : i + 1] for i in range(v.shape[0])], axis=1)


def column_of(k, copy=0):
    return pl.ds(pl.multiple_of(32 * copy + 8 * lax.rem(lax.axis_index("x") + (X - k), X), 8), 8)


def prepare_kernel(emb_ref, cent_ref, mine_ref, copies_ref, cent, sems, cent_sem):
    read = pltpu.make_async_copy(cent_ref, cent, cent_sem)
    read.start()
    at = pl.multiple_of(lax.axis_index("c") * HALF, HALF)
    waits = []
    for i in range(0, HALF, 64):
        waits.append(
            pltpu.make_async_copy(
                emb_ref.at[pl.ds(at + i, 64)], mine_ref.at[pl.ds(i, 64)], sems.at[i // 64]
            )
        )
        waits[-1].start()
    read.wait()
    for i in range(Z):
        copies_ref[pl.ds(i * OWN, OWN), :] = cent[...].astype(BF16)
    for wait in waits:
        wait.wait()


def prepare(emb, cent):
    return pl.pallas_call(
        prepare_kernel,
        out_shape=(pltpu.VMEM((HALF, D), BF16), pltpu.VMEM((K, D), BF16)),
        in_specs=[ANY, ANY],
        out_specs=(VMEM,) * 2,
        scratch_shapes=[
            pltpu.VMEM((OWN, D), F32),
            pltpu.SemaphoreType.DMA((HALF // 64,)),
            pltpu.SemaphoreType.DMA,
        ],
        compiler_params=limit(4),
        name="prepare",
    )(in_hbm(emb), in_hbm(cent))


def relay_kernel(left_ref, right_ref, low_ref, high_ref):
    low_ref[...] = left_ref[pl.ds(0, QUARTER), :]
    high_ref[...] = right_ref[pl.ds(QUARTER, QUARTER), :]


def relay(left, right):
    return pl.pallas_call(
        relay_kernel,
        out_shape=(pltpu.VMEM((QUARTER, D), BF16),) * 2,
        in_specs=[VMEM] * 2,
        out_specs=(VMEM,) * 2,
        compiler_params=limit(4),
        name="relay",
    )(left, right)


def score_rows(cent, half_squares, emb, p_ref, m_ref):
    dots = lax.dot_general(cent, emb, (((1,), (1,)), ((), ())), preferred_element_type=F32)
    logits = dots * SCALE - half_squares
    peak = jnp.max(logits, axis=0, keepdims=True)
    p = jnp.exp2(logits - peak)
    total = jnp.sum(p, axis=0, keepdims=True)
    p_ref[...] = p.astype(BF16)
    m_ref[...] = rows_to_tile(peak)
    return rows_to_tile(peak + jnp.log2(total))


def half_squares_of(cent):
    wide = cent.astype(F32)
    return (0.5 * SCALE) * jnp.sum(wide * wide, axis=1, keepdims=True)


def spread(part, lse, lses_ref):
    for j, k in enumerate(part):
        for i in range(X * Y):
            lses_ref[column_of(k, i), :] = lse[8 * j : 8 * j + 8]


def arrive_kernel(part, before, cent_ref, *refs):
    emb, p_ref, m_ref, l_ref = refs[-4:]
    pieces = refs[: len(refs) - 4 - before]
    earlier = refs[len(pieces) : -4]
    c = lax.axis_index("c")
    cent = cent_ref[...].astype(BF16)
    half_squares = half_squares_of(cent)
    if part == (0,):
        emb[...] = pieces[0][...]
    else:
        size = pieces[0].shape[0]
        n = HALF // size
        for i, piece in enumerate(pieces):
            half = c if i // n % 2 == 0 else 1 - c
            at = pl.multiple_of(i // (2 * n) * COL + half * HALF + i % n * size, size)
            emb[pl.ds(at, size), :] = piece[...]
    lse = score_rows(cent, half_squares, emb[...], p_ref, m_ref)
    if before:
        spread(part, lse, l_ref)
        for other, ref in zip(PARTS, earlier):
            spread(other, ref[...], l_ref)
    else:
        l_ref[...] = lse


def arrive(cent, part, pieces, earlier=()):
    rows = COL * len(part)
    return pl.pallas_call(
        functools.partial(arrive_kernel, part, len(earlier)),
        out_shape=(
            pltpu.VMEM((rows, D), BF16),
            pltpu.VMEM((K, rows), BF16),
            pltpu.VMEM((rows // 128, 128), F32),
            shape(X * Y * 32 if earlier else rows // 128, 128),
        ),
        in_specs=[VMEM] * (1 + len(pieces) + len(earlier)),
        out_specs=(VMEM,) * 4,
        compiler_params=limit(16),
        name="arrive",
    )(cent, *pieces, *earlier)


def score_kernel(cent_ref, *refs):
    n = len(PARTS)
    embs, ps, ms, l_ref = refs[:n], refs[n : 2 * n], refs[2 * n : 3 * n], refs[3 * n]
    cent = cent_ref[...]
    half_squares = half_squares_of(cent)
    for part, emb, p_ref, m_ref in zip(PARTS, embs, ps, ms):
        spread(part, score_rows(cent, half_squares, emb[...], p_ref, m_ref), l_ref)


def score(cent, embs):
    n = len(PARTS)
    outs = pl.pallas_call(
        score_kernel,
        out_shape=(
            *(pltpu.VMEM((K, r), BF16) for r in ROWS),
            *(pltpu.VMEM((r // 128, 128), F32) for r in ROWS),
            shape(X * Y * 32, 128),
        ),
        in_specs=[VMEM] * (1 + n),
        out_specs=(VMEM,) * (2 * n + 1),
        compiler_params=limit(16),
        name="score",
    )(cent, *embs)
    return outs[:n], outs[n : 2 * n], outs[2 * n]


def sum_kernel(lses_ref, others_ref, *refs):
    n = len(PARTS)
    ps, ms, embs = refs[:n], refs[n : 2 * n], refs[2 * n : 3 * n]
    out_ref, row_ref, lse_ref = refs[3 * n :]
    lses = [r[pl.ds(i * 32, 32), :] for r in (lses_ref, others_ref) for i in range(X * Y)]
    peak = functools.reduce(jnp.maximum, lses)
    total = sum(jnp.exp2(v - peak) for v in lses)
    lse_ref[...] = peak + jnp.log2(total)
    row_ref[...] = lse_ref[column_of(0), :] * math.log(2.0)
    weights = jnp.zeros((K, 128), F32)
    sums = jnp.zeros((K, D), F32)
    for part, p_ref, m_ref, emb in zip(PARTS, ps, ms, embs):
        resps = []
        for j, k in enumerate(part):
            factor = tile_to_rows(jnp.exp2(m_ref[pl.ds(j * 8, 8), :] - lse_ref[column_of(k), :]))
            resp = (p_ref[:, pl.ds(j * COL, COL)].astype(F32) * factor).astype(BF16)
            wide = resp.astype(F32)
            for i in range(COL // 128):
                weights += wide[:, i * 128 : (i + 1) * 128]
            resps.append(resp)
        sums += jnp.dot(jnp.concatenate(resps, axis=1), emb[...], preferred_element_type=F32)
    counts = jnp.sum(weights, axis=1, keepdims=True)
    high = counts.astype(BF16).astype(F32)
    low = counts - high
    lane = lax.broadcasted_iota(jnp.int32, (16, 128), 1)
    for i in range(Z):
        for t in range(D // 128):
            out_ref[pl.ds(i * PACK + t * OWN, OWN), :] = sums[
                i * OWN : (i + 1) * OWN, t * 128 : (t + 1) * 128
            ].astype(BF16)
        tail = jnp.zeros((16, 128), F32)
        for q, v in enumerate((high, low)):
            for h in range(2):
                at = i * OWN + h * 16
                tail = jnp.where(lane == 2 * q + h, v[at : at + 16], tail)
        out_ref[pl.ds(i * PACK + PACK - 16, 16), :] = tail.astype(BF16)


def sums_of(lses, others, ps, ms, embs):
    n = len(PARTS)
    return pl.pallas_call(
        sum_kernel,
        out_shape=(shape(Z * PACK, 128, dtype=BF16), shape(8, 128)),
        in_specs=[VMEM] * (2 + 3 * n),
        out_specs=(VMEM, VMEM),
        scratch_shapes=[pltpu.VMEM((X * 8, 128), F32)],
        compiler_params=limit(16),
        name="sums",
    )(lses, others, *ps, *ms, *embs)


def update_kernel(last, got_ref, cur_ref, new_ref, out_ref):
    def total(at, n):
        return sum(got_ref[pl.ds(i * PACK + at, n), :].astype(F32) for i in range(Z))

    tail = total(PACK - 16, 16)
    tail = tail[:, :2] + tail[:, 2:4]
    counts = jnp.concatenate([tail[:, :1], tail[:, 1:]], axis=0)
    for t in range(D // 128):
        lanes = slice(t * 128, (t + 1) * 128)
        new = (total(t * OWN, OWN) + cur_ref[:, lanes]) / (counts + 1.0)
        new_ref[:, lanes] = new
        if not last:
            for i in range(Z):
                out_ref[pl.ds(i * OWN, OWN), lanes] = new.astype(BF16)
    if last:
        row = lax.broadcasted_iota(jnp.int32, (OWN, OWN), 0)
        lane = lax.broadcasted_iota(jnp.int32, (OWN, OWN), 1)
        out_ref[...] = jnp.sum(jnp.where(row == lane, counts, 0.0), axis=0, keepdims=True)


def update(got, current, last):
    return pl.pallas_call(
        functools.partial(update_kernel, last),
        out_shape=(shape(OWN, D), shape(1, OWN) if last else shape(K, D, dtype=BF16)),
        in_specs=[VMEM, VMEM],
        out_specs=(VMEM, VMEM),
        compiler_params=limit(8),
        name="update",
    )(got, current)


def shift(v, axis, size, k):
    return lax.ppermute(v, axis, [(i, (i + k) % size) for i in range(size)])


def swap(v):
    return shift(v, "c", C, 1)


def on_device(embeddings, centroids):
    mine, copies = prepare(embeddings, centroids)
    left, right = shift(mine, "x", X, 1), shift(mine, "x", X, 3)
    cent = lax.all_to_all(copies, "z", 0, 0, tiled=True)
    own = arrive(cent, PARTS[0], (embeddings,))
    left, right, first = lax.optimization_barrier((left, right, own[3]))
    low, high = relay(left, right)
    far_low, far_high = shift(low, "x", X, 1), shift(high, "x", X, 3)
    near = arrive(cent, PARTS[1], (left, swap(left), right, swap(right)))
    far_low, far_high, second = lax.optimization_barrier((far_low, far_high, near[3]))
    far = arrive(cent, PARTS[2], (far_low, far_high, swap(far_low), swap(far_high)), (first, second))
    embs, ps, ms, (_, _, lses) = zip(own, near, far)
    current = centroids
    for step in range(ITERS):
        if step > 0:
            cent = lax.all_to_all(out, "z", 0, 0, tiled=True)
            ps, ms, lses = score(cent, embs)
        lses = lax.all_to_all(lses, ("x", "y"), 0, 0, tiled=True)
        sums, row_lse = sums_of(lses, swap(lses), ps, ms, embs)
        got = lax.all_to_all(sums, "z", 0, 0, tiled=True)
        current, out = update(got, current, step == ITERS - 1)
    return current, out.reshape(OWN), row_lse.reshape(COL)


def solution(mesh):
    split = Mesh(mesh.devices.reshape(Z, X, Y, C), ("z", "x", "y", "c"))
    dp, every = ("z", "x"), ("z", "x", "y", "c")
    return jax.shard_map(
        on_device,
        mesh=split,
        in_specs=(P(dp, None), P(every, None)),
        out_specs=(P(every, None), P(every), P(dp)),
        check_vma=False,
    )
```

time: 491 us -> 140 us (0.29)
  waiting for transfers between devices: 240 us -> 14.3 us
  blocking collectives: 193 us -> 104 us
  matrix products: 21.4 us -> 0 us
  other arithmetic: 19.8 us -> 0 us
  Pallas kernels: 0 us -> 13.2 us
  between operations: 13.9 us -> 0.71 us
  starting transfers between devices: 0.12 us -> 5.56 us
    psum x4 -> x0, blocking collectives: 168 us -> none  [the longest x2 143 us: on_device(): all_sums, all_counts = lax.psum((sums, weights), 'dp')]
    psum x2 -> x0, waiting for transfers between devices: 155 us -> none  [on_device(): all_sums, all_counts = lax.psum((sums, weights), 'dp')]
    all_to_all x0 -> x6, blocking collectives: none -> 104 us  [the longest x2 38.7 us: on_device(): got = lax.all_to_all(sums, 'z', 0, 0, tiled=True)]
    all_gather x1 -> x0, waiting for transfers between devices: 84.3 us -> none  [on_device(): whole = lax.all_gather(centroids, 'dp', axis=0, tiled=True)]
    pmax x2 -> x0, blocking collectives: 24.8 us -> none  [expect(): global_peak = lax.pmax(local_peak, 'cent')]
    dot_general x4 -> x0, matrix products: 21.4 us -> none  [the longest x2 12 us: expect(): lax.dot_general(resp, embeddings, (((0,), (0,)), ((), ())), preferred_ele...]
    reduce_sum x6 -> x0, other arithmetic: 18.1 us -> none  [the longest x2 6.3 us: expect(): weights = jnp.sum(resp.astype(jnp.float32), axis=0)]
    ppermute x0 -> x10, waiting for transfers between devices: none -> 14.3 us  [shift(): return lax.ppermute(v, axis, [(i, (i + k) % size) for i in range(size)])]
  transfers between devices with their start and end apart: 3 -> 10, of which waited for: 3 -> 7; matrix products, arithmetic and copies ran while one was open for 1% -> 0% of each run, Pallas kernels for 0% -> 2%
where the time goes in v3:
time: 140 us; the launch traced here: 138 us
  blocking collectives  104 us (74%)
  waiting for transfers between devices  14.3 us (10%)
  Pallas kernels  13.2 us (9%)
  starting transfers between devices  5.56 us (4%)
    all_to_all x2, blocking collectives, on_device(): got = lax.all_to_all(sums, 'z', 0, 0, tiled=True)  38.7 us
    all_to_all x2, blocking collectives, on_device(): lses = lax.all_to_all(lses, ('x', 'y'), 0, 0, tiled=True)  26.7 us
    all_to_all x1, blocking collectives, on_device(): cent = lax.all_to_all(copies, 'z', 0, 0, tiled=True)  22.1 us
    all_to_all x1, blocking collectives, on_device(): cent = lax.all_to_all(out, 'z', 0, 0, tiled=True)  16.3 us
    ppermute x10, waiting for transfers between devices, shift(): return lax.ppermute(v, axis, [(i, (i + k) % size) for i in range(size)])  14.3 us
    ppermute x10, starting transfers between devices, shift(): return lax.ppermute(v, axis, [(i, (i + k) % size) for i in range(size)])  5.56 us
    pallas_call x2, Pallas kernels, sums_of(): pl.pallas_call(sum_kernel, out_shape=(shape(Z * PACK, 128, dtype=BF16), s...  5.11 us
    pallas_call x3, Pallas kernels, arrive(): pl.pallas_call(functools.partial(arrive_kernel, part, len(earlier)), out_...  3.24 us
  transfers between devices with their start and end apart: 10, of which 7 were waited for; matrix products, arithmetic and copies ran while one was open for 0% of the time, Pallas kernels for 2%

profile of v3, /device:TPU:2, one launch (start us, length us, event | category | flops | bytes accessed | tf_op | source)
XLA Modules:
  0.0 137.6 jit_solution(2516963407836969622)
XLA Ops:
  0.6 1.5 %prepare.1 = (bf16[512,768]{1,0:T(8,128)(2,1)S(1)}, bf16[256,768]{1,0:T(8,128)(2,1)S(1)}) custom-call(bf16[1024,768]{1,0:T(8,128)(2,1)} %refs_0_.1, f32[32,768]{1,0:T(8,128)} %cur_ref.1), custom_call_target="tpu_custom_call" | custom-call | tf_op jit(solution)/shard_map/prepare/pallas_call | solution.py:72
  2.1 2.3 %collective-permute-start.1 = (bf16[512,768]{1,0:T(8,128)(2,1)S(1)}, bf16[512,768]{1,0:T(8,128)(2,1)S(1)}, u32[]{:S(2)}, u32[]{:S(2)}) collective-permute-start(bf16[512,768]{1,0:T(8,128)(2,1)S(1)} %get-tuple-element.40), channel_id=1, source_target_pairs={{0,24},{8,0},{16,8},{24,16},{1,25},{9,1},{17,9},{25,17},{2,26},{10... | collective-permute-start | bytes 2359304 | tf_op jit(solution)/shard_map/ppermute | solution.py:276
  4.4 0.0 collective-permute-start
  4.4 22.1 %all_to_all.66 = bf16[8,32,768]{2,1,0:T(8,128)(2,1)S(1)} all-to-all(bf16[8,32,768]{2,1,0:T(8,128)(2,1)S(1)} %bitcast.26), channel_id=1, replica_groups=mesh['z'=8,'x'=4,'y'=4,'c'=2] {'z'}, dimensions={0} | all-to-all | bytes 786432 | tf_op jit(solution)/shard_map/all_to_all | solution.py:286
  26.6 0.8 arrive.3
  27.4 0.0 collective-permute-done.1.right_ref.refs_2_
  27.4 0.1 collective-permute-start.4
  27.5 0.5 collective-permute-start.5
  28.0 0.1 relay.1
  28.1 1.6 %collective-permute-start.2 = (bf16[256,768]{1,0:T(8,128)(2,1)S(1)}, bf16[256,768]{1,0:T(8,128)(2,1)S(1)}, u32[]{:S(2)}, u32[]{:S(2)}) collective-permute-start(bf16[256,768]{1,0:T(8,128)(2,1)S(1)} %get-tuple-element.44), channel_id=1, source_target_pairs={{0,8},{8,16},{16,24},{24,0},{1,9},{9,17},{17,25},{25,1},{2,10},{10... | collective-permute-start | bytes 1179656 | tf_op jit(solution)/shard_map/ppermute | solution.py:276
  29.6 0.5 collective-permute-start.3
  30.2 0.0 collective-permute-done.4.refs_1_
  30.2 0.7 collective-permute-done.5.refs_3_
  30.9 1.5 %arrive.4 = (bf16[2048,768]{1,0:T(8,128)(2,1)S(1)}, bf16[256,2048]{1,0:T(8,128)(2,1)S(1)}, f32[16,128]{1,0:T(8,128)S(1)}, f32[16,128]{1,0:T(8,128)S(1)}) custom-call(bf16[256,768]{1,0:T(8,128)(2,1)S(1)} %bitcast.15, bf16[512,768]{1,0:T(8,128)(2,1)S(1)} %collective-permute-done.left_ref.refs_0_, bf16[512,768]{1,0:T(8,128)(2,1)S(1)} %collective-permute-done.4.refs_1_, ...), custom_call_target="tpu_custom_call" | custom-call | tf_op jit(solution)/shard_map/arrive/pallas_call | solution.py:152
  32.4 6.9 %collective-permute-done.2.refs_0_ = bf16[256,768]{1,0:T(8,128)(2,1)S(1)} collective-permute-done((bf16[256,768]{1,0:T(8,128)(2,1)S(1)}, bf16[256,768]{1,0:T(8,128)(2,1)S(1)}, u32[]{:S(2)}, u32[]{:S(2)}) %collective-permute-start.2) | collective-permute-done | bytes 393248 | tf_op jit(solution)/shard_map/ppermute | solution.py:276
  39.3 1.9 %collective-permute-done.3.refs_1_ = bf16[256,768]{1,0:T(8,128)(2,1)S(1)} collective-permute-done((bf16[256,768]{1,0:T(8,128)(2,1)S(1)}, bf16[256,768]{1,0:T(8,128)(2,1)S(1)}, u32[]{:S(2)}, u32[]{:S(2)}) %collective-permute-start.3) | collective-permute-done | bytes 393248 | tf_op jit(solution)/shard_map/ppermute | solution.py:276
  41.1 0.5 collective-permute-start.7
  41.7 1.2 collective-permute-done.6.refs_2_
  42.9 0.6 collective-permute-done.7.refs_3_
  43.4 0.9 arrive.5
  44.4 14.7 %all_to_all.67 = f32[16,32,128]{2,1,0:T(8,128)S(1)} all-to-all(f32[16,32,128]{2,1,0:T(8,128)S(1)} %bitcast.28), channel_id=1, replica_groups=mesh['z'=8,'x'=4,'y'=4,'c'=2] {'x','y'}, dimensions={0} | all-to-all | bytes 524288 | tf_op jit(solution)/shard_map/all_to_all | solution.py:300
  59.1 1.5 %collective-permute-done.8.others_ref = f32[512,128]{1,0:T(8,128)S(1)} collective-permute-done((f32[512,128]{1,0:T(8,128)S(1)}, f32[512,128]{1,0:T(8,128)S(1)}, u32[]{:S(2)}, u32[]{:S(2)}) %collective-permute-start.8) | collective-permute-done | bytes 262176 | tf_op jit(solution)/shard_map/ppermute | solution.py:276
  60.6 2.6 %sums.2 = (bf16[1664,128]{1,0:T(8,128)(2,1)S(1)}, f32[8,128]{1,0:T(8,128)}) custom-call(f32[512,128]{1,0:T(8,128)S(1)} %bitcast.23, f32[512,128]{1,0:T(8,128)S(1)} %collective-permute-done.8.others_ref, bf16[256,1024]{1,0:T(8,128)(2,1)S(1)} %get-tuple-element.52.refs_0_, bf16[256,2048]{1,0:T(8,128)(2,1)S(1)} %get-tuple-element.53.refs_1_, ...), custom_call_target="tpu_custom_call" | custom-call | tf_op jit(solution)/shard_map/sums/pallas_call | solution.py:233
  63.2 20.4 %all_to_all.68 = bf16[8,208,128]{2,1,0:T(8,128)(2,1)S(1)} all-to-all(bf16[8,208,128]{2,1,0:T(8,128)(2,1)S(1)} %bitcast.25), channel_id=1, replica_groups=mesh['z'=8,'x'=4,'y'=4,'c'=2] {'z'}, dimensions={0} | all-to-all | bytes 851968 | tf_op jit(solution)/shard_map/all_to_all | solution.py:302
  83.6 0.2 update.2
  83.8 16.3 %all_to_all.69 = bf16[8,32,768]{2,1,0:T(8,128)(2,1)S(1)} all-to-all(bf16[8,32,768]{2,1,0:T(8,128)(2,1)S(1)} %bitcast.27), channel_id=1, replica_groups=mesh['z'=8,'x'=4,'y'=4,'c'=2] {'z'}, dimensions={0} | all-to-all | bytes 786432 | tf_op jit(solution)/shard_map/all_to_all | solution.py:298
  100.1 2.2 %score.1 = (bf16[256,1024]{1,0:T(8,128)(2,1)S(1)}, bf16[256,2048]{1,0:T(8,128)(2,1)S(1)}, bf16[256,1024]{1,0:T(8,128)(2,1)S(1)}, f32[8,128]{1,0:T(8,128)S(1)}, f...) custom-call(bf16[256,768]{1,0:T(8,128)(2,1)S(1)} %bitcast.19, ...), custom_call_target="tpu_custom_call" | custom-call | tf_op jit(solution)/shard_map/score/pallas_call | solution.py:178
  102.3 12.0 %all_to_all.70 = f32[16,32,128]{2,1,0:T(8,128)S(1)} all-to-all(f32[16,32,128]{2,1,0:T(8,128)S(1)} %bitcast.29), channel_id=1, replica_groups=mesh['z'=8,'x'=4,'y'=4,'c'=2] {'x','y'}, dimensions={0} | all-to-all | bytes 524288 | tf_op jit(solution)/shard_map/all_to_all | solution.py:300
  114.3 1.5 %collective-permute-done.9.others_ref = f32[512,128]{1,0:T(8,128)S(1)} collective-permute-done((f32[512,128]{1,0:T(8,128)S(1)}, f32[512,128]{1,0:T(8,128)S(1)}, u32[]{:S(2)}, u32[]{:S(2)}) %collective-permute-start.9) | collective-permute-done | bytes 262176 | tf_op jit(solution)/shard_map/ppermute | solution.py:276
  115.8 2.5 %sums.3 = (bf16[1664,128]{1,0:T(8,128)(2,1)S(1)}, f32[8,128]{1,0:T(8,128)}) custom-call(f32[512,128]{1,0:T(8,128)S(1)} %bitcast.21, f32[512,128]{1,0:T(8,128)S(1)} %collective-permute-done.9.others_ref, bf16[256,1024]{1,0:T(8,128)(2,1)S(1)} %get-tuple-element.64.refs_0_, bf16[256,2048]{1,0:T(8,128)(2,1)S(1)} %get-tuple-element.65.refs_1_, ...), custom_call_target="tpu_custom_call" | custom-call | tf_op jit(solution)/shard_map/sums/pallas_call | solution.py:233
  118.4 18.3 %all_to_all.71 = bf16[8,208,128]{2,1,0:T(8,128)(2,1)S(1)} all-to-all(bf16[8,208,128]{2,1,0:T(8,128)(2,1)S(1)} %bitcast.24), channel_id=1, replica_groups=mesh['z'=8,'x'=4,'y'=4,'c'=2] {'z'}, dimensions={0} | all-to-all | bytes 851968 | tf_op jit(solution)/shard_map/all_to_all | solution.py:302
  136.7 0.9 update.3
  (8 shorter events, 0.0 us)
Async XLA Ops:
  0.6 26.0 %copy-start = (bf16[1024,768]{1,0:T(8,128)(2,1)S(1)}, bf16[1024,768]{1,0:T(8,128)(2,1)}, u32[]{:S(2)}) copy-start(bf16[1024,768]{1,0:T(8,128)(2,1)} %refs_0_.1) | copy-start | bytes 4718596
  2.1 25.3 %collective-permute-start.1 = (bf16[512,768]{1,0:T(8,128)(2,1)S(1)}, bf16[512,768]{1,0:T(8,128)(2,1)S(1)}, u32[]{:S(2)}, u32[]{:S(2)}) collective-permute-start(bf16[512,768]{1,0:T(8,128)(2,1)S(1)} %get-tuple-element.40), channel_id=1, source_target_pairs={{0,24},{8,0},{16,8},{24,16},{1,25},{9,1},{17,9},{25,17},{2,26},{10... | collective-permute-start | bytes 2359304 | tf_op jit(solution)/shard_map/ppermute | solution.py:276
  4.4 23.0 %collective-permute-start = (bf16[512,768]{1,0:T(8,128)(2,1)S(1)}, bf16[512,768]{1,0:T(8,128)(2,1)S(1)}, u32[]{:S(2)}, u32[]{:S(2)}) collective-permute-start(bf16[512,768]{1,0:T(8,128)(2,1)S(1)} %get-tuple-element.40), channel_id=1, source_target_pairs={{0,8},{8,16},{16,24},{24,0},{1,9},{9,17},{17,25},{25,1},{2,10},{10... | collective-permute-start | bytes 2359304 | tf_op jit(solution)/shard_map/ppermute | solution.py:276
  27.4 2.8 %collective-permute-start.4 = (bf16[512,768]{1,0:T(8,128)(2,1)S(1)}, bf16[512,768]{1,0:T(8,128)(2,1)S(1)}, u32[]{:S(2)}, u32[]{:S(2)}) collective-permute-start(bf16[512,768]{1,0:T(8,128)(2,1)S(1)} %collective-permute-done.left_ref.refs_0_), channel_id=1, source_target_pairs={{0,1},{1,0},{2,3},{3,2},{4,5},{5,4},{6,7},{7,6},{8,9},{9,8},{10,11... | collective-permute-start | bytes 2359304 | tf_op jit(solution)/shard_map/ppermute | solution.py:276
  27.5 3.4 %collective-permute-start.5 = (bf16[512,768]{1,0:T(8,128)(2,1)S(1)}, bf16[512,768]{1,0:T(8,128)(2,1)S(1)}, u32[]{:S(2)}, u32[]{:S(2)}) collective-permute-start(bf16[512,768]{1,0:T(8,128)(2,1)S(1)} %collective-permute-done.1.right_ref.refs_2_), channel_id=1, source_target_pairs={{0,1},{1,0},{2,3},{3,2},{4,5},{5,4},{6,7},{7,6},{8,9},{9,8},{10,11... | collective-permute-start | bytes 2359304 | tf_op jit(solution)/shard_map/ppermute | solution.py:276
  28.1 11.2 %collective-permute-start.2 = (bf16[256,768]{1,0:T(8,128)(2,1)S(1)}, bf16[256,768]{1,0:T(8,128)(2,1)S(1)}, u32[]{:S(2)}, u32[]{:S(2)}) collective-permute-start(bf16[256,768]{1,0:T(8,128)(2,1)S(1)} %get-tuple-element.44), channel_id=1, source_target_pairs={{0,8},{8,16},{16,24},{24,0},{1,9},{9,17},{17,25},{25,1},{2,10},{10... | collective-permute-start | bytes 1179656 | tf_op jit(solution)/shard_map/ppermute | solution.py:276
  29.6 11.5 %collective-permute-start.3 = (bf16[256,768]{1,0:T(8,128)(2,1)S(1)}, bf16[256,768]{1,0:T(8,128)(2,1)S(1)}, u32[]{:S(2)}, u32[]{:S(2)}) collective-permute-start(bf16[256,768]{1,0:T(8,128)(2,1)S(1)} %get-tuple-element.45), channel_id=1, source_target_pairs={{0,24},{8,0},{16,8},{24,16},{1,25},{9,1},{17,9},{25,17},{2,26},{10... | collective-permute-start | bytes 1179656 | tf_op jit(solution)/shard_map/ppermute | solution.py:276
  41.1 1.7 %collective-permute-start.6 = (bf16[256,768]{1,0:T(8,128)(2,1)S(1)}, bf16[256,768]{1,0:T(8,128)(2,1)S(1)}, u32[]{:S(2)}, u32[]{:S(2)}) collective-permute-start(bf16[256,768]{1,0:T(8,128)(2,1)S(1)} %collective-permute-done.2.refs_0_), channel_id=1, source_target_pairs={{0,1},{1,0},{2,3},{3,2},{4,5},{5,4},{6,7},{7,6},{8,9},{9,8},{10,11... | collective-permute-start | bytes 1179656 | tf_op jit(solution)/shard_map/ppermute | solution.py:276
  41.1 2.3 %collective-permute-start.7 = (bf16[256,768]{1,0:T(8,128)(2,1)S(1)}, bf16[256,768]{1,0:T(8,128)(2,1)S(1)}, u32[]{:S(2)}, u32[]{:S(2)}) collective-permute-start(bf16[256,768]{1,0:T(8,128)(2,1)S(1)} %collective-permute-done.3.refs_1_), channel_id=1, source_target_pairs={{0,1},{1,0},{2,3},{3,2},{4,5},{5,4},{6,7},{7,6},{8,9},{9,8},{10,11... | collective-permute-start | bytes 1179656 | tf_op jit(solution)/shard_map/ppermute | solution.py:276
  59.1 1.5 %collective-permute-start.8 = (f32[512,128]{1,0:T(8,128)S(1)}, f32[512,128]{1,0:T(8,128)S(1)}, u32[]{:S(2)}, u32[]{:S(2)}) collective-permute-start(f32[512,128]{1,0:T(8,128)S(1)} %bitcast.22), channel_id=1, source_target_pairs={{0,1},{1,0},{2,3},{3,2},{4,5},{5,4},{6,7},{7,6},{8,9},{9,8},{10,11... | collective-permute-start | bytes 786440 | tf_op jit(solution)/shard_map/ppermute | solution.py:276
  60.6 22.9 %copy-start.1 = (f32[32,768]{1,0:T(8,128)S(1)}, f32[32,768]{1,0:T(8,128)}, u32[]{:S(2)}) copy-start(f32[32,768]{1,0:T(8,128)} %cur_ref.1) | copy-start | bytes 294916
  114.3 1.5 %collective-permute-start.9 = (f32[512,128]{1,0:T(8,128)S(1)}, f32[512,128]{1,0:T(8,128)S(1)}, u32[]{:S(2)}, u32[]{:S(2)}) collective-permute-start(f32[512,128]{1,0:T(8,128)S(1)} %bitcast.20), channel_id=1, source_target_pairs={{0,1},{1,0},{2,3},{3,2},{4,5},{5,4},{6,7},{7,6},{8,9},{9,8},{10,11... | collective-permute-start | bytes 786440 | tf_op jit(solution)/shard_map/ppermute | solution.py:276

commit v4 on v3

--- a/solution.py
+++ b/solution.py
@@ -45,8 +45,8 @@
     return jnp.concatenate([v[i : i + 1] for i in range(v.shape[0])], axis=1)
 
 
-def column_of(k, copy=0):
-    return pl.ds(pl.multiple_of(32 * copy + 8 * lax.rem(lax.axis_index("x") + (X - k), X), 8), 8)
+def column_of(k):
+    return pl.ds(pl.multiple_of(8 * lax.rem(lax.axis_index("x") + (X - k), X), 8), 8)
 
 
 def prepare_kernel(emb_ref, cent_ref, mine_ref, copies_ref, cent, sems, cent_sem):
@@ -116,10 +116,9 @@
     return (0.5 * SCALE) * jnp.sum(wide * wide, axis=1, keepdims=True)
 
 
-def spread(part, lse, lses_ref):
+def spread(part, lse, lse_ref):
     for j, k in enumerate(part):
-        for i in range(X * Y):
-            lses_ref[column_of(k, i), :] = lse[8 * j : 8 * j + 8]
+        lse_ref[column_of(k), :] = lse[8 * j : 8 * j + 8]
 
 
 def arrive_kernel(part, before, cent_ref, *refs):
@@ -155,7 +154,7 @@
             pltpu.VMEM((rows, D), BF16),
             pltpu.VMEM((K, rows), BF16),
             pltpu.VMEM((rows // 128, 128), F32),
-            shape(X * Y * 32 if earlier else rows // 128, 128),
+            pltpu.VMEM((X * 8 if earlier else rows // 128, 128), F32),
         ),
         in_specs=[VMEM] * (1 + len(pieces) + len(earlier)),
         out_specs=(VMEM,) * 4,
@@ -180,7 +179,7 @@
         out_shape=(
             *(pltpu.VMEM((K, r), BF16) for r in ROWS),
             *(pltpu.VMEM((r // 128, 128), F32) for r in ROWS),
-            shape(X * Y * 32, 128),
+            pltpu.VMEM((X * 8, 128), F32),
         ),
         in_specs=[VMEM] * (1 + n),
         out_specs=(VMEM,) * (2 * n + 1),
@@ -190,11 +189,30 @@
     return outs[:n], outs[n : 2 * n], outs[2 * n]
 
 
-def sum_kernel(lses_ref, others_ref, *refs):
+def combine_kernel(a_ref, b_ref, out_ref):
+    a, b = a_ref[...], b_ref[...]
+    peak = jnp.maximum(a, b)
+    both = peak + jnp.log2(jnp.exp2(a - peak) + jnp.exp2(b - peak))
+    for i in range(X * Y):
+        out_ref[pl.ds(i * 32, 32), :] = both
+
+
+def combine(a, b):
+    return pl.pallas_call(
+        combine_kernel,
+        out_shape=pltpu.VMEM((X * Y * 32, 128), F32),
+        in_specs=[VMEM] * 2,
+        out_specs=VMEM,
+        compiler_params=limit(2),
+        name="combine",
+    )(a, b)
+
+
+def sum_kernel(lses_ref, *refs):
     n = len(PARTS)
     ps, ms, embs = refs[:n], refs[n : 2 * n], refs[2 * n : 3 * n]
     out_ref, row_ref, lse_ref = refs[3 * n :]
-    lses = [r[pl.ds(i * 32, 32), :] for r in (lses_ref, others_ref) for i in range(X * Y)]
+    lses = [lses_ref[pl.ds(i * 32, 32), :] for i in range(X * Y)]
     peak = functools.reduce(jnp.maximum, lses)
     total = sum(jnp.exp2(v - peak) for v in lses)
     lse_ref[...] = peak + jnp.log2(total)
@@ -228,17 +246,17 @@
         out_ref[pl.ds(i * PACK + PACK - 16, 16), :] = tail.astype(BF16)
 
 
-def sums_of(lses, others, ps, ms, embs):
+def sums_of(lses, ps, ms, embs):
     n = len(PARTS)
     return pl.pallas_call(
         sum_kernel,
         out_shape=(shape(Z * PACK, 128, dtype=BF16), shape(8, 128)),
-        in_specs=[VMEM] * (2 + 3 * n),
+        in_specs=[VMEM] * (1 + 3 * n),
         out_specs=(VMEM, VMEM),
         scratch_shapes=[pltpu.VMEM((X * 8, 128), F32)],
         compiler_params=limit(16),
         name="sums",
-    )(lses, others, *ps, *ms, *embs)
+    )(lses, *ps, *ms, *embs)
 
 
 def update_kernel(last, got_ref, cur_ref, new_ref, out_ref):
@@ -280,10 +298,16 @@
     return shift(v, "c", C, 1)
 
 
+def exchange(v, axes, n):
+    second = list(range(n))[::-1]
+    groups = [[C * i for i in range(n)], [C * i + 1 for i in second]]
+    return lax.all_to_all(v, (*axes, "c"), 0, 0, axis_index_groups=groups, tiled=True)
+
+
 def on_device(embeddings, centroids):
     mine, copies = prepare(embeddings, centroids)
     left, right = shift(mine, "x", X, 1), shift(mine, "x", X, 3)
-    cent = lax.all_to_all(copies, "z", 0, 0, tiled=True)
+    cent = exchange(copies, ("z",), Z)
     own = arrive(cent, PARTS[0], (embeddings,))
     left, right, first = lax.optimization_barrier((left, right, own[3]))
     low, high = relay(left, right)
@@ -291,15 +315,15 @@
     near = arrive(cent, PARTS[1], (left, swap(left), right, swap(right)))
     far_low, far_high, second = lax.optimization_barrier((far_low, far_high, near[3]))
     far = arrive(cent, PARTS[2], (far_low, far_high, swap(far_low), swap(far_high)), (first, second))
-    embs, ps, ms, (_, _, lses) = zip(own, near, far)
+    embs, ps, ms, (_, _, lse) = zip(own, near, far)
     current = centroids
     for step in range(ITERS):
         if step > 0:
-            cent = lax.all_to_all(out, "z", 0, 0, tiled=True)
-            ps, ms, lses = score(cent, embs)
-        lses = lax.all_to_all(lses, ("x", "y"), 0, 0, tiled=True)
-        sums, row_lse = sums_of(lses, swap(lses), ps, ms, embs)
-        got = lax.all_to_all(sums, "z", 0, 0, tiled=True)
+            cent = exchange(out, ("z",), Z)
+            ps, ms, lse = score(cent, embs)
+        lses = exchange(combine(lse, swap(lse)), ("x", "y"), X * Y)
+        sums, row_lse = sums_of(lses, ps, ms, embs)
+        got = exchange(sums, ("z",), Z)
         current, out = update(got, current, step == ITERS - 1)
     return current, out.reshape(OWN), row_lse.reshape(COL)
 

time: 140 us -> 129 us (0.921); the launches traced: 138 us -> 129 us
  blocking collectives: 104 us -> 96.5 us
  waiting for transfers between devices: 14.3 us -> 12.8 us
    all_to_all x6, blocking collectives: 104 us -> 96.5 us  [exchange(): lax.all_to_all(v, (*axes, 'c'), 0, 0, axis_index_groups=groups, tiled=True)]
    ppermute x10, waiting for transfers between devices: 14.3 us -> 12.8 us  [shift(): return lax.ppermute(v, axis, [(i, (i + k) % size) for i in range(size)])]
where the time goes in v4:
time: 129 us
  blocking collectives  96.5 us (75%)
  Pallas kernels  13.2 us (10%)
  waiting for transfers between devices  12.8 us (10%)
  starting transfers between devices  5.96 us (5%)
    all_to_all x6, blocking collectives, exchange(): lax.all_to_all(v, (*axes, 'c'), 0, 0, axis_index_groups=groups, tiled=True)  96.5 us
    ppermute x10, waiting for transfers between devices, shift(): return lax.ppermute(v, axis, [(i, (i + k) % size) for i in range(size)])  12.8 us
    ppermute x10, starting transfers between devices, shift(): return lax.ppermute(v, axis, [(i, (i + k) % size) for i in range(size)])  5.96 us
    pallas_call x2, Pallas kernels, sums_of(): pl.pallas_call(sum_kernel, out_shape=(shape(Z * PACK, 128, dtype=BF16), s...  5.02 us
    pallas_call x3, Pallas kernels, arrive(): pl.pallas_call(functools.partial(arrive_kernel, part, len(earlier)), out_...  3.23 us
  transfers between devices with their start and end apart: 10, of which 7 were waited for; matrix products, arithmetic and copies ran while one was open for 0% of the time, Pallas kernels for 2%

profile of v4, /device:TPU:2, one launch (start us, length us, event | category | flops | bytes accessed | tf_op | source)
XLA Modules:
  0.0 129.2 jit_solution(2808872747291767067)
XLA Ops:
  0.6 1.5 %prepare.1 = (bf16[512,768]{1,0:T(8,128)(2,1)S(1)}, bf16[256,768]{1,0:T(8,128)(2,1)S(1)}) custom-call(bf16[1024,768]{1,0:T(8,128)(2,1)} %refs_0_.1, f32[32,768]{1,0:T(8,128)} %cur_ref.1), custom_call_target="tpu_custom_call" | custom-call | tf_op jit(solution)/shard_map/prepare/pallas_call | solution.py:72
  2.1 1.6 %collective-permute-start = (bf16[512,768]{1,0:T(8,128)(2,1)S(1)}, bf16[512,768]{1,0:T(8,128)(2,1)S(1)}, u32[]{:S(2)}, u32[]{:S(2)}) collective-permute-start(bf16[512,768]{1,0:T(8,128)(2,1)S(1)} %get-tuple-element.40), channel_id=1, source_target_pairs={{0,8},{8,16},{16,24},{24,0},{1,9},{9,17},{17,25},{25,1},{2,10},{10... | collective-permute-start | bytes 2359304 | tf_op jit(solution)/shard_map/ppermute | solution.py:294
  3.7 0.9 collective-permute-start.1
  4.5 19.9 %all_to_all.66 = bf16[8,32,768]{2,1,0:T(8,128)(2,1)S(1)} all-to-all(bf16[8,32,768]{2,1,0:T(8,128)(2,1)S(1)} %bitcast.26), channel_id=1, replica_groups={{0,32,64,96,128,160,192,224},{225,193,161,129,97,65,33,1},{2,34,66,98,1..., dimensions={0} | all-to-all | bytes 786432 | tf_op jit(solution)/shard_map/all_to_all | solution.py:304
  24.4 0.8 arrive.3
  25.3 0.1 collective-permute-start.4
  25.4 0.5 collective-permute-start.5
  25.9 0.1 relay.1
  25.9 1.6 %collective-permute-start.2 = (bf16[256,768]{1,0:T(8,128)(2,1)S(1)}, bf16[256,768]{1,0:T(8,128)(2,1)S(1)}, u32[]{:S(2)}, u32[]{:S(2)}) collective-permute-start(bf16[256,768]{1,0:T(8,128)(2,1)S(1)} %get-tuple-element.44), channel_id=1, source_target_pairs={{0,8},{8,16},{16,24},{24,0},{1,9},{9,17},{17,25},{25,1},{2,10},{10... | collective-permute-start | bytes 1179656 | tf_op jit(solution)/shard_map/ppermute | solution.py:294
  27.5 0.5 collective-permute-start.3
  28.0 0.7 collective-permute-done.5.refs_3_
  28.8 1.5 %arrive.4 = (bf16[2048,768]{1,0:T(8,128)(2,1)S(1)}, bf16[256,2048]{1,0:T(8,128)(2,1)S(1)}, f32[16,128]{1,0:T(8,128)S(1)}, f32[16,128]{1,0:T(8,128)S(1)}) custom-call(bf16[256,768]{1,0:T(8,128)(2,1)S(1)} %bitcast.15, bf16[512,768]{1,0:T(8,128)(2,1)S(1)} %collective-permute-done.left_ref.refs_0_, bf16[512,768]{1,0:T(8,128)(2,1)S(1)} %collective-permute-done.4.refs_1_, ...), custom_call_target="tpu_custom_call" | custom-call | tf_op jit(solution)/shard_map/arrive/pallas_call | solution.py:151
  30.3 6.8 %collective-permute-done.2.refs_0_ = bf16[256,768]{1,0:T(8,128)(2,1)S(1)} collective-permute-done((bf16[256,768]{1,0:T(8,128)(2,1)S(1)}, bf16[256,768]{1,0:T(8,128)(2,1)S(1)}, u32[]{:S(2)}, u32[]{:S(2)}) %collective-permute-start.2) | collective-permute-done | bytes 393248 | tf_op jit(solution)/shard_map/ppermute | solution.py:294
  37.1 1.2 collective-permute-done.3.refs_1_
  38.3 0.5 collective-permute-start.7
  38.8 1.2 collective-permute-done.6.refs_2_
  40.1 0.6 collective-permute-done.7.refs_3_
  40.6 0.9 arrive.5
  41.5 0.2 collective-permute-start.8
  41.7 1.0 collective-permute-done.8.b_ref
  42.8 15.2 %all_to_all.67 = f32[16,32,128]{2,1,0:T(8,128)S(1)} all-to-all(f32[16,32,128]{2,1,0:T(8,128)S(1)} %bitcast.22), channel_id=1, replica_groups={{0,2,4,6,8,10,12,14,16,18,20,22,24,26,28,30},{31,29,27,25,23,21,19,17,1..., dimensions={0} | all-to-all | bytes 524288 | tf_op jit(solution)/shard_map/all_to_all | solution.py:304
  58.1 2.5 %sums.2 = (bf16[1664,128]{1,0:T(8,128)(2,1)S(1)}, f32[8,128]{1,0:T(8,128)}) custom-call(f32[512,128]{1,0:T(8,128)S(1)} %bitcast.21, bf16[256,1024]{1,0:T(8,128)(2,1)S(1)} %get-tuple-element.52.refs_0_, bf16[256,2048]{1,0:T(8,128)(2,1)S(1)} %get-tuple-element.53.refs_1_, bf16[256,1024]{1,0:T(8,128)(2,1)S(1)} %get-tuple-element.54.refs_2_, ...), custom_call_target="tpu_custom_call" | custom-call | tf_op jit(solution)/shard_map/sums/pallas_call | solution.py:251
  60.6 16.8 %all_to_all.68 = bf16[8,208,128]{2,1,0:T(8,128)(2,1)S(1)} all-to-all(bf16[8,208,128]{2,1,0:T(8,128)(2,1)S(1)} %bitcast.25), channel_id=1, replica_groups={{0,32,64,96,128,160,192,224},{225,193,161,129,97,65,33,1},{2,34,66,98,1..., dimensions={0} | all-to-all | bytes 851968 | tf_op jit(solution)/shard_map/all_to_all | solution.py:304
  77.4 0.2 update.2
  77.6 14.8 %all_to_all.69 = bf16[8,32,768]{2,1,0:T(8,128)(2,1)S(1)} all-to-all(bf16[8,32,768]{2,1,0:T(8,128)(2,1)S(1)} %bitcast.27), channel_id=1, replica_groups={{0,32,64,96,128,160,192,224},{225,193,161,129,97,65,33,1},{2,34,66,98,1..., dimensions={0} | all-to-all | bytes 786432 | tf_op jit(solution)/shard_map/all_to_all | solution.py:304
  92.5 2.2 %score.1 = (bf16[256,1024]{1,0:T(8,128)(2,1)S(1)}, bf16[256,2048]{1,0:T(8,128)(2,1)S(1)}, bf16[256,1024]{1,0:T(8,128)(2,1)S(1)}, f32[8,128]{1,0:T(8,128)S(1)}, f...) custom-call(bf16[256,768]{1,0:T(8,128)(2,1)S(1)} %bitcast.19, ...), custom_call_target="tpu_custom_call" | custom-call | tf_op jit(solution)/shard_map/score/pallas_call | solution.py:177
  94.7 0.1 collective-permute-start.9
  94.8 1.2 collective-permute-done.9.b_ref
  96.0 13.4 %all_to_all.70 = f32[16,32,128]{2,1,0:T(8,128)S(1)} all-to-all(f32[16,32,128]{2,1,0:T(8,128)S(1)} %bitcast.23), channel_id=1, replica_groups={{0,2,4,6,8,10,12,14,16,18,20,22,24,26,28,30},{31,29,27,25,23,21,19,17,1..., dimensions={0} | all-to-all | bytes 524288 | tf_op jit(solution)/shard_map/all_to_all | solution.py:304
  109.4 2.5 %sums.3 = (bf16[1664,128]{1,0:T(8,128)(2,1)S(1)}, f32[8,128]{1,0:T(8,128)}) custom-call(f32[512,128]{1,0:T(8,128)S(1)} %bitcast.20, bf16[256,1024]{1,0:T(8,128)(2,1)S(1)} %get-tuple-element.64.refs_0_, bf16[256,2048]{1,0:T(8,128)(2,1)S(1)} %get-tuple-element.65.refs_1_, bf16[256,1024]{1,0:T(8,128)(2,1)S(1)} %get-tuple-element.66.refs_2_, ...), custom_call_target="tpu_custom_call" | custom-call | tf_op jit(solution)/shard_map/sums/pallas_call | solution.py:251
  111.9 16.4 %all_to_all.71 = bf16[8,208,128]{2,1,0:T(8,128)(2,1)S(1)} all-to-all(bf16[8,208,128]{2,1,0:T(8,128)(2,1)S(1)} %bitcast.24), channel_id=1, replica_groups={{0,32,64,96,128,160,192,224},{225,193,161,129,97,65,33,1},{2,34,66,98,1..., dimensions={0} | all-to-all | bytes 851968 | tf_op jit(solution)/shard_map/all_to_all | solution.py:304
  128.3 0.9 update.3
  (10 shorter events, 0.1 us)
Async XLA Ops:
  0.6 23.8 %copy-start = (bf16[1024,768]{1,0:T(8,128)(2,1)S(1)}, bf16[1024,768]{1,0:T(8,128)(2,1)}, u32[]{:S(2)}) copy-start(bf16[1024,768]{1,0:T(8,128)(2,1)} %refs_0_.1) | copy-start | bytes 4718596
  2.1 23.2 %collective-permute-start = (bf16[512,768]{1,0:T(8,128)(2,1)S(1)}, bf16[512,768]{1,0:T(8,128)(2,1)S(1)}, u32[]{:S(2)}, u32[]{:S(2)}) collective-permute-start(bf16[512,768]{1,0:T(8,128)(2,1)S(1)} %get-tuple-element.40), channel_id=1, source_target_pairs={{0,8},{8,16},{16,24},{24,0},{1,9},{9,17},{17,25},{25,1},{2,10},{10... | collective-permute-start | bytes 2359304 | tf_op jit(solution)/shard_map/ppermute | solution.py:294
  3.7 21.6 %collective-permute-start.1 = (bf16[512,768]{1,0:T(8,128)(2,1)S(1)}, bf16[512,768]{1,0:T(8,128)(2,1)S(1)}, u32[]{:S(2)}, u32[]{:S(2)}) collective-permute-start(bf16[512,768]{1,0:T(8,128)(2,1)S(1)} %get-tuple-element.40), channel_id=1, source_target_pairs={{0,24},{8,0},{16,8},{24,16},{1,25},{9,1},{17,9},{25,17},{2,26},{10... | collective-permute-start | bytes 2359304 | tf_op jit(solution)/shard_map/ppermute | solution.py:294
  25.3 2.8 %collective-permute-start.4 = (bf16[512,768]{1,0:T(8,128)(2,1)S(1)}, bf16[512,768]{1,0:T(8,128)(2,1)S(1)}, u32[]{:S(2)}, u32[]{:S(2)}) collective-permute-start(bf16[512,768]{1,0:T(8,128)(2,1)S(1)} %collective-permute-done.left_ref.refs_0_), channel_id=1, source_target_pairs={{0,1},{1,0},{2,3},{3,2},{4,5},{5,4},{6,7},{7,6},{8,9},{9,8},{10,11... | collective-permute-start | bytes 2359304 | tf_op jit(solution)/shard_map/ppermute | solution.py:294
  25.4 3.4 %collective-permute-start.5 = (bf16[512,768]{1,0:T(8,128)(2,1)S(1)}, bf16[512,768]{1,0:T(8,128)(2,1)S(1)}, u32[]{:S(2)}, u32[]{:S(2)}) collective-permute-start(bf16[512,768]{1,0:T(8,128)(2,1)S(1)} %collective-permute-done.1.right_ref.refs_2_), channel_id=1, source_target_pairs={{0,1},{1,0},{2,3},{3,2},{4,5},{5,4},{6,7},{7,6},{8,9},{9,8},{10,11... | collective-permute-start | bytes 2359304 | tf_op jit(solution)/shard_map/ppermute | solution.py:294
  25.9 11.2 %collective-permute-start.2 = (bf16[256,768]{1,0:T(8,128)(2,1)S(1)}, bf16[256,768]{1,0:T(8,128)(2,1)S(1)}, u32[]{:S(2)}, u32[]{:S(2)}) collective-permute-start(bf16[256,768]{1,0:T(8,128)(2,1)S(1)} %get-tuple-element.44), channel_id=1, source_target_pairs={{0,8},{8,16},{16,24},{24,0},{1,9},{9,17},{17,25},{25,1},{2,10},{10... | collective-permute-start | bytes 1179656 | tf_op jit(solution)/shard_map/ppermute | solution.py:294
  27.5 10.8 %collective-permute-start.3 = (bf16[256,768]{1,0:T(8,128)(2,1)S(1)}, bf16[256,768]{1,0:T(8,128)(2,1)S(1)}, u32[]{:S(2)}, u32[]{:S(2)}) collective-permute-start(bf16[256,768]{1,0:T(8,128)(2,1)S(1)} %get-tuple-element.45), channel_id=1, source_target_pairs={{0,24},{8,0},{16,8},{24,16},{1,25},{9,1},{17,9},{25,17},{2,26},{10... | collective-permute-start | bytes 1179656 | tf_op jit(solution)/shard_map/ppermute | solution.py:294
  38.3 1.7 %collective-permute-start.6 = (bf16[256,768]{1,0:T(8,128)(2,1)S(1)}, bf16[256,768]{1,0:T(8,128)(2,1)S(1)}, u32[]{:S(2)}, u32[]{:S(2)}) collective-permute-start(bf16[256,768]{1,0:T(8,128)(2,1)S(1)} %collective-permute-done.2.refs_0_), channel_id=1, source_target_pairs={{0,1},{1,0},{2,3},{3,2},{4,5},{5,4},{6,7},{7,6},{8,9},{9,8},{10,11... | collective-permute-start | bytes 1179656 | tf_op jit(solution)/shard_map/ppermute | solution.py:294
  38.3 2.3 %collective-permute-start.7 = (bf16[256,768]{1,0:T(8,128)(2,1)S(1)}, bf16[256,768]{1,0:T(8,128)(2,1)S(1)}, u32[]{:S(2)}, u32[]{:S(2)}) collective-permute-start(bf16[256,768]{1,0:T(8,128)(2,1)S(1)} %collective-permute-done.3.refs_1_), channel_id=1, source_target_pairs={{0,1},{1,0},{2,3},{3,2},{4,5},{5,4},{6,7},{7,6},{8,9},{9,8},{10,11... | collective-permute-start | bytes 1179656 | tf_op jit(solution)/shard_map/ppermute | solution.py:294
  41.5 1.3 collective-permute-start.8
  58.0 19.3 %copy-start.1 = (f32[32,768]{1,0:T(8,128)S(1)}, f32[32,768]{1,0:T(8,128)}, u32[]{:S(2)}) copy-start(f32[32,768]{1,0:T(8,128)} %cur_ref.1) | copy-start | bytes 294916
  94.7 1.3 collective-permute-start.9

commit v5 on v4

--- a/solution.py
+++ b/solution.py
@@ -21,6 +21,8 @@
 SCALE = 50.0 * math.log2(math.e)
 VMEM = pl.BlockSpec(memory_space=pltpu.VMEM)
 ANY = pl.BlockSpec(memory_space=pl.ANY)
+RING = ((0, 4, 2, 6, 1, 5, 3, 7), (7, 3, 5, 1, 6, 2, 4, 0))
+PLANE = (tuple(range(X * Y)), tuple(range(X * Y))[::-1])
 PARTS = ((0,), (1, 3), (2,))
 ROWS = tuple(COL * len(part) for part in PARTS)
 
@@ -298,16 +300,15 @@
     return shift(v, "c", C, 1)
 
 
-def exchange(v, axes, n):
-    second = list(range(n))[::-1]
-    groups = [[C * i for i in range(n)], [C * i + 1 for i in second]]
+def exchange(v, axes, orders):
+    groups = [[C * i + c for i in orders[c]] for c in range(C)]
     return lax.all_to_all(v, (*axes, "c"), 0, 0, axis_index_groups=groups, tiled=True)
 
 
 def on_device(embeddings, centroids):
     mine, copies = prepare(embeddings, centroids)
     left, right = shift(mine, "x", X, 1), shift(mine, "x", X, 3)
-    cent = exchange(copies, ("z",), Z)
+    cent = exchange(copies, ("z",), RING)
     own = arrive(cent, PARTS[0], (embeddings,))
     left, right, first = lax.optimization_barrier((left, right, own[3]))
     low, high = relay(left, right)
@@ -319,11 +320,11 @@
     current = centroids
     for step in range(ITERS):
         if step > 0:
-            cent = exchange(out, ("z",), Z)
+            cent = exchange(out, ("z",), RING)
             ps, ms, lse = score(cent, embs)
-        lses = exchange(combine(lse, swap(lse)), ("x", "y"), X * Y)
+        lses = exchange(combine(lse, swap(lse)), ("x", "y"), PLANE)
         sums, row_lse = sums_of(lses, ps, ms, embs)
-        got = exchange(sums, ("z",), Z)
+        got = exchange(sums, ("z",), RING)
         current, out = update(got, current, step == ITERS - 1)
     return current, out.reshape(OWN), row_lse.reshape(COL)
 

time: 129 us -> 128 us (level)
  blocking collectives: 96.5 us -> 94.7 us
    all_to_all x6, blocking collectives: 96.5 us -> 94.7 us  [exchange(): lax.all_to_all(v, (*axes, 'c'), 0, 0, axis_index_groups=groups, tiled=True)]
where the time goes in v5:
time: 128 us; the launch traced here: 127 us
  blocking collectives  94.7 us (74%)
  Pallas kernels  13.1 us (10%)
  waiting for transfers between devices  12.8 us (10%)
  starting transfers between devices  5.96 us (5%)
    all_to_all x6, blocking collectives, exchange(): lax.all_to_all(v, (*axes, 'c'), 0, 0, axis_index_groups=groups, tiled=True)  94.7 us
    ppermute x10, waiting for transfers between devices, shift(): return lax.ppermute(v, axis, [(i, (i + k) % size) for i in range(size)])  12.8 us
    ppermute x10, starting transfers between devices, shift(): return lax.ppermute(v, axis, [(i, (i + k) % size) for i in range(size)])  5.96 us
    pallas_call x2, Pallas kernels, sums_of(): pl.pallas_call(sum_kernel, out_shape=(shape(Z * PACK, 128, dtype=BF16), s...  5.02 us
    pallas_call x3, Pallas kernels, arrive(): pl.pallas_call(functools.partial(arrive_kernel, part, len(earlier)), out_...  3.21 us
  transfers between devices with their start and end apart: 10, of which 7 were waited for; matrix products, arithmetic and copies ran while one was open for 0% of the time, Pallas kernels for 2%

profile of v5, /device:TPU:2, one launch (start us, length us, event | category | flops | bytes accessed | tf_op | source)
XLA Modules:
  0.0 127.3 jit_solution(16033650301665274146)
XLA Ops:
  0.6 1.5 %prepare.1 = (bf16[512,768]{1,0:T(8,128)(2,1)S(1)}, bf16[256,768]{1,0:T(8,128)(2,1)S(1)}) custom-call(bf16[1024,768]{1,0:T(8,128)(2,1)} %refs_0_.1, f32[32,768]{1,0:T(8,128)} %cur_ref.1), custom_call_target="tpu_custom_call" | custom-call | tf_op jit(solution)/shard_map/prepare/pallas_call | solution.py:74
  2.1 1.6 %collective-permute-start = (bf16[512,768]{1,0:T(8,128)(2,1)S(1)}, bf16[512,768]{1,0:T(8,128)(2,1)S(1)}, u32[]{:S(2)}, u32[]{:S(2)}) collective-permute-start(bf16[512,768]{1,0:T(8,128)(2,1)S(1)} %get-tuple-element.40), channel_id=1, source_target_pairs={{0,8},{8,16},{16,24},{24,0},{1,9},{9,17},{17,25},{25,1},{2,10},{10... | collective-permute-start | bytes 2359304 | tf_op jit(solution)/shard_map/ppermute | solution.py:296
  3.7 0.9 collective-permute-start.1
  4.5 18.8 %all_to_all.66 = bf16[8,32,768]{2,1,0:T(8,128)(2,1)S(1)} all-to-all(bf16[8,32,768]{2,1,0:T(8,128)(2,1)S(1)} %bitcast.26), channel_id=1, replica_groups={{0,128,64,192,32,160,96,224},{225,97,161,33,193,65,129,1},{2,130,66,194..., dimensions={0} | all-to-all | bytes 786432 | tf_op jit(solution)/shard_map/all_to_all | solution.py:305
  23.4 0.8 arrive.3
  24.2 0.1 collective-permute-start.4
  24.3 0.5 collective-permute-start.5
  24.8 0.1 relay.1
  24.9 1.6 %collective-permute-start.2 = (bf16[256,768]{1,0:T(8,128)(2,1)S(1)}, bf16[256,768]{1,0:T(8,128)(2,1)S(1)}, u32[]{:S(2)}, u32[]{:S(2)}) collective-permute-start(bf16[256,768]{1,0:T(8,128)(2,1)S(1)} %get-tuple-element.44), channel_id=1, source_target_pairs={{0,8},{8,16},{16,24},{24,0},{1,9},{9,17},{17,25},{25,1},{2,10},{10... | collective-permute-start | bytes 1179656 | tf_op jit(solution)/shard_map/ppermute | solution.py:296
  26.4 0.5 collective-permute-start.3
  27.0 0.7 collective-permute-done.5.refs_3_
  27.7 1.5 %arrive.4 = (bf16[2048,768]{1,0:T(8,128)(2,1)S(1)}, bf16[256,2048]{1,0:T(8,128)(2,1)S(1)}, f32[16,128]{1,0:T(8,128)S(1)}, f32[16,128]{1,0:T(8,128)S(1)}) custom-call(bf16[256,768]{1,0:T(8,128)(2,1)S(1)} %bitcast.15, bf16[512,768]{1,0:T(8,128)(2,1)S(1)} %collective-permute-done.left_ref.refs_0_, bf16[512,768]{1,0:T(8,128)(2,1)S(1)} %collective-permute-done.4.refs_1_, ...), custom_call_target="tpu_custom_call" | custom-call | tf_op jit(solution)/shard_map/arrive/pallas_call | solution.py:153
  29.2 6.9 %collective-permute-done.2.refs_0_ = bf16[256,768]{1,0:T(8,128)(2,1)S(1)} collective-permute-done((bf16[256,768]{1,0:T(8,128)(2,1)S(1)}, bf16[256,768]{1,0:T(8,128)(2,1)S(1)}, u32[]{:S(2)}, u32[]{:S(2)}) %collective-permute-start.2) | collective-permute-done | bytes 393248 | tf_op jit(solution)/shard_map/ppermute | solution.py:296
  36.1 1.2 collective-permute-done.3.refs_1_
  37.3 0.5 collective-permute-start.7
  37.8 1.2 collective-permute-done.6.refs_2_
  39.0 0.6 collective-permute-done.7.refs_3_
  39.6 0.9 arrive.5
  40.5 0.2 collective-permute-start.8
  40.7 1.0 collective-permute-done.8.b_ref
  41.8 15.2 %all_to_all.67 = f32[16,32,128]{2,1,0:T(8,128)S(1)} all-to-all(f32[16,32,128]{2,1,0:T(8,128)S(1)} %bitcast.22), channel_id=1, replica_groups={{0,2,4,6,8,10,12,14,16,18,20,22,24,26,28,30},{31,29,27,25,23,21,19,17,1..., dimensions={0} | all-to-all | bytes 524288 | tf_op jit(solution)/shard_map/all_to_all | solution.py:305
  57.0 2.5 %sums.2 = (bf16[1664,128]{1,0:T(8,128)(2,1)S(1)}, f32[8,128]{1,0:T(8,128)}) custom-call(f32[512,128]{1,0:T(8,128)S(1)} %bitcast.21, bf16[256,1024]{1,0:T(8,128)(2,1)S(1)} %get-tuple-element.52.refs_0_, bf16[256,2048]{1,0:T(8,128)(2,1)S(1)} %get-tuple-element.53.refs_1_, bf16[256,1024]{1,0:T(8,128)(2,1)S(1)} %get-tuple-element.54.refs_2_, ...), custom_call_target="tpu_custom_call" | custom-call | tf_op jit(solution)/shard_map/sums/pallas_call | solution.py:253
  59.5 16.3 %all_to_all.68 = bf16[8,208,128]{2,1,0:T(8,128)(2,1)S(1)} all-to-all(bf16[8,208,128]{2,1,0:T(8,128)(2,1)S(1)} %bitcast.25), channel_id=1, replica_groups={{0,128,64,192,32,160,96,224},{225,97,161,33,193,65,129,1},{2,130,66,194..., dimensions={0} | all-to-all | bytes 851968 | tf_op jit(solution)/shard_map/all_to_all | solution.py:305
  75.8 0.2 update.2
  76.0 15.2 %all_to_all.69 = bf16[8,32,768]{2,1,0:T(8,128)(2,1)S(1)} all-to-all(bf16[8,32,768]{2,1,0:T(8,128)(2,1)S(1)} %bitcast.27), channel_id=1, replica_groups={{0,128,64,192,32,160,96,224},{225,97,161,33,193,65,129,1},{2,130,66,194..., dimensions={0} | all-to-all | bytes 786432 | tf_op jit(solution)/shard_map/all_to_all | solution.py:305
  91.2 2.2 %score.1 = (bf16[256,1024]{1,0:T(8,128)(2,1)S(1)}, bf16[256,2048]{1,0:T(8,128)(2,1)S(1)}, bf16[256,1024]{1,0:T(8,128)(2,1)S(1)}, f32[8,128]{1,0:T(8,128)S(1)}, f...) custom-call(bf16[256,768]{1,0:T(8,128)(2,1)S(1)} %bitcast.19, ...), custom_call_target="tpu_custom_call" | custom-call | tf_op jit(solution)/shard_map/score/pallas_call | solution.py:179
  93.4 0.1 collective-permute-start.9
  93.5 1.2 collective-permute-done.9.b_ref
  94.8 13.5 %all_to_all.70 = f32[16,32,128]{2,1,0:T(8,128)S(1)} all-to-all(f32[16,32,128]{2,1,0:T(8,128)S(1)} %bitcast.23), channel_id=1, replica_groups={{0,2,4,6,8,10,12,14,16,18,20,22,24,26,28,30},{31,29,27,25,23,21,19,17,1..., dimensions={0} | all-to-all | bytes 524288 | tf_op jit(solution)/shard_map/all_to_all | solution.py:305
  108.3 2.5 %sums.3 = (bf16[1664,128]{1,0:T(8,128)(2,1)S(1)}, f32[8,128]{1,0:T(8,128)}) custom-call(f32[512,128]{1,0:T(8,128)S(1)} %bitcast.20, bf16[256,1024]{1,0:T(8,128)(2,1)S(1)} %get-tuple-element.64.refs_0_, bf16[256,2048]{1,0:T(8,128)(2,1)S(1)} %get-tuple-element.65.refs_1_, bf16[256,1024]{1,0:T(8,128)(2,1)S(1)} %get-tuple-element.66.refs_2_, ...), custom_call_target="tpu_custom_call" | custom-call | tf_op jit(solution)/shard_map/sums/pallas_call | solution.py:253
  110.8 15.7 %all_to_all.71 = bf16[8,208,128]{2,1,0:T(8,128)(2,1)S(1)} all-to-all(bf16[8,208,128]{2,1,0:T(8,128)(2,1)S(1)} %bitcast.24), channel_id=1, replica_groups={{0,128,64,192,32,160,96,224},{225,97,161,33,193,65,129,1},{2,130,66,194..., dimensions={0} | all-to-all | bytes 851968 | tf_op jit(solution)/shard_map/all_to_all | solution.py:305
  126.5 0.9 update.3
  (10 shorter events, 0.1 us)
Async XLA Ops:
  0.6 22.7 %copy-start = (bf16[1024,768]{1,0:T(8,128)(2,1)S(1)}, bf16[1024,768]{1,0:T(8,128)(2,1)}, u32[]{:S(2)}) copy-start(bf16[1024,768]{1,0:T(8,128)(2,1)} %refs_0_.1) | copy-start | bytes 4718596
  2.1 22.1 %collective-permute-start = (bf16[512,768]{1,0:T(8,128)(2,1)S(1)}, bf16[512,768]{1,0:T(8,128)(2,1)S(1)}, u32[]{:S(2)}, u32[]{:S(2)}) collective-permute-start(bf16[512,768]{1,0:T(8,128)(2,1)S(1)} %get-tuple-element.40), channel_id=1, source_target_pairs={{0,8},{8,16},{16,24},{24,0},{1,9},{9,17},{17,25},{25,1},{2,10},{10... | collective-permute-start | bytes 2359304 | tf_op jit(solution)/shard_map/ppermute | solution.py:296
  3.7 20.5 %collective-permute-start.1 = (bf16[512,768]{1,0:T(8,128)(2,1)S(1)}, bf16[512,768]{1,0:T(8,128)(2,1)S(1)}, u32[]{:S(2)}, u32[]{:S(2)}) collective-permute-start(bf16[512,768]{1,0:T(8,128)(2,1)S(1)} %get-tuple-element.40), channel_id=1, source_target_pairs={{0,24},{8,0},{16,8},{24,16},{1,25},{9,1},{17,9},{25,17},{2,26},{10... | collective-permute-start | bytes 2359304 | tf_op jit(solution)/shard_map/ppermute | solution.py:296
  24.2 2.8 %collective-permute-start.4 = (bf16[512,768]{1,0:T(8,128)(2,1)S(1)}, bf16[512,768]{1,0:T(8,128)(2,1)S(1)}, u32[]{:S(2)}, u32[]{:S(2)}) collective-permute-start(bf16[512,768]{1,0:T(8,128)(2,1)S(1)} %collective-permute-done.left_ref.refs_0_), channel_id=1, source_target_pairs={{0,1},{1,0},{2,3},{3,2},{4,5},{5,4},{6,7},{7,6},{8,9},{9,8},{10,11... | collective-permute-start | bytes 2359304 | tf_op jit(solution)/shard_map/ppermute | solution.py:296
  24.3 3.4 %collective-permute-start.5 = (bf16[512,768]{1,0:T(8,128)(2,1)S(1)}, bf16[512,768]{1,0:T(8,128)(2,1)S(1)}, u32[]{:S(2)}, u32[]{:S(2)}) collective-permute-start(bf16[512,768]{1,0:T(8,128)(2,1)S(1)} %collective-permute-done.1.right_ref.refs_2_), channel_id=1, source_target_pairs={{0,1},{1,0},{2,3},{3,2},{4,5},{5,4},{6,7},{7,6},{8,9},{9,8},{10,11... | collective-permute-start | bytes 2359304 | tf_op jit(solution)/shard_map/ppermute | solution.py:296
  24.9 11.2 %collective-permute-start.2 = (bf16[256,768]{1,0:T(8,128)(2,1)S(1)}, bf16[256,768]{1,0:T(8,128)(2,1)S(1)}, u32[]{:S(2)}, u32[]{:S(2)}) collective-permute-start(bf16[256,768]{1,0:T(8,128)(2,1)S(1)} %get-tuple-element.44), channel_id=1, source_target_pairs={{0,8},{8,16},{16,24},{24,0},{1,9},{9,17},{17,25},{25,1},{2,10},{10... | collective-permute-start | bytes 1179656 | tf_op jit(solution)/shard_map/ppermute | solution.py:296
  26.4 10.8 %collective-permute-start.3 = (bf16[256,768]{1,0:T(8,128)(2,1)S(1)}, bf16[256,768]{1,0:T(8,128)(2,1)S(1)}, u32[]{:S(2)}, u32[]{:S(2)}) collective-permute-start(bf16[256,768]{1,0:T(8,128)(2,1)S(1)} %get-tuple-element.45), channel_id=1, source_target_pairs={{0,24},{8,0},{16,8},{24,16},{1,25},{9,1},{17,9},{25,17},{2,26},{10... | collective-permute-start | bytes 1179656 | tf_op jit(solution)/shard_map/ppermute | solution.py:296
  37.3 1.7 %collective-permute-start.6 = (bf16[256,768]{1,0:T(8,128)(2,1)S(1)}, bf16[256,768]{1,0:T(8,128)(2,1)S(1)}, u32[]{:S(2)}, u32[]{:S(2)}) collective-permute-start(bf16[256,768]{1,0:T(8,128)(2,1)S(1)} %collective-permute-done.2.refs_0_), channel_id=1, source_target_pairs={{0,1},{1,0},{2,3},{3,2},{4,5},{5,4},{6,7},{7,6},{8,9},{9,8},{10,11... | collective-permute-start | bytes 1179656 | tf_op jit(solution)/shard_map/ppermute | solution.py:296
  37.3 2.3 %collective-permute-start.7 = (bf16[256,768]{1,0:T(8,128)(2,1)S(1)}, bf16[256,768]{1,0:T(8,128)(2,1)S(1)}, u32[]{:S(2)}, u32[]{:S(2)}) collective-permute-start(bf16[256,768]{1,0:T(8,128)(2,1)S(1)} %collective-permute-done.3.refs_1_), channel_id=1, source_target_pairs={{0,1},{1,0},{2,3},{3,2},{4,5},{5,4},{6,7},{7,6},{8,9},{9,8},{10,11... | collective-permute-start | bytes 1179656 | tf_op jit(solution)/shard_map/ppermute | solution.py:296
  40.5 1.3 collective-permute-start.8
  57.0 18.8 %copy-start.1 = (f32[32,768]{1,0:T(8,128)S(1)}, f32[32,768]{1,0:T(8,128)}, u32[]{:S(2)}) copy-start(f32[32,768]{1,0:T(8,128)} %cur_ref.1) | copy-start | bytes 294916
  93.4 1.3 collective-permute-start.9

commit v6 on v5

--- a/solution.py
+++ b/solution.py
@@ -15,7 +15,8 @@
 OWN = 32
 K = Z * OWN
 COL = 1024
-HALF, QUARTER = COL // 2, COL // 4
+HALF = COL // 2
+QUARTER = HALF // Y
 PACK = OWN * D // 128 + 16
 F32, BF16 = jnp.float32, jnp.bfloat16
 SCALE = 50.0 * math.log2(math.e)
@@ -49,6 +50,29 @@
 
 def column_of(k):
     return pl.ds(pl.multiple_of(8 * lax.rem(lax.axis_index("x") + (X - k), X), 8), 8)
+
+
+def quarter_kernel(emb_ref, quarter_ref, sems):
+    at = lax.axis_index("c") * HALF + lax.axis_index("y") * QUARTER
+    waits = []
+    for i in range(0, QUARTER, 32):
+        rows = pl.ds(pl.multiple_of(at + i, 32), 32)
+        waits.append(pltpu.make_async_copy(emb_ref.at[rows], quarter_ref.at[pl.ds(i, 32)], sems.at[i // 32]))
+        waits[-1].start()
+    for wait in waits:
+        wait.wait()
+
+
+def quarter_of(emb):
+    return pl.pallas_call(
+        quarter_kernel,
+        out_shape=pltpu.VMEM((QUARTER, D), BF16),
+        in_specs=[ANY],
+        out_specs=VMEM,
+        scratch_shapes=[pltpu.SemaphoreType.DMA((QUARTER // 32,))],
+        compiler_params=limit(4),
+        name="quarter",
+    )(in_hbm(emb))
 
 
 def prepare_kernel(emb_ref, cent_ref, mine_ref, copies_ref, cent, sems, cent_sem):
@@ -86,20 +110,22 @@
     )(in_hbm(emb), in_hbm(cent))
 
 
-def relay_kernel(left_ref, right_ref, low_ref, high_ref):
-    low_ref[...] = left_ref[pl.ds(0, QUARTER), :]
-    high_ref[...] = right_ref[pl.ds(QUARTER, QUARTER), :]
-
-
-def relay(left, right):
-    return pl.pallas_call(
-        relay_kernel,
-        out_shape=(pltpu.VMEM((QUARTER, D), BF16),) * 2,
-        in_specs=[VMEM] * 2,
-        out_specs=(VMEM,) * 2,
+def join_kernel(*refs):
+    y = lax.axis_index("y")
+    for i, ref in enumerate(refs[:-1]):
+        at = pl.multiple_of(QUARTER * lax.rem(y + (Y - i), Y), QUARTER)
+        refs[-1][pl.ds(at, QUARTER), :] = ref[...]
+
+
+def join(quarters):
+    return pl.pallas_call(
+        join_kernel,
+        out_shape=pltpu.VMEM((HALF, D), BF16),
+        in_specs=[VMEM] * Y,
+        out_specs=VMEM,
         compiler_params=limit(4),
-        name="relay",
-    )(left, right)
+        name="join",
+    )(*quarters)
 
 
 def score_rows(cent, half_squares, emb, p_ref, m_ref):
@@ -306,16 +332,17 @@
 
 
 def on_device(embeddings, centroids):
+    far = shift(quarter_of(embeddings), "x", X, 2)
     mine, copies = prepare(embeddings, centroids)
     left, right = shift(mine, "x", X, 1), shift(mine, "x", X, 3)
+    quarters = [shift(far, "y", Y, k) for k in range(1, Y)]
+    copies, far = lax.optimization_barrier((copies, far))
     cent = exchange(copies, ("z",), RING)
     own = arrive(cent, PARTS[0], (embeddings,))
-    left, right, first = lax.optimization_barrier((left, right, own[3]))
-    low, high = relay(left, right)
-    far_low, far_high = shift(low, "x", X, 1), shift(high, "x", X, 3)
+    left, right, quarters, first = lax.optimization_barrier((left, right, quarters, own[3]))
+    far = join((far, *quarters))
     near = arrive(cent, PARTS[1], (left, swap(left), right, swap(right)))
-    far_low, far_high, second = lax.optimization_barrier((far_low, far_high, near[3]))
-    far = arrive(cent, PARTS[2], (far_low, far_high, swap(far_low), swap(far_high)), (first, second))
+    far = arrive(cent, PARTS[2], (far, swap(far)), (first, near[3]))
     embs, ps, ms, (_, _, lse) = zip(own, near, far)
     current = centroids
     for step in range(ITERS):

time: 128 us -> 125 us (0.977)
  blocking collectives: 94.7 us -> 76.2 us
  starting transfers between devices: 5.96 us -> 19.6 us
  Pallas kernels: 13.1 us -> 15.6 us
  waiting for transfers between devices: 12.8 us -> 11.3 us
  local copies, waits for them, and re-layouts: 0.01 us -> 1.46 us
    all_to_all x6 -> x5, blocking collectives: 94.7 us -> 76.2 us  [exchange(): lax.all_to_all(v, (*axes, 'c'), 0, 0, axis_index_groups=groups, tiled=True)]
    all_to_all x0 -> x1, starting transfers between devices: none -> 8.47 us  [exchange(): lax.all_to_all(v, (*axes, 'c'), 0, 0, axis_index_groups=groups, tiled=True)]
    ppermute x10 -> x11, waiting for transfers between devices: 12.8 us -> 6.94 us  [shift(): return lax.ppermute(v, axis, [(i, (i + k) % size) for i in range(size)])]
    ppermute x10 -> x11, starting transfers between devices: 5.96 us -> 11.2 us  [shift(): return lax.ppermute(v, axis, [(i, (i + k) % size) for i in range(size)])]
    all_to_all x0 -> x1, waiting for transfers between devices: none -> 4.4 us  [exchange(): lax.all_to_all(v, (*axes, 'c'), 0, 0, axis_index_groups=groups, tiled=True)]
    pallas_call x1 -> x2, Pallas kernels: 0.05 us -> 2.1 us  [the longest x1 1.18 us: join(): pl.pallas_call(join_kernel, out_shape=pltpu.VMEM((HALF, D), BF16), in_spe...]
    unnamed x4 -> x10, local copies, waits for them, and re-layouts: 0.01 us -> 1.46 us
  transfers between devices with their start and end apart: 10 -> 12, of which waited for: 7 -> 7; matrix products, arithmetic and copies ran while one was open for 0% -> 0% of each run, Pallas kernels for 2% -> 5%
where the time goes in v6:
time: 125 us
  blocking collectives  76.2 us (61%)
  starting transfers between devices  19.6 us (16%)
  Pallas kernels  15.6 us (12%)
  waiting for transfers between devices  11.3 us (9%)
  local copies, waits for them, and re-layouts  1.46 us (1%)
    all_to_all x5, blocking collectives, exchange(): lax.all_to_all(v, (*axes, 'c'), 0, 0, axis_index_groups=groups, tiled=True)  76.2 us
    ppermute x11, starting transfers between devices, shift(): return lax.ppermute(v, axis, [(i, (i + k) % size) for i in range(size)])  11.2 us
    all_to_all x1, starting transfers between devices, exchange(): lax.all_to_all(v, (*axes, 'c'), 0, 0, axis_index_groups=groups, tiled=True)  8.47 us
    ppermute x11, waiting for transfers between devices, shift(): return lax.ppermute(v, axis, [(i, (i + k) % size) for i in range(size)])  6.94 us
    pallas_call x2, Pallas kernels, sums_of(): pl.pallas_call(sum_kernel, out_shape=(shape(Z * PACK, 128, dtype=BF16), s...  4.86 us
    all_to_all x1, waiting for transfers between devices, exchange(): lax.all_to_all(v, (*axes, 'c'), 0, 0, axis_index_groups=groups, tiled=True)  4.4 us
    pallas_call x3, Pallas kernels, arrive(): pl.pallas_call(functools.partial(arrive_kernel, part, len(earlier)), out_...  3.15 us
  transfers between devices with their start and end apart: 12, of which 7 were waited for; matrix products, arithmetic and copies ran while one was open for 0% of the time, Pallas kernels for 5%

profile of v6, /device:TPU:2, one launch (start us, length us, event | category | flops | bytes accessed | tf_op | source)
XLA Modules:
  0.0 125.0 jit_solution(13293413608198807603)
XLA Ops:
  0.6 0.9 quarter.1
  1.6 2.2 %collective-permute-start = (bf16[128,768]{1,0:T(8,128)(2,1)S(1)}, bf16[128,768]{1,0:T(8,128)(2,1)S(1)}, u32[]{:S(2)}, u32[]{:S(2)}) collective-permute-start(bf16[128,768]{1,0:T(8,128)(2,1)S(1)} %quarter.1), channel_id=1, source_target_pairs={{0,16},{8,24},{16,0},{24,8},{1,17},{9,25},{17,1},{25,9},{2,18},{10... | collective-permute-start | bytes 589832 | tf_op jit(solution)/shard_map/ppermute | solution.py:322
  3.8 2.2 %prepare.1 = (bf16[512,768]{1,0:T(8,128)(2,1)}, bf16[256,768]{1,0:T(8,128)(2,1)S(1)}) custom-call(bf16[1024,768]{1,0:T(8,128)(2,1)} %refs_0_.1, f32[32,768]{1,0:T(8,128)} %cur_ref.1), custom_call_target="tpu_custom_call" | custom-call | tf_op jit(solution)/shard_map/prepare/pallas_call | solution.py:98
  6.0 0.8 copy-done.2
  6.8 1.6 %collective-permute-start.1 = (bf16[512,768]{1,0:T(8,128)(2,1)}, bf16[512,768]{1,0:T(8,128)(2,1)S(1)}, u32[]{:S(2)}, u32[]{:S(2)}) collective-permute-start(bf16[512,768]{1,0:T(8,128)(2,1)} %get-tuple-element.42), channel_id=1, source_target_pairs={{0,8},{8,16},{16,24},{24,0},{1,9},{9,17},{17,25},{25,1},{2,10},{10... | collective-permute-start | bytes 2359304 | tf_op jit(solution)/shard_map/ppermute | solution.py:322
  8.4 0.4 collective-permute-start.2
  8.8 1.1 collective-permute-done.refs_0_
  9.9 0.7 copy-done.3
  10.6 8.5 %all-to-all-start = ((bf16[8,32,768]{2,1,0:T(8,128)(2,1)}), bf16[8,32,768]{2,1,0:T(8,128)(2,1)S(1)}, u32[]{:S(2)}, u32[]{:S(2)}) async-start(bf16[8,32,768]{2,1,0:T(8,128)(2,1)} %bitcast.26), calls=%async_computation | async-start | bytes 786432 | tf_op jit(solution)/shard_map/all_to_all | solution.py:331
  19.0 1.6 %collective-permute-start.3 = (bf16[128,768]{1,0:T(8,128)(2,1)}, bf16[128,768]{1,0:T(8,128)(2,1)}, u32[]{:S(2)}, u32[]{:S(2)}) collective-permute-start(bf16[128,768]{1,0:T(8,128)(2,1)} %copy-done.3), channel_id=1, source_target_pairs={{0,2},{2,4},{4,6},{6,0},{1,3},{3,5},{5,7},{7,1},{8,10},{10,12},{12... | collective-permute-start | bytes 589832 | tf_op jit(solution)/shard_map/ppermute | solution.py:322
  20.6 2.9 %collective-permute-start.4 = (bf16[128,768]{1,0:T(8,128)(2,1)}, bf16[128,768]{1,0:T(8,128)(2,1)}, u32[]{:S(2)}, u32[]{:S(2)}) collective-permute-start(bf16[128,768]{1,0:T(8,128)(2,1)} %copy-done.3), channel_id=1, source_target_pairs={{0,4},{2,6},{4,0},{6,2},{1,5},{3,7},{5,1},{7,3},{8,12},{10,14},{12... | collective-permute-start | bytes 589832 | tf_op jit(solution)/shard_map/ppermute | solution.py:322
  23.5 1.3 %collective-permute-start.5 = (bf16[128,768]{1,0:T(8,128)(2,1)}, bf16[128,768]{1,0:T(8,128)(2,1)}, u32[]{:S(2)}, u32[]{:S(2)}) collective-permute-start(bf16[128,768]{1,0:T(8,128)(2,1)} %copy-done.3), channel_id=1, source_target_pairs={{0,6},{2,0},{4,2},{6,4},{1,7},{3,1},{5,3},{7,5},{8,14},{10,8},{12,... | collective-permute-start | bytes 589832 | tf_op jit(solution)/shard_map/ppermute | solution.py:322
  24.9 4.4 %all-to-all-done = bf16[8,32,768]{2,1,0:T(8,128)(2,1)S(1)} async-done(((bf16[8,32,768]{2,1,0:T(8,128)(2,1)}), bf16[8,32,768]{2,1,0:T(8,128)(2,1)S(1)}, u32[]{:S(2)}, u32[]{:S(2)}) %all-to-all-start) | async-done | bytes 393248 | tf_op jit(solution)/shard_map/all_to_all | solution.py:331
  29.3 0.8 arrive.3
  30.1 2.1 %collective-permute-done.4.refs_2_ = bf16[128,768]{1,0:T(8,128)(2,1)} collective-permute-done((bf16[128,768]{1,0:T(8,128)(2,1)}, bf16[128,768]{1,0:T(8,128)(2,1)}, u32[]{:S(2)}, u32[]{:S(2)}) %collective-permute-start.4) | collective-permute-done | bytes 196640 | tf_op jit(solution)/shard_map/ppermute | solution.py:322
  32.3 0.5 collective-permute-start.8
  32.8 1.2 join.1.refs_0_
  34.2 0.4 collective-permute-done.7.refs_1_
  34.6 1.1 collective-permute-done.8.refs_3_
  35.7 1.5 %arrive.4 = (bf16[2048,768]{1,0:T(8,128)(2,1)S(1)}, bf16[256,2048]{1,0:T(8,128)(2,1)S(1)}, f32[16,128]{1,0:T(8,128)S(1)}, f32[16,128]{1,0:T(8,128)S(1)}) custom-call(bf16[256,768]{1,0:T(8,128)(2,1)S(1)} %bitcast.15, bf16[512,768]{1,0:T(8,128)(2,1)S(1)} %collective-permute-done.1.refs_0_, bf16[512,768]{1,0:T(8,128)(2,1)S(1)} %collective-permute-done.7.refs_1_, ...), custom_call_target="tpu_custom_call" | custom-call | tf_op jit(solution)/shard_map/arrive/pallas_call | solution.py:179
  37.2 0.9 arrive.5
  38.3 1.0 collective-permute-done.9.b_ref
  39.4 13.4 %all_to_all.66 = f32[16,32,128]{2,1,0:T(8,128)S(1)} all-to-all(f32[16,32,128]{2,1,0:T(8,128)S(1)} %bitcast.22), channel_id=1, replica_groups={{0,2,4,6,8,10,12,14,16,18,20,22,24,26,28,30},{31,29,27,25,23,21,19,17,1..., dimensions={0} | all-to-all | bytes 524288 | tf_op jit(solution)/shard_map/all_to_all | solution.py:331
  52.8 2.4 %sums.2 = (bf16[1664,128]{1,0:T(8,128)(2,1)S(1)}, f32[8,128]{1,0:T(8,128)}) custom-call(f32[512,128]{1,0:T(8,128)S(1)} %bitcast.21, bf16[256,1024]{1,0:T(8,128)(2,1)S(1)} %get-tuple-element.52.refs_0_, bf16[256,2048]{1,0:T(8,128)(2,1)S(1)} %get-tuple-element.53.refs_1_, bf16[256,1024]{1,0:T(8,128)(2,1)S(1)} %get-tuple-element.54.refs_2_, ...), custom_call_target="tpu_custom_call" | custom-call | tf_op jit(solution)/shard_map/sums/pallas_call | solution.py:279
  55.2 17.0 %all_to_all.67 = bf16[8,208,128]{2,1,0:T(8,128)(2,1)S(1)} all-to-all(bf16[8,208,128]{2,1,0:T(8,128)(2,1)S(1)} %bitcast.25), channel_id=1, replica_groups={{0,128,64,192,32,160,96,224},{225,97,161,33,193,65,129,1},{2,130,66,194..., dimensions={0} | all-to-all | bytes 851968 | tf_op jit(solution)/shard_map/all_to_all | solution.py:331
  72.5 16.5 %all_to_all.68 = bf16[8,32,768]{2,1,0:T(8,128)(2,1)S(1)} all-to-all(bf16[8,32,768]{2,1,0:T(8,128)(2,1)S(1)} %bitcast.27), channel_id=1, replica_groups={{0,128,64,192,32,160,96,224},{225,97,161,33,193,65,129,1},{2,130,66,194..., dimensions={0} | all-to-all | bytes 786432 | tf_op jit(solution)/shard_map/all_to_all | solution.py:331
  89.0 2.1 %score.1 = (bf16[256,1024]{1,0:T(8,128)(2,1)S(1)}, bf16[256,2048]{1,0:T(8,128)(2,1)S(1)}, bf16[256,1024]{1,0:T(8,128)(2,1)S(1)}, f32[8,128]{1,0:T(8,128)S(1)}, f...) custom-call(bf16[256,768]{1,0:T(8,128)(2,1)S(1)} %bitcast.19, ...), custom_call_target="tpu_custom_call" | custom-call | tf_op jit(solution)/shard_map/score/pallas_call | solution.py:205
  91.2 1.2 collective-permute-done.10.b_ref
  92.4 12.8 %all_to_all.69 = f32[16,32,128]{2,1,0:T(8,128)S(1)} all-to-all(f32[16,32,128]{2,1,0:T(8,128)S(1)} %bitcast.23), channel_id=1, replica_groups={{0,2,4,6,8,10,12,14,16,18,20,22,24,26,28,30},{31,29,27,25,23,21,19,17,1..., dimensions={0} | all-to-all | bytes 524288 | tf_op jit(solution)/shard_map/all_to_all | solution.py:331
  105.2 2.4 %sums.3 = (bf16[1664,128]{1,0:T(8,128)(2,1)S(1)}, f32[8,128]{1,0:T(8,128)}) custom-call(f32[512,128]{1,0:T(8,128)S(1)} %bitcast.20, bf16[256,1024]{1,0:T(8,128)(2,1)S(1)} %get-tuple-element.64.refs_0_, bf16[256,2048]{1,0:T(8,128)(2,1)S(1)} %get-tuple-element.65.refs_1_, bf16[256,1024]{1,0:T(8,128)(2,1)S(1)} %get-tuple-element.66.refs_2_, ...), custom_call_target="tpu_custom_call" | custom-call | tf_op jit(solution)/shard_map/sums/pallas_call | solution.py:279
  107.7 16.5 %all_to_all.70 = bf16[8,208,128]{2,1,0:T(8,128)(2,1)S(1)} all-to-all(bf16[8,208,128]{2,1,0:T(8,128)(2,1)S(1)} %bitcast.24), channel_id=1, replica_groups={{0,128,64,192,32,160,96,224},{225,97,161,33,193,65,129,1},{2,130,66,194..., dimensions={0} | all-to-all | bytes 851968 | tf_op jit(solution)/shard_map/all_to_all | solution.py:331
  124.1 0.9 update.3
  (20 shorter events, 1.0 us)
Async XLA Ops:
  1.6 27.7 %copy-start = (bf16[1024,768]{1,0:T(8,128)(2,1)S(1)}, bf16[1024,768]{1,0:T(8,128)(2,1)}, u32[]{:S(2)}) copy-start(bf16[1024,768]{1,0:T(8,128)(2,1)} %refs_0_.1) | copy-start | bytes 4718596
  1.6 8.3 %collective-permute-start = (bf16[128,768]{1,0:T(8,128)(2,1)S(1)}, bf16[128,768]{1,0:T(8,128)(2,1)S(1)}, u32[]{:S(2)}, u32[]{:S(2)}) collective-permute-start(bf16[128,768]{1,0:T(8,128)(2,1)S(1)} %quarter.1), channel_id=1, source_target_pairs={{0,16},{8,24},{16,0},{24,8},{1,17},{9,25},{17,1},{25,9},{2,18},{10... | collective-permute-start | bytes 589832 | tf_op jit(solution)/shard_map/ppermute | solution.py:322
  6.0 0.8 copy-start.2
  6.8 25.5 %collective-permute-start.1 = (bf16[512,768]{1,0:T(8,128)(2,1)}, bf16[512,768]{1,0:T(8,128)(2,1)S(1)}, u32[]{:S(2)}, u32[]{:S(2)}) collective-permute-start(bf16[512,768]{1,0:T(8,128)(2,1)} %get-tuple-element.42), channel_id=1, source_target_pairs={{0,8},{8,16},{16,24},{24,0},{1,9},{9,17},{17,25},{25,1},{2,10},{10... | collective-permute-start | bytes 2359304 | tf_op jit(solution)/shard_map/ppermute | solution.py:322
  8.4 23.8 %collective-permute-start.2 = (bf16[512,768]{1,0:T(8,128)(2,1)}, bf16[512,768]{1,0:T(8,128)(2,1)S(1)}, u32[]{:S(2)}, u32[]{:S(2)}) collective-permute-start(bf16[512,768]{1,0:T(8,128)(2,1)} %get-tuple-element.42), channel_id=1, source_target_pairs={{0,24},{8,0},{16,8},{24,16},{1,25},{9,1},{17,9},{25,17},{2,26},{10... | collective-permute-start | bytes 2359304 | tf_op jit(solution)/shard_map/ppermute | solution.py:322
  9.9 0.7 copy-start.3
  10.6 18.7 %all-to-all-start = ((bf16[8,32,768]{2,1,0:T(8,128)(2,1)}), bf16[8,32,768]{2,1,0:T(8,128)(2,1)S(1)}, u32[]{:S(2)}, u32[]{:S(2)}) async-start(bf16[8,32,768]{2,1,0:T(8,128)(2,1)} %bitcast.26), calls=%async_computation | async-start | bytes 786432 | tf_op jit(solution)/shard_map/all_to_all | solution.py:331
  19.0 11.1 %collective-permute-start.3 = (bf16[128,768]{1,0:T(8,128)(2,1)}, bf16[128,768]{1,0:T(8,128)(2,1)}, u32[]{:S(2)}, u32[]{:S(2)}) collective-permute-start(bf16[128,768]{1,0:T(8,128)(2,1)} %copy-done.3), channel_id=1, source_target_pairs={{0,2},{2,4},{4,6},{6,0},{1,3},{3,5},{5,7},{7,1},{8,10},{10,12},{12... | collective-permute-start | bytes 589832 | tf_op jit(solution)/shard_map/ppermute | solution.py:322
  20.6 11.6 %collective-permute-start.4 = (bf16[128,768]{1,0:T(8,128)(2,1)}, bf16[128,768]{1,0:T(8,128)(2,1)}, u32[]{:S(2)}, u32[]{:S(2)}) collective-permute-start(bf16[128,768]{1,0:T(8,128)(2,1)} %copy-done.3), channel_id=1, source_target_pairs={{0,4},{2,6},{4,0},{6,2},{1,5},{3,7},{5,1},{7,3},{8,12},{10,14},{12... | collective-permute-start | bytes 589832 | tf_op jit(solution)/shard_map/ppermute | solution.py:322
  23.5 8.7 %collective-permute-start.5 = (bf16[128,768]{1,0:T(8,128)(2,1)}, bf16[128,768]{1,0:T(8,128)(2,1)}, u32[]{:S(2)}, u32[]{:S(2)}) collective-permute-start(bf16[128,768]{1,0:T(8,128)(2,1)} %copy-done.3), channel_id=1, source_target_pairs={{0,6},{2,0},{4,2},{6,4},{1,7},{3,1},{5,3},{7,5},{8,14},{10,8},{12,... | collective-permute-start | bytes 589832 | tf_op jit(solution)/shard_map/ppermute | solution.py:322
  29.3 3.6 %copy-start.4 = (bf16[128,768]{1,0:T(8,128)(2,1)S(1)}, bf16[128,768]{1,0:T(8,128)(2,1)}, u32[]{:S(2)}) copy-start(bf16[128,768]{1,0:T(8,128)(2,1)} %copy-done.3) | copy-start | bytes 589828
  32.2 2.4 %collective-permute-start.7 = (bf16[512,768]{1,0:T(8,128)(2,1)S(1)}, bf16[512,768]{1,0:T(8,128)(2,1)S(1)}, u32[]{:S(2)}, u32[]{:S(2)}) collective-permute-start(bf16[512,768]{1,0:T(8,128)(2,1)S(1)} %collective-permute-done.1.refs_0_), channel_id=1, source_target_pairs={{0,1},{1,0},{2,3},{3,2},{4,5},{5,4},{6,7},{7,6},{8,9},{9,8},{10,11... | collective-permute-start | bytes 2359304 | tf_op jit(solution)/shard_map/ppermute | solution.py:322
  32.3 3.4 %collective-permute-start.8 = (bf16[512,768]{1,0:T(8,128)(2,1)S(1)}, bf16[512,768]{1,0:T(8,128)(2,1)S(1)}, u32[]{:S(2)}, u32[]{:S(2)}) collective-permute-start(bf16[512,768]{1,0:T(8,128)(2,1)S(1)} %collective-permute-done.2.refs_2_), channel_id=1, source_target_pairs={{0,1},{1,0},{2,3},{3,2},{4,5},{5,4},{6,7},{7,6},{8,9},{9,8},{10,11... | collective-permute-start | bytes 2359304 | tf_op jit(solution)/shard_map/ppermute | solution.py:322
  34.0 3.2 %collective-permute-start.6 = (bf16[512,768]{1,0:T(8,128)(2,1)S(1)}, bf16[512,768]{1,0:T(8,128)(2,1)S(1)}, u32[]{:S(2)}, u32[]{:S(2)}) collective-permute-start(bf16[512,768]{1,0:T(8,128)(2,1)S(1)} %join.1.refs_0_), channel_id=1, source_target_pairs={{0,1},{1,0},{2,3},{3,2},{4,5},{5,4},{6,7},{7,6},{8,9},{9,8},{10,11... | collective-permute-start | bytes 2359304 | tf_op jit(solution)/shard_map/ppermute | solution.py:322
  38.1 1.3 %collective-permute-start.9 = (f32[32,128]{1,0:T(8,128)S(1)}, f32[32,128]{1,0:T(8,128)S(1)}, u32[]{:S(2)}, u32[]{:S(2)}) collective-permute-start(f32[32,128]{1,0:T(8,128)S(1)} %get-tuple-element.51.a_ref), channel_id=1, source_target_pairs={{0,1},{1,0},{2,3},{3,2},{4,5},{5,4},{6,7},{7,6},{8,9},{9,8},{10,11... | collective-permute-start | bytes 49160 | tf_op jit(solution)/shard_map/ppermute | solution.py:322
  52.8 19.5 %copy-start.1 = (f32[32,768]{1,0:T(8,128)S(1)}, f32[32,768]{1,0:T(8,128)}, u32[]{:S(2)}) copy-start(f32[32,768]{1,0:T(8,128)} %cur_ref.1) | copy-start | bytes 294916
  91.1 1.3 %collective-permute-start.10 = (f32[32,128]{1,0:T(8,128)S(1)}, f32[32,128]{1,0:T(8,128)S(1)}, u32[]{:S(2)}, u32[]{:S(2)}) collective-permute-start(f32[32,128]{1,0:T(8,128)S(1)} %get-tuple-element.63.a_ref), channel_id=1, source_target_pairs={{0,1},{1,0},{2,3},{3,2},{4,5},{5,4},{6,7},{7,6},{8,9},{9,8},{10,11... | collective-permute-start | bytes 49160 | tf_op jit(solution)/shard_map/ppermute | solution.py:322

commit v7 on v6

--- a/solution.py
+++ b/solution.py
@@ -236,15 +236,16 @@
     )(a, b)
 
 
-def sum_kernel(lses_ref, *refs):
+def sum_kernel(last, lses_ref, *refs):
     n = len(PARTS)
     ps, ms, embs = refs[:n], refs[n : 2 * n], refs[2 * n : 3 * n]
-    out_ref, row_ref, lse_ref = refs[3 * n :]
+    out_ref, lse_ref = refs[3 * n], refs[-1]
     lses = [lses_ref[pl.ds(i * 32, 32), :] for i in range(X * Y)]
     peak = functools.reduce(jnp.maximum, lses)
     total = sum(jnp.exp2(v - peak) for v in lses)
     lse_ref[...] = peak + jnp.log2(total)
-    row_ref[...] = lse_ref[column_of(0), :] * math.log(2.0)
+    if last:
+        refs[3 * n + 1][...] = lse_ref[column_of(0), :] * math.log(2.0)
     weights = jnp.zeros((K, 128), F32)
     sums = jnp.zeros((K, D), F32)
     for part, p_ref, m_ref, emb in zip(PARTS, ps, ms, embs):
@@ -274,20 +275,26 @@
         out_ref[pl.ds(i * PACK + PACK - 16, 16), :] = tail.astype(BF16)
 
 
-def sums_of(lses, ps, ms, embs):
+def sums_of(lses, ps, ms, embs, last):
     n = len(PARTS)
     return pl.pallas_call(
-        sum_kernel,
-        out_shape=(shape(Z * PACK, 128, dtype=BF16), shape(8, 128)),
+        functools.partial(sum_kernel, last),
+        out_shape=(pltpu.VMEM((Z * PACK, 128), BF16), *([pltpu.VMEM((8, 128), F32)] if last else [])),
         in_specs=[VMEM] * (1 + 3 * n),
-        out_specs=(VMEM, VMEM),
+        out_specs=(VMEM,) * (1 + last),
         scratch_shapes=[pltpu.VMEM((X * 8, 128), F32)],
         compiler_params=limit(16),
         name="sums",
     )(lses, *ps, *ms, *embs)
 
 
-def update_kernel(last, got_ref, cur_ref, new_ref, out_ref):
+def update_kernel(last, got_ref, cur_ref, *refs):
+    if last:
+        lse_ref, new_ref, out_ref, row_ref = refs
+        row_ref[...] = lse_ref[...]
+    else:
+        new_ref, out_ref = refs
+
     def total(at, n):
         return sum(got_ref[pl.ds(i * PACK + at, n), :].astype(F32) for i in range(Z))
 
@@ -307,15 +314,18 @@
         out_ref[...] = jnp.sum(jnp.where(row == lane, counts, 0.0), axis=0, keepdims=True)
 
 
-def update(got, current, last):
+def update(got, current, row_lse=None):
+    last = row_lse is not None
     return pl.pallas_call(
         functools.partial(update_kernel, last),
-        out_shape=(shape(OWN, D), shape(1, OWN) if last else shape(K, D, dtype=BF16)),
-        in_specs=[VMEM, VMEM],
-        out_specs=(VMEM, VMEM),
+        out_shape=(
+            (shape(OWN, D), shape(1, OWN), shape(8, 128)) if last else (shape(OWN, D), shape(K, D, dtype=BF16))
+        ),
+        in_specs=[VMEM] * (2 + last),
+        out_specs=(VMEM,) * (2 + last),
         compiler_params=limit(8),
         name="update",
-    )(got, current)
+    )(got, current, *([row_lse] if last else []))
 
 
 def shift(v, axis, size, k):
@@ -350,10 +360,13 @@
             cent = exchange(out, ("z",), RING)
             ps, ms, lse = score(cent, embs)
         lses = exchange(combine(lse, swap(lse)), ("x", "y"), PLANE)
-        sums, row_lse = sums_of(lses, ps, ms, embs)
+        last = step == ITERS - 1
+        sums, *row_lse = sums_of(lses, ps, ms, embs, last)
         got = exchange(sums, ("z",), RING)
-        current, out = update(got, current, step == ITERS - 1)
-    return current, out.reshape(OWN), row_lse.reshape(COL)
+        if not last:
+            current, out = update(got, current)
+    current, counts, row_lse = update(got, current, row_lse[0])
+    return current, counts.reshape(OWN), row_lse.reshape(COL)
 
 
 def solution(mesh):

time: 125 us -> 124 us (level)
  no operation moved by 1% of the time
where the time goes in v7:
time: 124 us
  blocking collectives  76.2 us (61%)
  starting transfers between devices  19.6 us (16%)
  Pallas kernels  14.6 us (12%)
  waiting for transfers between devices  11.3 us (9%)
  local copies, waits for them, and re-layouts  1.45 us (1%)
    all_to_all x5, blocking collectives, exchange(): lax.all_to_all(v, (*axes, 'c'), 0, 0, axis_index_groups=groups, tiled=True)  76.2 us
    ppermute x11, starting transfers between devices, shift(): return lax.ppermute(v, axis, [(i, (i + k) % size) for i in range(size)])  11.2 us
    all_to_all x1, starting transfers between devices, exchange(): lax.all_to_all(v, (*axes, 'c'), 0, 0, axis_index_groups=groups, tiled=True)  8.47 us
    ppermute x11, waiting for transfers between devices, shift(): return lax.ppermute(v, axis, [(i, (i + k) % size) for i in range(size)])  6.94 us
    all_to_all x1, waiting for transfers between devices, exchange(): lax.all_to_all(v, (*axes, 'c'), 0, 0, axis_index_groups=groups, tiled=True)  4.4 us
    pallas_call x2, Pallas kernels, sums_of(): pl.pallas_call(functools.partial(sum_kernel, last), out_shape=(pltpu.VMEM...  3.84 us
    pallas_call x3, Pallas kernels, arrive(): pl.pallas_call(functools.partial(arrive_kernel, part, len(earlier)), out_...  3.15 us
  transfers between devices with their start and end apart: 12, of which 7 were waited for; matrix products, arithmetic and copies ran while one was open for 0% of the time, Pallas kernels for 5%

profile of v7, /device:TPU:2, one launch (start us, length us, event | category | flops | bytes accessed | tf_op | source)
XLA Modules:
  0.0 124.0 jit_solution(3422821906433903354)
XLA Ops:
  0.6 0.9 quarter.1
  1.6 2.2 %collective-permute-start = (bf16[128,768]{1,0:T(8,128)(2,1)S(1)}, bf16[128,768]{1,0:T(8,128)(2,1)S(1)}, u32[]{:S(2)}, u32[]{:S(2)}) collective-permute-start(bf16[128,768]{1,0:T(8,128)(2,1)S(1)} %quarter.1), channel_id=1, source_target_pairs={{0,16},{8,24},{16,0},{24,8},{1,17},{9,25},{17,1},{25,9},{2,18},{10... | collective-permute-start | bytes 589832 | tf_op jit(solution)/shard_map/ppermute | solution.py:332
  3.8 2.2 %prepare.1 = (bf16[512,768]{1,0:T(8,128)(2,1)}, bf16[256,768]{1,0:T(8,128)(2,1)S(1)}) custom-call(bf16[1024,768]{1,0:T(8,128)(2,1)} %refs_0_.1, f32[32,768]{1,0:T(8,128)} %cur_ref.1), custom_call_target="tpu_custom_call" | custom-call | tf_op jit(solution)/shard_map/prepare/pallas_call | solution.py:98
  6.0 0.8 copy-done.2
  6.8 1.6 %collective-permute-start.1 = (bf16[512,768]{1,0:T(8,128)(2,1)}, bf16[512,768]{1,0:T(8,128)(2,1)S(1)}, u32[]{:S(2)}, u32[]{:S(2)}) collective-permute-start(bf16[512,768]{1,0:T(8,128)(2,1)} %get-tuple-element.42), channel_id=1, source_target_pairs={{0,8},{8,16},{16,24},{24,0},{1,9},{9,17},{17,25},{25,1},{2,10},{10... | collective-permute-start | bytes 2359304 | tf_op jit(solution)/shard_map/ppermute | solution.py:332
  8.4 0.4 collective-permute-start.2
  8.8 1.1 collective-permute-done.refs_0_
  9.9 0.7 copy-done.3
  10.5 8.5 %all-to-all-start = ((bf16[8,32,768]{2,1,0:T(8,128)(2,1)}), bf16[8,32,768]{2,1,0:T(8,128)(2,1)S(1)}, u32[]{:S(2)}, u32[]{:S(2)}) async-start(bf16[8,32,768]{2,1,0:T(8,128)(2,1)} %bitcast.26), calls=%async_computation | async-start | bytes 786432 | tf_op jit(solution)/shard_map/all_to_all | solution.py:341
  19.0 1.6 %collective-permute-start.3 = (bf16[128,768]{1,0:T(8,128)(2,1)}, bf16[128,768]{1,0:T(8,128)(2,1)}, u32[]{:S(2)}, u32[]{:S(2)}) collective-permute-start(bf16[128,768]{1,0:T(8,128)(2,1)} %copy-done.3), channel_id=1, source_target_pairs={{0,2},{2,4},{4,6},{6,0},{1,3},{3,5},{5,7},{7,1},{8,10},{10,12},{12... | collective-permute-start | bytes 589832 | tf_op jit(solution)/shard_map/ppermute | solution.py:332
  20.6 2.9 %collective-permute-start.4 = (bf16[128,768]{1,0:T(8,128)(2,1)}, bf16[128,768]{1,0:T(8,128)(2,1)}, u32[]{:S(2)}, u32[]{:S(2)}) collective-permute-start(bf16[128,768]{1,0:T(8,128)(2,1)} %copy-done.3), channel_id=1, source_target_pairs={{0,4},{2,6},{4,0},{6,2},{1,5},{3,7},{5,1},{7,3},{8,12},{10,14},{12... | collective-permute-start | bytes 589832 | tf_op jit(solution)/shard_map/ppermute | solution.py:332
  23.5 1.3 %collective-permute-start.5 = (bf16[128,768]{1,0:T(8,128)(2,1)}, bf16[128,768]{1,0:T(8,128)(2,1)}, u32[]{:S(2)}, u32[]{:S(2)}) collective-permute-start(bf16[128,768]{1,0:T(8,128)(2,1)} %copy-done.3), channel_id=1, source_target_pairs={{0,6},{2,0},{4,2},{6,4},{1,7},{3,1},{5,3},{7,5},{8,14},{10,8},{12,... | collective-permute-start | bytes 589832 | tf_op jit(solution)/shard_map/ppermute | solution.py:332
  24.8 4.4 %all-to-all-done = bf16[8,32,768]{2,1,0:T(8,128)(2,1)S(1)} async-done(((bf16[8,32,768]{2,1,0:T(8,128)(2,1)}), bf16[8,32,768]{2,1,0:T(8,128)(2,1)S(1)}, u32[]{:S(2)}, u32[]{:S(2)}) %all-to-all-start) | async-done | bytes 393248 | tf_op jit(solution)/shard_map/all_to_all | solution.py:341
  29.2 0.8 arrive.3
  30.1 2.1 %collective-permute-done.4.refs_2_ = bf16[128,768]{1,0:T(8,128)(2,1)} collective-permute-done((bf16[128,768]{1,0:T(8,128)(2,1)}, bf16[128,768]{1,0:T(8,128)(2,1)}, u32[]{:S(2)}, u32[]{:S(2)}) %collective-permute-start.4) | collective-permute-done | bytes 196640 | tf_op jit(solution)/shard_map/ppermute | solution.py:332
  32.3 0.5 collective-permute-start.8
  32.8 1.2 join.1.refs_0_
  34.2 0.4 collective-permute-done.7.refs_1_
  34.6 1.1 collective-permute-done.8.refs_3_
  35.7 1.5 %arrive.4 = (bf16[2048,768]{1,0:T(8,128)(2,1)S(1)}, bf16[256,2048]{1,0:T(8,128)(2,1)S(1)}, f32[16,128]{1,0:T(8,128)S(1)}, f32[16,128]{1,0:T(8,128)S(1)}) custom-call(bf16[256,768]{1,0:T(8,128)(2,1)S(1)} %bitcast.15, bf16[512,768]{1,0:T(8,128)(2,1)S(1)} %collective-permute-done.1.refs_0_, bf16[512,768]{1,0:T(8,128)(2,1)S(1)} %collective-permute-done.7.refs_1_, ...), custom_call_target="tpu_custom_call" | custom-call | tf_op jit(solution)/shard_map/arrive/pallas_call | solution.py:179
  37.2 0.9 arrive.5
  38.3 1.0 collective-permute-done.9.b_ref
  39.4 13.4 %all_to_all.66 = f32[16,32,128]{2,1,0:T(8,128)S(1)} all-to-all(f32[16,32,128]{2,1,0:T(8,128)S(1)} %bitcast.23), channel_id=1, replica_groups={{0,2,4,6,8,10,12,14,16,18,20,22,24,26,28,30},{31,29,27,25,23,21,19,17,1..., dimensions={0} | all-to-all | bytes 524288 | tf_op jit(solution)/shard_map/all_to_all | solution.py:341
  52.8 1.9 %sums.2 = bf16[1664,128]{1,0:T(8,128)(2,1)S(1)} custom-call(f32[512,128]{1,0:T(8,128)S(1)} %bitcast.22, bf16[256,1024]{1,0:T(8,128)(2,1)S(1)} %get-tuple-element.52.refs_0_, bf16[256,2048]{1,0:T(8,128)(2,1)S(1)} %get-tuple-element.53.refs_1_, bf16[256,1024]{1,0:T(8,128)(2,1)S(1)} %get-tuple-element.54.refs_2_, f32[8,128]{1,0:T(8,128)S(1)} %get-tuple-element.55.refs_3_, ...), custom_call_target="tpu_custom_call" | custom-call | tf_op jit(solution)/shard_map/sums/pallas_call | solution.py:280
  54.7 17.0 %all_to_all.67 = bf16[8,208,128]{2,1,0:T(8,128)(2,1)S(1)} all-to-all(bf16[8,208,128]{2,1,0:T(8,128)(2,1)S(1)} %bitcast.19), channel_id=1, replica_groups={{0,128,64,192,32,160,96,224},{225,97,161,33,193,65,129,1},{2,130,66,194..., dimensions={0} | all-to-all | bytes 851968 | tf_op jit(solution)/shard_map/all_to_all | solution.py:341
  72.0 16.4 %all_to_all.68 = bf16[8,32,768]{2,1,0:T(8,128)(2,1)S(1)} all-to-all(bf16[8,32,768]{2,1,0:T(8,128)(2,1)S(1)} %bitcast.27), channel_id=1, replica_groups={{0,128,64,192,32,160,96,224},{225,97,161,33,193,65,129,1},{2,130,66,194..., dimensions={0} | all-to-all | bytes 786432 | tf_op jit(solution)/shard_map/all_to_all | solution.py:341
  88.4 2.1 %score.1 = (bf16[256,1024]{1,0:T(8,128)(2,1)S(1)}, bf16[256,2048]{1,0:T(8,128)(2,1)S(1)}, bf16[256,1024]{1,0:T(8,128)(2,1)S(1)}, f32[8,128]{1,0:T(8,128)S(1)}, f...) custom-call(bf16[256,768]{1,0:T(8,128)(2,1)S(1)} %bitcast.20, ...), custom_call_target="tpu_custom_call" | custom-call | tf_op jit(solution)/shard_map/score/pallas_call | solution.py:205
  90.6 1.2 collective-permute-done.10.b_ref
  91.8 12.9 %all_to_all.69 = f32[16,32,128]{2,1,0:T(8,128)S(1)} all-to-all(f32[16,32,128]{2,1,0:T(8,128)S(1)} %bitcast.24), channel_id=1, replica_groups={{0,2,4,6,8,10,12,14,16,18,20,22,24,26,28,30},{31,29,27,25,23,21,19,17,1..., dimensions={0} | all-to-all | bytes 524288 | tf_op jit(solution)/shard_map/all_to_all | solution.py:341
  104.7 1.9 %sums.3 = (bf16[1664,128]{1,0:T(8,128)(2,1)S(1)}, f32[8,128]{1,0:T(8,128)S(1)}) custom-call(f32[512,128]{1,0:T(8,128)S(1)} %bitcast.21, bf16[256,1024]{1,0:T(8,128)(2,1)S(1)} %get-tuple-element.63.refs_0_, bf16[256,2048]{1,0:T(8,128)(2,1)S(1)} %get-tuple-element.64.refs_1_, bf16[256,1024]{1,0:T(8,128)(2,1)S(1)} %get-tuple-element.65.refs_2_, ...), custom_call_target="tpu_custom_call" | custom-call | tf_op jit(solution)/shard_map/sums/pallas_call | solution.py:280
  106.6 16.5 %all_to_all.70 = bf16[8,208,128]{2,1,0:T(8,128)(2,1)S(1)} all-to-all(bf16[8,208,128]{2,1,0:T(8,128)(2,1)S(1)} %bitcast.25), channel_id=1, replica_groups={{0,128,64,192,32,160,96,224},{225,97,161,33,193,65,129,1},{2,130,66,194..., dimensions={0} | all-to-all | bytes 851968 | tf_op jit(solution)/shard_map/all_to_all | solution.py:341
  123.1 0.9 update.3
  (20 shorter events, 1.0 us)
Async XLA Ops:
  1.6 27.7 %copy-start = (bf16[1024,768]{1,0:T(8,128)(2,1)S(1)}, bf16[1024,768]{1,0:T(8,128)(2,1)}, u32[]{:S(2)}) copy-start(bf16[1024,768]{1,0:T(8,128)(2,1)} %refs_0_.1) | copy-start | bytes 4718596
  1.6 8.3 %collective-permute-start = (bf16[128,768]{1,0:T(8,128)(2,1)S(1)}, bf16[128,768]{1,0:T(8,128)(2,1)S(1)}, u32[]{:S(2)}, u32[]{:S(2)}) collective-permute-start(bf16[128,768]{1,0:T(8,128)(2,1)S(1)} %quarter.1), channel_id=1, source_target_pairs={{0,16},{8,24},{16,0},{24,8},{1,17},{9,25},{17,1},{25,9},{2,18},{10... | collective-permute-start | bytes 589832 | tf_op jit(solution)/shard_map/ppermute | solution.py:332
  6.0 0.8 copy-start.2
  6.8 25.4 %collective-permute-start.1 = (bf16[512,768]{1,0:T(8,128)(2,1)}, bf16[512,768]{1,0:T(8,128)(2,1)S(1)}, u32[]{:S(2)}, u32[]{:S(2)}) collective-permute-start(bf16[512,768]{1,0:T(8,128)(2,1)} %get-tuple-element.42), channel_id=1, source_target_pairs={{0,8},{8,16},{16,24},{24,0},{1,9},{9,17},{17,25},{25,1},{2,10},{10... | collective-permute-start | bytes 2359304 | tf_op jit(solution)/shard_map/ppermute | solution.py:332
  8.4 23.8 %collective-permute-start.2 = (bf16[512,768]{1,0:T(8,128)(2,1)}, bf16[512,768]{1,0:T(8,128)(2,1)S(1)}, u32[]{:S(2)}, u32[]{:S(2)}) collective-permute-start(bf16[512,768]{1,0:T(8,128)(2,1)} %get-tuple-element.42), channel_id=1, source_target_pairs={{0,24},{8,0},{16,8},{24,16},{1,25},{9,1},{17,9},{25,17},{2,26},{10... | collective-permute-start | bytes 2359304 | tf_op jit(solution)/shard_map/ppermute | solution.py:332
  9.9 0.7 copy-start.3
  10.5 18.7 %all-to-all-start = ((bf16[8,32,768]{2,1,0:T(8,128)(2,1)}), bf16[8,32,768]{2,1,0:T(8,128)(2,1)S(1)}, u32[]{:S(2)}, u32[]{:S(2)}) async-start(bf16[8,32,768]{2,1,0:T(8,128)(2,1)} %bitcast.26), calls=%async_computation | async-start | bytes 786432 | tf_op jit(solution)/shard_map/all_to_all | solution.py:341
  19.0 11.1 %collective-permute-start.3 = (bf16[128,768]{1,0:T(8,128)(2,1)}, bf16[128,768]{1,0:T(8,128)(2,1)}, u32[]{:S(2)}, u32[]{:S(2)}) collective-permute-start(bf16[128,768]{1,0:T(8,128)(2,1)} %copy-done.3), channel_id=1, source_target_pairs={{0,2},{2,4},{4,6},{6,0},{1,3},{3,5},{5,7},{7,1},{8,10},{10,12},{12... | collective-permute-start | bytes 589832 | tf_op jit(solution)/shard_map/ppermute | solution.py:332
  20.6 11.6 %collective-permute-start.4 = (bf16[128,768]{1,0:T(8,128)(2,1)}, bf16[128,768]{1,0:T(8,128)(2,1)}, u32[]{:S(2)}, u32[]{:S(2)}) collective-permute-start(bf16[128,768]{1,0:T(8,128)(2,1)} %copy-done.3), channel_id=1, source_target_pairs={{0,4},{2,6},{4,0},{6,2},{1,5},{3,7},{5,1},{7,3},{8,12},{10,14},{12... | collective-permute-start | bytes 589832 | tf_op jit(solution)/shard_map/ppermute | solution.py:332
  23.5 8.7 %collective-permute-start.5 = (bf16[128,768]{1,0:T(8,128)(2,1)}, bf16[128,768]{1,0:T(8,128)(2,1)}, u32[]{:S(2)}, u32[]{:S(2)}) collective-permute-start(bf16[128,768]{1,0:T(8,128)(2,1)} %copy-done.3), channel_id=1, source_target_pairs={{0,6},{2,0},{4,2},{6,4},{1,7},{3,1},{5,3},{7,5},{8,14},{10,8},{12,... | collective-permute-start | bytes 589832 | tf_op jit(solution)/shard_map/ppermute | solution.py:332
  29.2 3.6 %copy-start.4 = (bf16[128,768]{1,0:T(8,128)(2,1)S(1)}, bf16[128,768]{1,0:T(8,128)(2,1)}, u32[]{:S(2)}) copy-start(bf16[128,768]{1,0:T(8,128)(2,1)} %copy-done.3) | copy-start | bytes 589828
  32.2 2.4 %collective-permute-start.7 = (bf16[512,768]{1,0:T(8,128)(2,1)S(1)}, bf16[512,768]{1,0:T(8,128)(2,1)S(1)}, u32[]{:S(2)}, u32[]{:S(2)}) collective-permute-start(bf16[512,768]{1,0:T(8,128)(2,1)S(1)} %collective-permute-done.1.refs_0_), channel_id=1, source_target_pairs={{0,1},{1,0},{2,3},{3,2},{4,5},{5,4},{6,7},{7,6},{8,9},{9,8},{10,11... | collective-permute-start | bytes 2359304 | tf_op jit(solution)/shard_map/ppermute | solution.py:332
  32.3 3.4 %collective-permute-start.8 = (bf16[512,768]{1,0:T(8,128)(2,1)S(1)}, bf16[512,768]{1,0:T(8,128)(2,1)S(1)}, u32[]{:S(2)}, u32[]{:S(2)}) collective-permute-start(bf16[512,768]{1,0:T(8,128)(2,1)S(1)} %collective-permute-done.2.refs_2_), channel_id=1, source_target_pairs={{0,1},{1,0},{2,3},{3,2},{4,5},{5,4},{6,7},{7,6},{8,9},{9,8},{10,11... | collective-permute-start | bytes 2359304 | tf_op jit(solution)/shard_map/ppermute | solution.py:332
  34.0 3.2 %collective-permute-start.6 = (bf16[512,768]{1,0:T(8,128)(2,1)S(1)}, bf16[512,768]{1,0:T(8,128)(2,1)S(1)}, u32[]{:S(2)}, u32[]{:S(2)}) collective-permute-start(bf16[512,768]{1,0:T(8,128)(2,1)S(1)} %join.1.refs_0_), channel_id=1, source_target_pairs={{0,1},{1,0},{2,3},{3,2},{4,5},{5,4},{6,7},{7,6},{8,9},{9,8},{10,11... | collective-permute-start | bytes 2359304 | tf_op jit(solution)/shard_map/ppermute | solution.py:332
  38.0 1.3 %collective-permute-start.9 = (f32[32,128]{1,0:T(8,128)S(1)}, f32[32,128]{1,0:T(8,128)S(1)}, u32[]{:S(2)}, u32[]{:S(2)}) collective-permute-start(f32[32,128]{1,0:T(8,128)S(1)} %get-tuple-element.51.a_ref), channel_id=1, source_target_pairs={{0,1},{1,0},{2,3},{3,2},{4,5},{5,4},{6,7},{7,6},{8,9},{9,8},{10,11... | collective-permute-start | bytes 49160 | tf_op jit(solution)/shard_map/ppermute | solution.py:332
  52.8 18.9 %copy-start.1 = (f32[32,768]{1,0:T(8,128)S(1)}, f32[32,768]{1,0:T(8,128)}, u32[]{:S(2)}) copy-start(f32[32,768]{1,0:T(8,128)} %cur_ref.1) | copy-start | bytes 294916
  90.5 1.3 %collective-permute-start.10 = (f32[32,128]{1,0:T(8,128)S(1)}, f32[32,128]{1,0:T(8,128)S(1)}, u32[]{:S(2)}, u32[]{:S(2)}) collective-permute-start(f32[32,128]{1,0:T(8,128)S(1)} %get-tuple-element.62.a_ref), channel_id=1, source_target_pairs={{0,1},{1,0},{2,3},{3,2},{4,5},{5,4},{6,7},{7,6},{8,9},{9,8},{10,11... | collective-permute-start | bytes 49160 | tf_op jit(solution)/shard_map/ppermute | solution.py:332

commit v8 on v7

--- a/solution.py
+++ b/solution.py
@@ -75,34 +75,41 @@
     )(in_hbm(emb))
 
 
-def prepare_kernel(emb_ref, cent_ref, mine_ref, copies_ref, cent, sems, cent_sem):
+def prepare_kernel(emb_ref, cent_ref, mine_ref, copies_ref, mine, cent, copies, sems, out_sems, cent_sem, copies_sem):
     read = pltpu.make_async_copy(cent_ref, cent, cent_sem)
     read.start()
     at = pl.multiple_of(lax.axis_index("c") * HALF, HALF)
-    waits = []
-    for i in range(0, HALF, 64):
-        waits.append(
-            pltpu.make_async_copy(
-                emb_ref.at[pl.ds(at + i, 64)], mine_ref.at[pl.ds(i, 64)], sems.at[i // 64]
-            )
-        )
-        waits[-1].start()
+    reads, writes = [], []
+    for i in range(HALF // 64):
+        rows = pl.ds(i * 64, 64)
+        reads.append(pltpu.make_async_copy(emb_ref.at[pl.ds(at + i * 64, 64)], mine.at[rows], sems.at[i]))
+        writes.append(pltpu.make_async_copy(mine.at[rows], mine_ref.at[rows], out_sems.at[i]))
+        reads[-1].start()
     read.wait()
     for i in range(Z):
-        copies_ref[pl.ds(i * OWN, OWN), :] = cent[...].astype(BF16)
-    for wait in waits:
-        wait.wait()
+        copies[pl.ds(i * OWN, OWN), :] = cent[...].astype(BF16)
+    writes.append(pltpu.make_async_copy(copies, copies_ref, copies_sem))
+    writes[-1].start()
+    for i in range(HALF // 64):
+        reads[i].wait()
+        writes[i].start()
+    for write in writes:
+        write.wait()
 
 
 def prepare(emb, cent):
     return pl.pallas_call(
         prepare_kernel,
-        out_shape=(pltpu.VMEM((HALF, D), BF16), pltpu.VMEM((K, D), BF16)),
+        out_shape=(pltpu.HBM((HALF, D), BF16), pltpu.HBM((K, D), BF16)),
         in_specs=[ANY, ANY],
-        out_specs=(VMEM,) * 2,
+        out_specs=(ANY,) * 2,
         scratch_shapes=[
+            pltpu.VMEM((HALF, D), BF16),
             pltpu.VMEM((OWN, D), F32),
+            pltpu.VMEM((K, D), BF16),
             pltpu.SemaphoreType.DMA((HALF // 64,)),
+            pltpu.SemaphoreType.DMA((HALF // 64,)),
+            pltpu.SemaphoreType.DMA,
             pltpu.SemaphoreType.DMA,
         ],
         compiler_params=limit(4),

time: 124 us -> 124 us (level)
  no operation moved by 1% of the time
where the time goes in v8:
time: 124 us
  blocking collectives  76.1 us (61%)
  starting transfers between devices  19.7 us (16%)
  Pallas kernels  14.8 us (12%)
  waiting for transfers between devices  11.8 us (10%)
    all_to_all x5, blocking collectives, exchange(): lax.all_to_all(v, (*axes, 'c'), 0, 0, axis_index_groups=groups, tiled=True)  76.1 us
    ppermute x11, starting transfers between devices, shift(): return lax.ppermute(v, axis, [(i, (i + k) % size) for i in range(size)])  11.2 us
    all_to_all x1, starting transfers between devices, exchange(): lax.all_to_all(v, (*axes, 'c'), 0, 0, axis_index_groups=groups, tiled=True)  8.47 us
    ppermute x11, waiting for transfers between devices, shift(): return lax.ppermute(v, axis, [(i, (i + k) % size) for i in range(size)])  7.45 us
    all_to_all x1, waiting for transfers between devices, exchange(): lax.all_to_all(v, (*axes, 'c'), 0, 0, axis_index_groups=groups, tiled=True)  4.37 us
    pallas_call x2, Pallas kernels, sums_of(): pl.pallas_call(functools.partial(sum_kernel, last), out_shape=(pltpu.VMEM...  3.86 us
    pallas_call x3, Pallas kernels, arrive(): pl.pallas_call(functools.partial(arrive_kernel, part, len(earlier)), out_...  3.15 us
  transfers between devices with their start and end apart: 12, of which 7 were waited for; matrix products, arithmetic and copies ran while one was open for 0% of the time, Pallas kernels for 5%

profile of v8, /device:TPU:2, one launch (start us, length us, event | category | flops | bytes accessed | tf_op | source)
XLA Modules:
  0.0 124.0 jit_solution(12728846273568449702)
XLA Ops:
  0.6 0.9 quarter.1
  1.6 2.2 %collective-permute-start = (bf16[128,768]{1,0:T(8,128)(2,1)S(1)}, bf16[128,768]{1,0:T(8,128)(2,1)S(1)}, u32[]{:S(2)}, u32[]{:S(2)}) collective-permute-start(bf16[128,768]{1,0:T(8,128)(2,1)S(1)} %quarter.1), channel_id=1, source_target_pairs={{0,16},{8,24},{16,0},{24,8},{1,17},{9,25},{17,1},{25,9},{2,18},{10... | collective-permute-start | bytes 589832 | tf_op jit(solution)/shard_map/ppermute | solution.py:339
  3.8 2.4 %prepare.1 = (bf16[512,768]{1,0:T(8,128)(2,1)}, bf16[256,768]{1,0:T(8,128)(2,1)}) custom-call(bf16[1024,768]{1,0:T(8,128)(2,1)} %refs_0_.1, f32[32,768]{1,0:T(8,128)} %cur_ref.1), custom_call_target="tpu_custom_call" | custom-call | tf_op jit(solution)/shard_map/prepare/pallas_call | solution.py:101
  6.2 1.7 %collective-permute-start.1 = (bf16[512,768]{1,0:T(8,128)(2,1)}, bf16[512,768]{1,0:T(8,128)(2,1)S(1)}, u32[]{:S(2)}, u32[]{:S(2)}) collective-permute-start(bf16[512,768]{1,0:T(8,128)(2,1)} %get-tuple-element.42), channel_id=1, source_target_pairs={{0,8},{8,16},{16,24},{24,0},{1,9},{9,17},{17,25},{25,1},{2,10},{10... | collective-permute-start | bytes 2359304 | tf_op jit(solution)/shard_map/ppermute | solution.py:339
  7.9 0.4 collective-permute-start.2
  8.3 1.6 %collective-permute-done.refs_0_ = bf16[128,768]{1,0:T(8,128)(2,1)S(1)} collective-permute-done((bf16[128,768]{1,0:T(8,128)(2,1)S(1)}, bf16[128,768]{1,0:T(8,128)(2,1)S(1)}, u32[]{:S(2)}, u32[]{:S(2)}) %collective-permute-start) | collective-permute-done | bytes 196640 | tf_op jit(solution)/shard_map/ppermute | solution.py:339
  9.9 0.7 copy-done.2
  10.6 8.5 %all-to-all-start = ((bf16[8,32,768]{2,1,0:T(8,128)(2,1)}), bf16[8,32,768]{2,1,0:T(8,128)(2,1)S(1)}, u32[]{:S(2)}, u32[]{:S(2)}) async-start(bf16[8,32,768]{2,1,0:T(8,128)(2,1)} %bitcast.27), calls=%async_computation | async-start | bytes 786432 | tf_op jit(solution)/shard_map/all_to_all | solution.py:348
  19.1 1.6 %collective-permute-start.3 = (bf16[128,768]{1,0:T(8,128)(2,1)}, bf16[128,768]{1,0:T(8,128)(2,1)}, u32[]{:S(2)}, u32[]{:S(2)}) collective-permute-start(bf16[128,768]{1,0:T(8,128)(2,1)} %copy-done.2), channel_id=1, source_target_pairs={{0,2},{2,4},{4,6},{6,0},{1,3},{3,5},{5,7},{7,1},{8,10},{10,12},{12... | collective-permute-start | bytes 589832 | tf_op jit(solution)/shard_map/ppermute | solution.py:339
  20.6 2.9 %collective-permute-start.4 = (bf16[128,768]{1,0:T(8,128)(2,1)}, bf16[128,768]{1,0:T(8,128)(2,1)}, u32[]{:S(2)}, u32[]{:S(2)}) collective-permute-start(bf16[128,768]{1,0:T(8,128)(2,1)} %copy-done.2), channel_id=1, source_target_pairs={{0,4},{2,6},{4,0},{6,2},{1,5},{3,7},{5,1},{7,3},{8,12},{10,14},{12... | collective-permute-start | bytes 589832 | tf_op jit(solution)/shard_map/ppermute | solution.py:339
  23.5 1.3 %collective-permute-start.5 = (bf16[128,768]{1,0:T(8,128)(2,1)}, bf16[128,768]{1,0:T(8,128)(2,1)}, u32[]{:S(2)}, u32[]{:S(2)}) collective-permute-start(bf16[128,768]{1,0:T(8,128)(2,1)} %copy-done.2), channel_id=1, source_target_pairs={{0,6},{2,0},{4,2},{6,4},{1,7},{3,1},{5,3},{7,5},{8,14},{10,8},{12,... | collective-permute-start | bytes 589832 | tf_op jit(solution)/shard_map/ppermute | solution.py:339
  24.9 4.4 %all-to-all-done = bf16[8,32,768]{2,1,0:T(8,128)(2,1)S(1)} async-done(((bf16[8,32,768]{2,1,0:T(8,128)(2,1)}), bf16[8,32,768]{2,1,0:T(8,128)(2,1)S(1)}, u32[]{:S(2)}, u32[]{:S(2)}) %all-to-all-start) | async-done | bytes 393248 | tf_op jit(solution)/shard_map/all_to_all | solution.py:348
  29.3 0.8 arrive.3
  30.1 2.1 %collective-permute-done.4.refs_2_ = bf16[128,768]{1,0:T(8,128)(2,1)} collective-permute-done((bf16[128,768]{1,0:T(8,128)(2,1)}, bf16[128,768]{1,0:T(8,128)(2,1)}, u32[]{:S(2)}, u32[]{:S(2)}) %collective-permute-start.4) | collective-permute-done | bytes 196640 | tf_op jit(solution)/shard_map/ppermute | solution.py:339
  32.3 0.5 collective-permute-start.8
  32.8 1.2 join.1.refs_0_
  34.2 0.4 collective-permute-done.7.refs_1_
  34.6 1.1 collective-permute-done.8.refs_3_
  35.7 1.5 %arrive.4 = (bf16[2048,768]{1,0:T(8,128)(2,1)S(1)}, bf16[256,2048]{1,0:T(8,128)(2,1)S(1)}, f32[16,128]{1,0:T(8,128)S(1)}, f32[16,128]{1,0:T(8,128)S(1)}) custom-call(bf16[256,768]{1,0:T(8,128)(2,1)S(1)} %bitcast.15, bf16[512,768]{1,0:T(8,128)(2,1)S(1)} %collective-permute-done.1.refs_0_, bf16[512,768]{1,0:T(8,128)(2,1)S(1)} %collective-permute-done.7.refs_1_, ...), custom_call_target="tpu_custom_call" | custom-call | tf_op jit(solution)/shard_map/arrive/pallas_call | solution.py:186
  37.2 0.9 arrive.5
  38.3 1.0 collective-permute-done.9.b_ref
  39.4 13.4 %all_to_all.66 = f32[16,32,128]{2,1,0:T(8,128)S(1)} all-to-all(f32[16,32,128]{2,1,0:T(8,128)S(1)} %bitcast.23), channel_id=1, replica_groups={{0,2,4,6,8,10,12,14,16,18,20,22,24,26,28,30},{31,29,27,25,23,21,19,17,1..., dimensions={0} | all-to-all | bytes 524288 | tf_op jit(solution)/shard_map/all_to_all | solution.py:348
  52.7 1.9 %sums.2 = bf16[1664,128]{1,0:T(8,128)(2,1)S(1)} custom-call(f32[512,128]{1,0:T(8,128)S(1)} %bitcast.22, bf16[256,1024]{1,0:T(8,128)(2,1)S(1)} %get-tuple-element.52.refs_0_, bf16[256,2048]{1,0:T(8,128)(2,1)S(1)} %get-tuple-element.53.refs_1_, bf16[256,1024]{1,0:T(8,128)(2,1)S(1)} %get-tuple-element.54.refs_2_, f32[8,128]{1,0:T(8,128)S(1)} %get-tuple-element.55.refs_3_, ...), custom_call_target="tpu_custom_call" | custom-call | tf_op jit(solution)/shard_map/sums/pallas_call | solution.py:287
  54.7 16.7 %all_to_all.67 = bf16[8,208,128]{2,1,0:T(8,128)(2,1)S(1)} all-to-all(bf16[8,208,128]{2,1,0:T(8,128)(2,1)S(1)} %bitcast.19), channel_id=1, replica_groups={{0,128,64,192,32,160,96,224},{225,97,161,33,193,65,129,1},{2,130,66,194..., dimensions={0} | all-to-all | bytes 851968 | tf_op jit(solution)/shard_map/all_to_all | solution.py:348
  71.4 0.2 update.2
  71.6 16.1 %all_to_all.68 = bf16[8,32,768]{2,1,0:T(8,128)(2,1)S(1)} all-to-all(bf16[8,32,768]{2,1,0:T(8,128)(2,1)S(1)} %bitcast.26), channel_id=1, replica_groups={{0,128,64,192,32,160,96,224},{225,97,161,33,193,65,129,1},{2,130,66,194..., dimensions={0} | all-to-all | bytes 786432 | tf_op jit(solution)/shard_map/all_to_all | solution.py:348
  87.8 2.1 %score.1 = (bf16[256,1024]{1,0:T(8,128)(2,1)S(1)}, bf16[256,2048]{1,0:T(8,128)(2,1)S(1)}, bf16[256,1024]{1,0:T(8,128)(2,1)S(1)}, f32[8,128]{1,0:T(8,128)S(1)}, f...) custom-call(bf16[256,768]{1,0:T(8,128)(2,1)S(1)} %bitcast.20, ...), custom_call_target="tpu_custom_call" | custom-call | tf_op jit(solution)/shard_map/score/pallas_call | solution.py:212
  90.0 1.2 collective-permute-done.10.b_ref
  91.2 13.5 %all_to_all.69 = f32[16,32,128]{2,1,0:T(8,128)S(1)} all-to-all(f32[16,32,128]{2,1,0:T(8,128)S(1)} %bitcast.24), channel_id=1, replica_groups={{0,2,4,6,8,10,12,14,16,18,20,22,24,26,28,30},{31,29,27,25,23,21,19,17,1..., dimensions={0} | all-to-all | bytes 524288 | tf_op jit(solution)/shard_map/all_to_all | solution.py:348
  104.7 1.9 %sums.3 = (bf16[1664,128]{1,0:T(8,128)(2,1)S(1)}, f32[8,128]{1,0:T(8,128)S(1)}) custom-call(f32[512,128]{1,0:T(8,128)S(1)} %bitcast.21, bf16[256,1024]{1,0:T(8,128)(2,1)S(1)} %get-tuple-element.63.refs_0_, bf16[256,2048]{1,0:T(8,128)(2,1)S(1)} %get-tuple-element.64.refs_1_, bf16[256,1024]{1,0:T(8,128)(2,1)S(1)} %get-tuple-element.65.refs_2_, ...), custom_call_target="tpu_custom_call" | custom-call | tf_op jit(solution)/shard_map/sums/pallas_call | solution.py:287
  106.6 16.5 %all_to_all.70 = bf16[8,208,128]{2,1,0:T(8,128)(2,1)S(1)} all-to-all(bf16[8,208,128]{2,1,0:T(8,128)(2,1)S(1)} %bitcast.25), channel_id=1, replica_groups={{0,128,64,192,32,160,96,224},{225,97,161,33,193,65,129,1},{2,130,66,194..., dimensions={0} | all-to-all | bytes 851968 | tf_op jit(solution)/shard_map/all_to_all | solution.py:348
  123.1 0.9 update.3
  (18 shorter events, 0.7 us)
Async XLA Ops:
  1.6 27.7 %copy-start = (bf16[1024,768]{1,0:T(8,128)(2,1)S(1)}, bf16[1024,768]{1,0:T(8,128)(2,1)}, u32[]{:S(2)}) copy-start(bf16[1024,768]{1,0:T(8,128)(2,1)} %refs_0_.1) | copy-start | bytes 4718596
  1.6 8.3 %collective-permute-start = (bf16[128,768]{1,0:T(8,128)(2,1)S(1)}, bf16[128,768]{1,0:T(8,128)(2,1)S(1)}, u32[]{:S(2)}, u32[]{:S(2)}) collective-permute-start(bf16[128,768]{1,0:T(8,128)(2,1)S(1)} %quarter.1), channel_id=1, source_target_pairs={{0,16},{8,24},{16,0},{24,8},{1,17},{9,25},{17,1},{25,9},{2,18},{10... | collective-permute-start | bytes 589832 | tf_op jit(solution)/shard_map/ppermute | solution.py:339
  6.2 26.0 %collective-permute-start.1 = (bf16[512,768]{1,0:T(8,128)(2,1)}, bf16[512,768]{1,0:T(8,128)(2,1)S(1)}, u32[]{:S(2)}, u32[]{:S(2)}) collective-permute-start(bf16[512,768]{1,0:T(8,128)(2,1)} %get-tuple-element.42), channel_id=1, source_target_pairs={{0,8},{8,16},{16,24},{24,0},{1,9},{9,17},{17,25},{25,1},{2,10},{10... | collective-permute-start | bytes 2359304 | tf_op jit(solution)/shard_map/ppermute | solution.py:339
  7.9 24.3 %collective-permute-start.2 = (bf16[512,768]{1,0:T(8,128)(2,1)}, bf16[512,768]{1,0:T(8,128)(2,1)S(1)}, u32[]{:S(2)}, u32[]{:S(2)}) collective-permute-start(bf16[512,768]{1,0:T(8,128)(2,1)} %get-tuple-element.42), channel_id=1, source_target_pairs={{0,24},{8,0},{16,8},{24,16},{1,25},{9,1},{17,9},{25,17},{2,26},{10... | collective-permute-start | bytes 2359304 | tf_op jit(solution)/shard_map/ppermute | solution.py:339
  9.9 0.7 copy-start.2
  10.6 18.7 %all-to-all-start = ((bf16[8,32,768]{2,1,0:T(8,128)(2,1)}), bf16[8,32,768]{2,1,0:T(8,128)(2,1)S(1)}, u32[]{:S(2)}, u32[]{:S(2)}) async-start(bf16[8,32,768]{2,1,0:T(8,128)(2,1)} %bitcast.27), calls=%async_computation | async-start | bytes 786432 | tf_op jit(solution)/shard_map/all_to_all | solution.py:348
  19.1 11.0 %collective-permute-start.3 = (bf16[128,768]{1,0:T(8,128)(2,1)}, bf16[128,768]{1,0:T(8,128)(2,1)}, u32[]{:S(2)}, u32[]{:S(2)}) collective-permute-start(bf16[128,768]{1,0:T(8,128)(2,1)} %copy-done.2), channel_id=1, source_target_pairs={{0,2},{2,4},{4,6},{6,0},{1,3},{3,5},{5,7},{7,1},{8,10},{10,12},{12... | collective-permute-start | bytes 589832 | tf_op jit(solution)/shard_map/ppermute | solution.py:339
  20.6 11.6 %collective-permute-start.4 = (bf16[128,768]{1,0:T(8,128)(2,1)}, bf16[128,768]{1,0:T(8,128)(2,1)}, u32[]{:S(2)}, u32[]{:S(2)}) collective-permute-start(bf16[128,768]{1,0:T(8,128)(2,1)} %copy-done.2), channel_id=1, source_target_pairs={{0,4},{2,6},{4,0},{6,2},{1,5},{3,7},{5,1},{7,3},{8,12},{10,14},{12... | collective-permute-start | bytes 589832 | tf_op jit(solution)/shard_map/ppermute | solution.py:339
  23.5 8.7 %collective-permute-start.5 = (bf16[128,768]{1,0:T(8,128)(2,1)}, bf16[128,768]{1,0:T(8,128)(2,1)}, u32[]{:S(2)}, u32[]{:S(2)}) collective-permute-start(bf16[128,768]{1,0:T(8,128)(2,1)} %copy-done.2), channel_id=1, source_target_pairs={{0,6},{2,0},{4,2},{6,4},{1,7},{3,1},{5,3},{7,5},{8,14},{10,8},{12,... | collective-permute-start | bytes 589832 | tf_op jit(solution)/shard_map/ppermute | solution.py:339
  29.2 3.6 %copy-start.3 = (bf16[128,768]{1,0:T(8,128)(2,1)S(1)}, bf16[128,768]{1,0:T(8,128)(2,1)}, u32[]{:S(2)}) copy-start(bf16[128,768]{1,0:T(8,128)(2,1)} %copy-done.2) | copy-start | bytes 589828
  32.2 2.4 %collective-permute-start.7 = (bf16[512,768]{1,0:T(8,128)(2,1)S(1)}, bf16[512,768]{1,0:T(8,128)(2,1)S(1)}, u32[]{:S(2)}, u32[]{:S(2)}) collective-permute-start(bf16[512,768]{1,0:T(8,128)(2,1)S(1)} %collective-permute-done.1.refs_0_), channel_id=1, source_target_pairs={{0,1},{1,0},{2,3},{3,2},{4,5},{5,4},{6,7},{7,6},{8,9},{9,8},{10,11... | collective-permute-start | bytes 2359304 | tf_op jit(solution)/shard_map/ppermute | solution.py:339
  32.3 3.4 %collective-permute-start.8 = (bf16[512,768]{1,0:T(8,128)(2,1)S(1)}, bf16[512,768]{1,0:T(8,128)(2,1)S(1)}, u32[]{:S(2)}, u32[]{:S(2)}) collective-permute-start(bf16[512,768]{1,0:T(8,128)(2,1)S(1)} %collective-permute-done.2.refs_2_), channel_id=1, source_target_pairs={{0,1},{1,0},{2,3},{3,2},{4,5},{5,4},{6,7},{7,6},{8,9},{9,8},{10,11... | collective-permute-start | bytes 2359304 | tf_op jit(solution)/shard_map/ppermute | solution.py:339
  34.0 3.2 %collective-permute-start.6 = (bf16[512,768]{1,0:T(8,128)(2,1)S(1)}, bf16[512,768]{1,0:T(8,128)(2,1)S(1)}, u32[]{:S(2)}, u32[]{:S(2)}) collective-permute-start(bf16[512,768]{1,0:T(8,128)(2,1)S(1)} %join.1.refs_0_), channel_id=1, source_target_pairs={{0,1},{1,0},{2,3},{3,2},{4,5},{5,4},{6,7},{7,6},{8,9},{9,8},{10,11... | collective-permute-start | bytes 2359304 | tf_op jit(solution)/shard_map/ppermute | solution.py:339
  38.1 1.3 %collective-permute-start.9 = (f32[32,128]{1,0:T(8,128)S(1)}, f32[32,128]{1,0:T(8,128)S(1)}, u32[]{:S(2)}, u32[]{:S(2)}) collective-permute-start(f32[32,128]{1,0:T(8,128)S(1)} %get-tuple-element.51.a_ref), channel_id=1, source_target_pairs={{0,1},{1,0},{2,3},{3,2},{4,5},{5,4},{6,7},{7,6},{8,9},{9,8},{10,11... | collective-permute-start | bytes 49160 | tf_op jit(solution)/shard_map/ppermute | solution.py:339
  52.7 18.6 %copy-start.1 = (f32[32,768]{1,0:T(8,128)S(1)}, f32[32,768]{1,0:T(8,128)}, u32[]{:S(2)}) copy-start(f32[32,768]{1,0:T(8,128)} %cur_ref.1) | copy-start | bytes 294916
  89.9 1.3 %collective-permute-start.10 = (f32[32,128]{1,0:T(8,128)S(1)}, f32[32,128]{1,0:T(8,128)S(1)}, u32[]{:S(2)}, u32[]{:S(2)}) collective-permute-start(f32[32,128]{1,0:T(8,128)S(1)} %get-tuple-element.62.a_ref), channel_id=1, source_target_pairs={{0,1},{1,0},{2,3},{3,2},{4,5},{5,4},{6,7},{7,6},{8,9},{9,8},{10,11... | collective-permute-start | bytes 49160 | tf_op jit(solution)/shard_map/ppermute | solution.py:339

commit v9 on v8

--- a/solution.py
+++ b/solution.py
@@ -352,7 +352,8 @@
     far = shift(quarter_of(embeddings), "x", X, 2)
     mine, copies = prepare(embeddings, centroids)
     left, right = shift(mine, "x", X, 1), shift(mine, "x", X, 3)
-    quarters = [shift(far, "y", Y, k) for k in range(1, Y)]
+    quarters = {k: shift(far, "y", Y, k) for k in (2, 1, 3)}
+    quarters = [quarters[k] for k in range(1, Y)]
     copies, far = lax.optimization_barrier((copies, far))
     cent = exchange(copies, ("z",), RING)
     own = arrive(cent, PARTS[0], (embeddings,))

time: 124 us -> 124 us (level)
  no operation moved by 1% of the time
where the time goes in v9:
time: 124 us
  blocking collectives  76.1 us (61%)
  starting transfers between devices  19.7 us (16%)
  Pallas kernels  14.8 us (12%)
  waiting for transfers between devices  11.8 us (10%)
    all_to_all x5, blocking collectives, exchange(): lax.all_to_all(v, (*axes, 'c'), 0, 0, axis_index_groups=groups, tiled=True)  76.1 us
    ppermute x11, starting transfers between devices, shift(): return lax.ppermute(v, axis, [(i, (i + k) % size) for i in range(size)])  11.2 us
    all_to_all x1, starting transfers between devices, exchange(): lax.all_to_all(v, (*axes, 'c'), 0, 0, axis_index_groups=groups, tiled=True)  8.47 us
    ppermute x11, waiting for transfers between devices, shift(): return lax.ppermute(v, axis, [(i, (i + k) % size) for i in range(size)])  7.45 us
    all_to_all x1, waiting for transfers between devices, exchange(): lax.all_to_all(v, (*axes, 'c'), 0, 0, axis_index_groups=groups, tiled=True)  4.37 us
    pallas_call x2, Pallas kernels, sums_of(): pl.pallas_call(functools.partial(sum_kernel, last), out_shape=(pltpu.VMEM...  3.86 us
    pallas_call x3, Pallas kernels, arrive(): pl.pallas_call(functools.partial(arrive_kernel, part, len(earlier)), out_...  3.15 us
  transfers between devices with their start and end apart: 12, of which 7 were waited for; matrix products, arithmetic and copies ran while one was open for 0% of the time, Pallas kernels for 5%

profile of v9, /device:TPU:2, one launch (start us, length us, event | category | flops | bytes accessed | tf_op | source)
XLA Modules:
  0.0 124.0 jit_solution(12728846273568449702)
XLA Ops:
  0.6 0.9 quarter.1
  1.6 2.2 %collective-permute-start = (bf16[128,768]{1,0:T(8,128)(2,1)S(1)}, bf16[128,768]{1,0:T(8,128)(2,1)S(1)}, u32[]{:S(2)}, u32[]{:S(2)}) collective-permute-start(bf16[128,768]{1,0:T(8,128)(2,1)S(1)} %quarter.1), channel_id=1, source_target_pairs={{0,16},{8,24},{16,0},{24,8},{1,17},{9,25},{17,1},{25,9},{2,18},{10... | collective-permute-start | bytes 589832 | tf_op jit(solution)/shard_map/ppermute | solution.py:339
  3.8 2.4 %prepare.1 = (bf16[512,768]{1,0:T(8,128)(2,1)}, bf16[256,768]{1,0:T(8,128)(2,1)}) custom-call(bf16[1024,768]{1,0:T(8,128)(2,1)} %refs_0_.1, f32[32,768]{1,0:T(8,128)} %cur_ref.1), custom_call_target="tpu_custom_call" | custom-call | tf_op jit(solution)/shard_map/prepare/pallas_call | solution.py:101
  6.2 1.7 %collective-permute-start.1 = (bf16[512,768]{1,0:T(8,128)(2,1)}, bf16[512,768]{1,0:T(8,128)(2,1)S(1)}, u32[]{:S(2)}, u32[]{:S(2)}) collective-permute-start(bf16[512,768]{1,0:T(8,128)(2,1)} %get-tuple-element.42), channel_id=1, source_target_pairs={{0,8},{8,16},{16,24},{24,0},{1,9},{9,17},{17,25},{25,1},{2,10},{10... | collective-permute-start | bytes 2359304 | tf_op jit(solution)/shard_map/ppermute | solution.py:339
  7.9 0.4 collective-permute-start.2
  8.3 1.6 %collective-permute-done.refs_0_ = bf16[128,768]{1,0:T(8,128)(2,1)S(1)} collective-permute-done((bf16[128,768]{1,0:T(8,128)(2,1)S(1)}, bf16[128,768]{1,0:T(8,128)(2,1)S(1)}, u32[]{:S(2)}, u32[]{:S(2)}) %collective-permute-start) | collective-permute-done | bytes 196640 | tf_op jit(solution)/shard_map/ppermute | solution.py:339
  9.9 0.7 copy-done.2
  10.6 8.5 %all-to-all-start = ((bf16[8,32,768]{2,1,0:T(8,128)(2,1)}), bf16[8,32,768]{2,1,0:T(8,128)(2,1)S(1)}, u32[]{:S(2)}, u32[]{:S(2)}) async-start(bf16[8,32,768]{2,1,0:T(8,128)(2,1)} %bitcast.27), calls=%async_computation | async-start | bytes 786432 | tf_op jit(solution)/shard_map/all_to_all | solution.py:348
  19.1 1.6 %collective-permute-start.3 = (bf16[128,768]{1,0:T(8,128)(2,1)}, bf16[128,768]{1,0:T(8,128)(2,1)}, u32[]{:S(2)}, u32[]{:S(2)}) collective-permute-start(bf16[128,768]{1,0:T(8,128)(2,1)} %copy-done.2), channel_id=1, source_target_pairs={{0,2},{2,4},{4,6},{6,0},{1,3},{3,5},{5,7},{7,1},{8,10},{10,12},{12... | collective-permute-start | bytes 589832 | tf_op jit(solution)/shard_map/ppermute | solution.py:339
  20.6 2.9 %collective-permute-start.4 = (bf16[128,768]{1,0:T(8,128)(2,1)}, bf16[128,768]{1,0:T(8,128)(2,1)}, u32[]{:S(2)}, u32[]{:S(2)}) collective-permute-start(bf16[128,768]{1,0:T(8,128)(2,1)} %copy-done.2), channel_id=1, source_target_pairs={{0,4},{2,6},{4,0},{6,2},{1,5},{3,7},{5,1},{7,3},{8,12},{10,14},{12... | collective-permute-start | bytes 589832 | tf_op jit(solution)/shard_map/ppermute | solution.py:339
  23.5 1.3 %collective-permute-start.5 = (bf16[128,768]{1,0:T(8,128)(2,1)}, bf16[128,768]{1,0:T(8,128)(2,1)}, u32[]{:S(2)}, u32[]{:S(2)}) collective-permute-start(bf16[128,768]{1,0:T(8,128)(2,1)} %copy-done.2), channel_id=1, source_target_pairs={{0,6},{2,0},{4,2},{6,4},{1,7},{3,1},{5,3},{7,5},{8,14},{10,8},{12,... | collective-permute-start | bytes 589832 | tf_op jit(solution)/shard_map/ppermute | solution.py:339
  24.9 4.4 %all-to-all-done = bf16[8,32,768]{2,1,0:T(8,128)(2,1)S(1)} async-done(((bf16[8,32,768]{2,1,0:T(8,128)(2,1)}), bf16[8,32,768]{2,1,0:T(8,128)(2,1)S(1)}, u32[]{:S(2)}, u32[]{:S(2)}) %all-to-all-start) | async-done | bytes 393248 | tf_op jit(solution)/shard_map/all_to_all | solution.py:348
  29.3 0.8 arrive.3
  30.1 2.1 %collective-permute-done.4.refs_2_ = bf16[128,768]{1,0:T(8,128)(2,1)} collective-permute-done((bf16[128,768]{1,0:T(8,128)(2,1)}, bf16[128,768]{1,0:T(8,128)(2,1)}, u32[]{:S(2)}, u32[]{:S(2)}) %collective-permute-start.4) | collective-permute-done | bytes 196640 | tf_op jit(solution)/shard_map/ppermute | solution.py:339
  32.3 0.5 collective-permute-start.8
  32.8 1.2 join.1.refs_0_
  34.2 0.4 collective-permute-done.7.refs_1_
  34.6 1.1 collective-permute-done.8.refs_3_
  35.7 1.5 %arrive.4 = (bf16[2048,768]{1,0:T(8,128)(2,1)S(1)}, bf16[256,2048]{1,0:T(8,128)(2,1)S(1)}, f32[16,128]{1,0:T(8,128)S(1)}, f32[16,128]{1,0:T(8,128)S(1)}) custom-call(bf16[256,768]{1,0:T(8,128)(2,1)S(1)} %bitcast.15, bf16[512,768]{1,0:T(8,128)(2,1)S(1)} %collective-permute-done.1.refs_0_, bf16[512,768]{1,0:T(8,128)(2,1)S(1)} %collective-permute-done.7.refs_1_, ...), custom_call_target="tpu_custom_call" | custom-call | tf_op jit(solution)/shard_map/arrive/pallas_call | solution.py:186
  37.2 0.9 arrive.5
  38.3 1.0 collective-permute-done.9.b_ref
  39.4 13.4 %all_to_all.66 = f32[16,32,128]{2,1,0:T(8,128)S(1)} all-to-all(f32[16,32,128]{2,1,0:T(8,128)S(1)} %bitcast.23), channel_id=1, replica_groups={{0,2,4,6,8,10,12,14,16,18,20,22,24,26,28,30},{31,29,27,25,23,21,19,17,1..., dimensions={0} | all-to-all | bytes 524288 | tf_op jit(solution)/shard_map/all_to_all | solution.py:348
  52.7 1.9 %sums.2 = bf16[1664,128]{1,0:T(8,128)(2,1)S(1)} custom-call(f32[512,128]{1,0:T(8,128)S(1)} %bitcast.22, bf16[256,1024]{1,0:T(8,128)(2,1)S(1)} %get-tuple-element.52.refs_0_, bf16[256,2048]{1,0:T(8,128)(2,1)S(1)} %get-tuple-element.53.refs_1_, bf16[256,1024]{1,0:T(8,128)(2,1)S(1)} %get-tuple-element.54.refs_2_, f32[8,128]{1,0:T(8,128)S(1)} %get-tuple-element.55.refs_3_, ...), custom_call_target="tpu_custom_call" | custom-call | tf_op jit(solution)/shard_map/sums/pallas_call | solution.py:287
  54.7 16.7 %all_to_all.67 = bf16[8,208,128]{2,1,0:T(8,128)(2,1)S(1)} all-to-all(bf16[8,208,128]{2,1,0:T(8,128)(2,1)S(1)} %bitcast.19), channel_id=1, replica_groups={{0,128,64,192,32,160,96,224},{225,97,161,33,193,65,129,1},{2,130,66,194..., dimensions={0} | all-to-all | bytes 851968 | tf_op jit(solution)/shard_map/all_to_all | solution.py:348
  71.4 0.2 update.2
  71.6 16.1 %all_to_all.68 = bf16[8,32,768]{2,1,0:T(8,128)(2,1)S(1)} all-to-all(bf16[8,32,768]{2,1,0:T(8,128)(2,1)S(1)} %bitcast.26), channel_id=1, replica_groups={{0,128,64,192,32,160,96,224},{225,97,161,33,193,65,129,1},{2,130,66,194..., dimensions={0} | all-to-all | bytes 786432 | tf_op jit(solution)/shard_map/all_to_all | solution.py:348
  87.8 2.1 %score.1 = (bf16[256,1024]{1,0:T(8,128)(2,1)S(1)}, bf16[256,2048]{1,0:T(8,128)(2,1)S(1)}, bf16[256,1024]{1,0:T(8,128)(2,1)S(1)}, f32[8,128]{1,0:T(8,128)S(1)}, f...) custom-call(bf16[256,768]{1,0:T(8,128)(2,1)S(1)} %bitcast.20, ...), custom_call_target="tpu_custom_call" | custom-call | tf_op jit(solution)/shard_map/score/pallas_call | solution.py:212
  90.0 1.2 collective-permute-done.10.b_ref
  91.2 13.5 %all_to_all.69 = f32[16,32,128]{2,1,0:T(8,128)S(1)} all-to-all(f32[16,32,128]{2,1,0:T(8,128)S(1)} %bitcast.24), channel_id=1, replica_groups={{0,2,4,6,8,10,12,14,16,18,20,22,24,26,28,30},{31,29,27,25,23,21,19,17,1..., dimensions={0} | all-to-all | bytes 524288 | tf_op jit(solution)/shard_map/all_to_all | solution.py:348
  104.7 1.9 %sums.3 = (bf16[1664,128]{1,0:T(8,128)(2,1)S(1)}, f32[8,128]{1,0:T(8,128)S(1)}) custom-call(f32[512,128]{1,0:T(8,128)S(1)} %bitcast.21, bf16[256,1024]{1,0:T(8,128)(2,1)S(1)} %get-tuple-element.63.refs_0_, bf16[256,2048]{1,0:T(8,128)(2,1)S(1)} %get-tuple-element.64.refs_1_, bf16[256,1024]{1,0:T(8,128)(2,1)S(1)} %get-tuple-element.65.refs_2_, ...), custom_call_target="tpu_custom_call" | custom-call | tf_op jit(solution)/shard_map/sums/pallas_call | solution.py:287
  106.6 16.5 %all_to_all.70 = bf16[8,208,128]{2,1,0:T(8,128)(2,1)S(1)} all-to-all(bf16[8,208,128]{2,1,0:T(8,128)(2,1)S(1)} %bitcast.25), channel_id=1, replica_groups={{0,128,64,192,32,160,96,224},{225,97,161,33,193,65,129,1},{2,130,66,194..., dimensions={0} | all-to-all | bytes 851968 | tf_op jit(solution)/shard_map/all_to_all | solution.py:348
  123.1 0.9 update.3
  (18 shorter events, 0.7 us)
Async XLA Ops:
  1.6 27.7 %copy-start = (bf16[1024,768]{1,0:T(8,128)(2,1)S(1)}, bf16[1024,768]{1,0:T(8,128)(2,1)}, u32[]{:S(2)}) copy-start(bf16[1024,768]{1,0:T(8,128)(2,1)} %refs_0_.1) | copy-start | bytes 4718596
  1.6 8.3 %collective-permute-start = (bf16[128,768]{1,0:T(8,128)(2,1)S(1)}, bf16[128,768]{1,0:T(8,128)(2,1)S(1)}, u32[]{:S(2)}, u32[]{:S(2)}) collective-permute-start(bf16[128,768]{1,0:T(8,128)(2,1)S(1)} %quarter.1), channel_id=1, source_target_pairs={{0,16},{8,24},{16,0},{24,8},{1,17},{9,25},{17,1},{25,9},{2,18},{10... | collective-permute-start | bytes 589832 | tf_op jit(solution)/shard_map/ppermute | solution.py:339
  6.2 26.0 %collective-permute-start.1 = (bf16[512,768]{1,0:T(8,128)(2,1)}, bf16[512,768]{1,0:T(8,128)(2,1)S(1)}, u32[]{:S(2)}, u32[]{:S(2)}) collective-permute-start(bf16[512,768]{1,0:T(8,128)(2,1)} %get-tuple-element.42), channel_id=1, source_target_pairs={{0,8},{8,16},{16,24},{24,0},{1,9},{9,17},{17,25},{25,1},{2,10},{10... | collective-permute-start | bytes 2359304 | tf_op jit(solution)/shard_map/ppermute | solution.py:339
  7.9 24.3 %collective-permute-start.2 = (bf16[512,768]{1,0:T(8,128)(2,1)}, bf16[512,768]{1,0:T(8,128)(2,1)S(1)}, u32[]{:S(2)}, u32[]{:S(2)}) collective-permute-start(bf16[512,768]{1,0:T(8,128)(2,1)} %get-tuple-element.42), channel_id=1, source_target_pairs={{0,24},{8,0},{16,8},{24,16},{1,25},{9,1},{17,9},{25,17},{2,26},{10... | collective-permute-start | bytes 2359304 | tf_op jit(solution)/shard_map/ppermute | solution.py:339
  9.9 0.7 copy-start.2
  10.6 18.7 %all-to-all-start = ((bf16[8,32,768]{2,1,0:T(8,128)(2,1)}), bf16[8,32,768]{2,1,0:T(8,128)(2,1)S(1)}, u32[]{:S(2)}, u32[]{:S(2)}) async-start(bf16[8,32,768]{2,1,0:T(8,128)(2,1)} %bitcast.27), calls=%async_computation | async-start | bytes 786432 | tf_op jit(solution)/shard_map/all_to_all | solution.py:348
  19.1 11.0 %collective-permute-start.3 = (bf16[128,768]{1,0:T(8,128)(2,1)}, bf16[128,768]{1,0:T(8,128)(2,1)}, u32[]{:S(2)}, u32[]{:S(2)}) collective-permute-start(bf16[128,768]{1,0:T(8,128)(2,1)} %copy-done.2), channel_id=1, source_target_pairs={{0,2},{2,4},{4,6},{6,0},{1,3},{3,5},{5,7},{7,1},{8,10},{10,12},{12... | collective-permute-start | bytes 589832 | tf_op jit(solution)/shard_map/ppermute | solution.py:339
  20.6 11.6 %collective-permute-start.4 = (bf16[128,768]{1,0:T(8,128)(2,1)}, bf16[128,768]{1,0:T(8,128)(2,1)}, u32[]{:S(2)}, u32[]{:S(2)}) collective-permute-start(bf16[128,768]{1,0:T(8,128)(2,1)} %copy-done.2), channel_id=1, source_target_pairs={{0,4},{2,6},{4,0},{6,2},{1,5},{3,7},{5,1},{7,3},{8,12},{10,14},{12... | collective-permute-start | bytes 589832 | tf_op jit(solution)/shard_map/ppermute | solution.py:339
  23.5 8.7 %collective-permute-start.5 = (bf16[128,768]{1,0:T(8,128)(2,1)}, bf16[128,768]{1,0:T(8,128)(2,1)}, u32[]{:S(2)}, u32[]{:S(2)}) collective-permute-start(bf16[128,768]{1,0:T(8,128)(2,1)} %copy-done.2), channel_id=1, source_target_pairs={{0,6},{2,0},{4,2},{6,4},{1,7},{3,1},{5,3},{7,5},{8,14},{10,8},{12,... | collective-permute-start | bytes 589832 | tf_op jit(solution)/shard_map/ppermute | solution.py:339
  29.2 3.6 %copy-start.3 = (bf16[128,768]{1,0:T(8,128)(2,1)S(1)}, bf16[128,768]{1,0:T(8,128)(2,1)}, u32[]{:S(2)}) copy-start(bf16[128,768]{1,0:T(8,128)(2,1)} %copy-done.2) | copy-start | bytes 589828
  32.2 2.4 %collective-permute-start.7 = (bf16[512,768]{1,0:T(8,128)(2,1)S(1)}, bf16[512,768]{1,0:T(8,128)(2,1)S(1)}, u32[]{:S(2)}, u32[]{:S(2)}) collective-permute-start(bf16[512,768]{1,0:T(8,128)(2,1)S(1)} %collective-permute-done.1.refs_0_), channel_id=1, source_target_pairs={{0,1},{1,0},{2,3},{3,2},{4,5},{5,4},{6,7},{7,6},{8,9},{9,8},{10,11... | collective-permute-start | bytes 2359304 | tf_op jit(solution)/shard_map/ppermute | solution.py:339
  32.3 3.4 %collective-permute-start.8 = (bf16[512,768]{1,0:T(8,128)(2,1)S(1)}, bf16[512,768]{1,0:T(8,128)(2,1)S(1)}, u32[]{:S(2)}, u32[]{:S(2)}) collective-permute-start(bf16[512,768]{1,0:T(8,128)(2,1)S(1)} %collective-permute-done.2.refs_2_), channel_id=1, source_target_pairs={{0,1},{1,0},{2,3},{3,2},{4,5},{5,4},{6,7},{7,6},{8,9},{9,8},{10,11... | collective-permute-start | bytes 2359304 | tf_op jit(solution)/shard_map/ppermute | solution.py:339
  34.0 3.2 %collective-permute-start.6 = (bf16[512,768]{1,0:T(8,128)(2,1)S(1)}, bf16[512,768]{1,0:T(8,128)(2,1)S(1)}, u32[]{:S(2)}, u32[]{:S(2)}) collective-permute-start(bf16[512,768]{1,0:T(8,128)(2,1)S(1)} %join.1.refs_0_), channel_id=1, source_target_pairs={{0,1},{1,0},{2,3},{3,2},{4,5},{5,4},{6,7},{7,6},{8,9},{9,8},{10,11... | collective-permute-start | bytes 2359304 | tf_op jit(solution)/shard_map/ppermute | solution.py:339
  38.1 1.3 %collective-permute-start.9 = (f32[32,128]{1,0:T(8,128)S(1)}, f32[32,128]{1,0:T(8,128)S(1)}, u32[]{:S(2)}, u32[]{:S(2)}) collective-permute-start(f32[32,128]{1,0:T(8,128)S(1)} %get-tuple-element.51.a_ref), channel_id=1, source_target_pairs={{0,1},{1,0},{2,3},{3,2},{4,5},{5,4},{6,7},{7,6},{8,9},{9,8},{10,11... | collective-permute-start | bytes 49160 | tf_op jit(solution)/shard_map/ppermute | solution.py:339
  52.7 18.6 %copy-start.1 = (f32[32,768]{1,0:T(8,128)S(1)}, f32[32,768]{1,0:T(8,128)}, u32[]{:S(2)}) copy-start(f32[32,768]{1,0:T(8,128)} %cur_ref.1) | copy-start | bytes 294916
  89.9 1.3 %collective-permute-start.10 = (f32[32,128]{1,0:T(8,128)S(1)}, f32[32,128]{1,0:T(8,128)S(1)}, u32[]{:S(2)}, u32[]{:S(2)}) collective-permute-start(f32[32,128]{1,0:T(8,128)S(1)} %get-tuple-element.62.a_ref), channel_id=1, source_target_pairs={{0,1},{1,0},{2,3},{3,2},{4,5},{5,4},{6,7},{7,6},{8,9},{9,8},{10,11... | collective-permute-start | bytes 49160 | tf_op jit(solution)/shard_map/ppermute | solution.py:339

commit v10 on v8

--- a/solution.py
+++ b/solution.py
@@ -22,7 +22,7 @@
 SCALE = 50.0 * math.log2(math.e)
 VMEM = pl.BlockSpec(memory_space=pltpu.VMEM)
 ANY = pl.BlockSpec(memory_space=pl.ANY)
-RING = ((0, 4, 2, 6, 1, 5, 3, 7), (7, 3, 5, 1, 6, 2, 4, 0))
+RING = (tuple(range(Z))[::-1], tuple(range(Z))[::-1])
 PLANE = (tuple(range(X * Y)), tuple(range(X * Y))[::-1])
 PARTS = ((0,), (1, 3), (2,))
 ROWS = tuple(COL * len(part) for part in PARTS)

time: 124 us -> 124 us (level)
  no operation moved by 1% of the time
where the time goes in v10:
time: 124 us; the launch traced here: 123 us
  blocking collectives  75.2 us (61%)
  starting transfers between devices  20.5 us (17%)
  Pallas kernels  14.9 us (12%)
  waiting for transfers between devices  11 us (9%)
    all_to_all x5, blocking collectives, exchange(): lax.all_to_all(v, (*axes, 'c'), 0, 0, axis_index_groups=groups, tiled=True)  75.2 us
    ppermute x11, starting transfers between devices, shift(): return lax.ppermute(v, axis, [(i, (i + k) % size) for i in range(size)])  11.2 us
    all_to_all x1, starting transfers between devices, exchange(): lax.all_to_all(v, (*axes, 'c'), 0, 0, axis_index_groups=groups, tiled=True)  9.25 us
    ppermute x11, waiting for transfers between devices, shift(): return lax.ppermute(v, axis, [(i, (i + k) % size) for i in range(size)])  7.2 us
    pallas_call x2, Pallas kernels, sums_of(): pl.pallas_call(functools.partial(sum_kernel, last), out_shape=(pltpu.VMEM...  3.86 us
    all_to_all x1, waiting for transfers between devices, exchange(): lax.all_to_all(v, (*axes, 'c'), 0, 0, axis_index_groups=groups, tiled=True)  3.82 us
    pallas_call x3, Pallas kernels, arrive(): pl.pallas_call(functools.partial(arrive_kernel, part, len(earlier)), out_...  3.16 us
  transfers between devices with their start and end apart: 12, of which 7 were waited for; matrix products, arithmetic and copies ran while one was open for 0% of the time, Pallas kernels for 5%

profile of v10, /device:TPU:2, one launch (start us, length us, event | category | flops | bytes accessed | tf_op | source)
XLA Modules:
  0.0 123.1 jit_solution(9450691520681803053)
XLA Ops:
  0.6 0.9 quarter.1
  1.6 2.2 %collective-permute-start = (bf16[128,768]{1,0:T(8,128)(2,1)S(1)}, bf16[128,768]{1,0:T(8,128)(2,1)S(1)}, u32[]{:S(2)}, u32[]{:S(2)}) collective-permute-start(bf16[128,768]{1,0:T(8,128)(2,1)S(1)} %quarter.1), channel_id=1, source_target_pairs={{0,16},{8,24},{16,0},{24,8},{1,17},{9,25},{17,1},{25,9},{2,18},{10... | collective-permute-start | bytes 589832 | tf_op jit(solution)/shard_map/ppermute | solution.py:339
  3.8 2.4 %prepare.1 = (bf16[512,768]{1,0:T(8,128)(2,1)}, bf16[256,768]{1,0:T(8,128)(2,1)}) custom-call(bf16[1024,768]{1,0:T(8,128)(2,1)} %refs_0_.1, f32[32,768]{1,0:T(8,128)} %cur_ref.1), custom_call_target="tpu_custom_call" | custom-call | tf_op jit(solution)/shard_map/prepare/pallas_call | solution.py:101
  6.2 1.7 %collective-permute-start.1 = (bf16[512,768]{1,0:T(8,128)(2,1)}, bf16[512,768]{1,0:T(8,128)(2,1)S(1)}, u32[]{:S(2)}, u32[]{:S(2)}) collective-permute-start(bf16[512,768]{1,0:T(8,128)(2,1)} %get-tuple-element.42), channel_id=1, source_target_pairs={{0,8},{8,16},{16,24},{24,0},{1,9},{9,17},{17,25},{25,1},{2,10},{10... | collective-permute-start | bytes 2359304 | tf_op jit(solution)/shard_map/ppermute | solution.py:339
  7.9 0.4 collective-permute-start.2
  8.3 1.6 %collective-permute-done.refs_0_ = bf16[128,768]{1,0:T(8,128)(2,1)S(1)} collective-permute-done((bf16[128,768]{1,0:T(8,128)(2,1)S(1)}, bf16[128,768]{1,0:T(8,128)(2,1)S(1)}, u32[]{:S(2)}, u32[]{:S(2)}) %collective-permute-start) | collective-permute-done | bytes 196640 | tf_op jit(solution)/shard_map/ppermute | solution.py:339
  9.9 0.7 copy-done.2
  10.6 9.2 %all-to-all-start = ((bf16[8,32,768]{2,1,0:T(8,128)(2,1)}), bf16[8,32,768]{2,1,0:T(8,128)(2,1)S(1)}, u32[]{:S(2)}, u32[]{:S(2)}) async-start(bf16[8,32,768]{2,1,0:T(8,128)(2,1)} %bitcast.27), calls=%async_computation | async-start | bytes 786432 | tf_op jit(solution)/shard_map/all_to_all | solution.py:348
  19.8 1.6 %collective-permute-start.3 = (bf16[128,768]{1,0:T(8,128)(2,1)}, bf16[128,768]{1,0:T(8,128)(2,1)}, u32[]{:S(2)}, u32[]{:S(2)}) collective-permute-start(bf16[128,768]{1,0:T(8,128)(2,1)} %copy-done.2), channel_id=1, source_target_pairs={{0,2},{2,4},{4,6},{6,0},{1,3},{3,5},{5,7},{7,1},{8,10},{10,12},{12... | collective-permute-start | bytes 589832 | tf_op jit(solution)/shard_map/ppermute | solution.py:339
  21.4 2.9 %collective-permute-start.4 = (bf16[128,768]{1,0:T(8,128)(2,1)}, bf16[128,768]{1,0:T(8,128)(2,1)}, u32[]{:S(2)}, u32[]{:S(2)}) collective-permute-start(bf16[128,768]{1,0:T(8,128)(2,1)} %copy-done.2), channel_id=1, source_target_pairs={{0,4},{2,6},{4,0},{6,2},{1,5},{3,7},{5,1},{7,3},{8,12},{10,14},{12... | collective-permute-start | bytes 589832 | tf_op jit(solution)/shard_map/ppermute | solution.py:339
  24.3 1.3 %collective-permute-start.5 = (bf16[128,768]{1,0:T(8,128)(2,1)}, bf16[128,768]{1,0:T(8,128)(2,1)}, u32[]{:S(2)}, u32[]{:S(2)}) collective-permute-start(bf16[128,768]{1,0:T(8,128)(2,1)} %copy-done.2), channel_id=1, source_target_pairs={{0,6},{2,0},{4,2},{6,4},{1,7},{3,1},{5,3},{7,5},{8,14},{10,8},{12,... | collective-permute-start | bytes 589832 | tf_op jit(solution)/shard_map/ppermute | solution.py:339
  25.7 3.8 %all-to-all-done = bf16[8,32,768]{2,1,0:T(8,128)(2,1)S(1)} async-done(((bf16[8,32,768]{2,1,0:T(8,128)(2,1)}), bf16[8,32,768]{2,1,0:T(8,128)(2,1)S(1)}, u32[]{:S(2)}, u32[]{:S(2)}) %all-to-all-start) | async-done | bytes 393248 | tf_op jit(solution)/shard_map/all_to_all | solution.py:348
  29.5 0.8 arrive.3
  30.3 1.9 %collective-permute-done.4.refs_2_ = bf16[128,768]{1,0:T(8,128)(2,1)} collective-permute-done((bf16[128,768]{1,0:T(8,128)(2,1)}, bf16[128,768]{1,0:T(8,128)(2,1)}, u32[]{:S(2)}, u32[]{:S(2)}) %collective-permute-start.4) | collective-permute-done | bytes 196640 | tf_op jit(solution)/shard_map/ppermute | solution.py:339
  32.3 0.5 collective-permute-start.8
  32.8 1.2 join.1.refs_0_
  34.2 0.4 collective-permute-done.7.refs_1_
  34.6 1.1 collective-permute-done.8.refs_3_
  35.7 1.5 %arrive.4 = (bf16[2048,768]{1,0:T(8,128)(2,1)S(1)}, bf16[256,2048]{1,0:T(8,128)(2,1)S(1)}, f32[16,128]{1,0:T(8,128)S(1)}, f32[16,128]{1,0:T(8,128)S(1)}) custom-call(bf16[256,768]{1,0:T(8,128)(2,1)S(1)} %bitcast.15, bf16[512,768]{1,0:T(8,128)(2,1)S(1)} %collective-permute-done.1.refs_0_, bf16[512,768]{1,0:T(8,128)(2,1)S(1)} %collective-permute-done.7.refs_1_, ...), custom_call_target="tpu_custom_call" | custom-call | tf_op jit(solution)/shard_map/arrive/pallas_call | solution.py:186
  37.2 0.9 arrive.5
  38.3 1.0 collective-permute-done.9.b_ref
  39.4 13.4 %all_to_all.66 = f32[16,32,128]{2,1,0:T(8,128)S(1)} all-to-all(f32[16,32,128]{2,1,0:T(8,128)S(1)} %bitcast.23), channel_id=1, replica_groups={{0,2,4,6,8,10,12,14,16,18,20,22,24,26,28,30},{31,29,27,25,23,21,19,17,1..., dimensions={0} | all-to-all | bytes 524288 | tf_op jit(solution)/shard_map/all_to_all | solution.py:348
  52.8 1.9 %sums.2 = bf16[1664,128]{1,0:T(8,128)(2,1)S(1)} custom-call(f32[512,128]{1,0:T(8,128)S(1)} %bitcast.22, bf16[256,1024]{1,0:T(8,128)(2,1)S(1)} %get-tuple-element.52.refs_0_, bf16[256,2048]{1,0:T(8,128)(2,1)S(1)} %get-tuple-element.53.refs_1_, bf16[256,1024]{1,0:T(8,128)(2,1)S(1)} %get-tuple-element.54.refs_2_, f32[8,128]{1,0:T(8,128)S(1)} %get-tuple-element.55.refs_3_, ...), custom_call_target="tpu_custom_call" | custom-call | tf_op jit(solution)/shard_map/sums/pallas_call | solution.py:287
  54.7 16.5 %all_to_all.67 = bf16[8,208,128]{2,1,0:T(8,128)(2,1)S(1)} all-to-all(bf16[8,208,128]{2,1,0:T(8,128)(2,1)S(1)} %bitcast.19), channel_id=1, replica_groups={{224,192,160,128,96,64,32,0},{225,193,161,129,97,65,33,1},{226,194,162,..., dimensions={0} | all-to-all | bytes 851968 | tf_op jit(solution)/shard_map/all_to_all | solution.py:348
  71.3 0.2 update.2
  71.5 16.6 %all_to_all.68 = bf16[8,32,768]{2,1,0:T(8,128)(2,1)S(1)} all-to-all(bf16[8,32,768]{2,1,0:T(8,128)(2,1)S(1)} %bitcast.26), channel_id=1, replica_groups={{224,192,160,128,96,64,32,0},{225,193,161,129,97,65,33,1},{226,194,162,..., dimensions={0} | all-to-all | bytes 786432 | tf_op jit(solution)/shard_map/all_to_all | solution.py:348
  88.2 2.1 %score.1 = (bf16[256,1024]{1,0:T(8,128)(2,1)S(1)}, bf16[256,2048]{1,0:T(8,128)(2,1)S(1)}, bf16[256,1024]{1,0:T(8,128)(2,1)S(1)}, f32[8,128]{1,0:T(8,128)S(1)}, f...) custom-call(bf16[256,768]{1,0:T(8,128)(2,1)S(1)} %bitcast.20, ...), custom_call_target="tpu_custom_call" | custom-call | tf_op jit(solution)/shard_map/score/pallas_call | solution.py:212
  90.4 1.2 collective-permute-done.10.b_ref
  91.6 12.5 %all_to_all.69 = f32[16,32,128]{2,1,0:T(8,128)S(1)} all-to-all(f32[16,32,128]{2,1,0:T(8,128)S(1)} %bitcast.24), channel_id=1, replica_groups={{0,2,4,6,8,10,12,14,16,18,20,22,24,26,28,30},{31,29,27,25,23,21,19,17,1..., dimensions={0} | all-to-all | bytes 524288 | tf_op jit(solution)/shard_map/all_to_all | solution.py:348
  104.1 1.9 %sums.3 = (bf16[1664,128]{1,0:T(8,128)(2,1)S(1)}, f32[8,128]{1,0:T(8,128)S(1)}) custom-call(f32[512,128]{1,0:T(8,128)S(1)} %bitcast.21, bf16[256,1024]{1,0:T(8,128)(2,1)S(1)} %get-tuple-element.63.refs_0_, bf16[256,2048]{1,0:T(8,128)(2,1)S(1)} %get-tuple-element.64.refs_1_, bf16[256,1024]{1,0:T(8,128)(2,1)S(1)} %get-tuple-element.65.refs_2_, ...), custom_call_target="tpu_custom_call" | custom-call | tf_op jit(solution)/shard_map/sums/pallas_call | solution.py:287
  106.0 16.2 %all_to_all.70 = bf16[8,208,128]{2,1,0:T(8,128)(2,1)S(1)} all-to-all(bf16[8,208,128]{2,1,0:T(8,128)(2,1)S(1)} %bitcast.25), channel_id=1, replica_groups={{224,192,160,128,96,64,32,0},{225,193,161,129,97,65,33,1},{226,194,162,..., dimensions={0} | all-to-all | bytes 851968 | tf_op jit(solution)/shard_map/all_to_all | solution.py:348
  122.2 0.9 update.3
  (18 shorter events, 0.7 us)
Async XLA Ops:
  1.6 27.9 %copy-start = (bf16[1024,768]{1,0:T(8,128)(2,1)S(1)}, bf16[1024,768]{1,0:T(8,128)(2,1)}, u32[]{:S(2)}) copy-start(bf16[1024,768]{1,0:T(8,128)(2,1)} %refs_0_.1) | copy-start | bytes 4718596
  1.6 8.3 %collective-permute-start = (bf16[128,768]{1,0:T(8,128)(2,1)S(1)}, bf16[128,768]{1,0:T(8,128)(2,1)S(1)}, u32[]{:S(2)}, u32[]{:S(2)}) collective-permute-start(bf16[128,768]{1,0:T(8,128)(2,1)S(1)} %quarter.1), channel_id=1, source_target_pairs={{0,16},{8,24},{16,0},{24,8},{1,17},{9,25},{17,1},{25,9},{2,18},{10... | collective-permute-start | bytes 589832 | tf_op jit(solution)/shard_map/ppermute | solution.py:339
  6.2 26.0 %collective-permute-start.1 = (bf16[512,768]{1,0:T(8,128)(2,1)}, bf16[512,768]{1,0:T(8,128)(2,1)S(1)}, u32[]{:S(2)}, u32[]{:S(2)}) collective-permute-start(bf16[512,768]{1,0:T(8,128)(2,1)} %get-tuple-element.42), channel_id=1, source_target_pairs={{0,8},{8,16},{16,24},{24,0},{1,9},{9,17},{17,25},{25,1},{2,10},{10... | collective-permute-start | bytes 2359304 | tf_op jit(solution)/shard_map/ppermute | solution.py:339
  7.9 24.3 %collective-permute-start.2 = (bf16[512,768]{1,0:T(8,128)(2,1)}, bf16[512,768]{1,0:T(8,128)(2,1)S(1)}, u32[]{:S(2)}, u32[]{:S(2)}) collective-permute-start(bf16[512,768]{1,0:T(8,128)(2,1)} %get-tuple-element.42), channel_id=1, source_target_pairs={{0,24},{8,0},{16,8},{24,16},{1,25},{9,1},{17,9},{25,17},{2,26},{10... | collective-permute-start | bytes 2359304 | tf_op jit(solution)/shard_map/ppermute | solution.py:339
  9.9 0.7 copy-start.2
  10.6 18.9 %all-to-all-start = ((bf16[8,32,768]{2,1,0:T(8,128)(2,1)}), bf16[8,32,768]{2,1,0:T(8,128)(2,1)S(1)}, u32[]{:S(2)}, u32[]{:S(2)}) async-start(bf16[8,32,768]{2,1,0:T(8,128)(2,1)} %bitcast.27), calls=%async_computation | async-start | bytes 786432 | tf_op jit(solution)/shard_map/all_to_all | solution.py:348
  19.8 10.5 %collective-permute-start.3 = (bf16[128,768]{1,0:T(8,128)(2,1)}, bf16[128,768]{1,0:T(8,128)(2,1)}, u32[]{:S(2)}, u32[]{:S(2)}) collective-permute-start(bf16[128,768]{1,0:T(8,128)(2,1)} %copy-done.2), channel_id=1, source_target_pairs={{0,2},{2,4},{4,6},{6,0},{1,3},{3,5},{5,7},{7,1},{8,10},{10,12},{12... | collective-permute-start | bytes 589832 | tf_op jit(solution)/shard_map/ppermute | solution.py:339
  21.4 10.8 %collective-permute-start.4 = (bf16[128,768]{1,0:T(8,128)(2,1)}, bf16[128,768]{1,0:T(8,128)(2,1)}, u32[]{:S(2)}, u32[]{:S(2)}) collective-permute-start(bf16[128,768]{1,0:T(8,128)(2,1)} %copy-done.2), channel_id=1, source_target_pairs={{0,4},{2,6},{4,0},{6,2},{1,5},{3,7},{5,1},{7,3},{8,12},{10,14},{12... | collective-permute-start | bytes 589832 | tf_op jit(solution)/shard_map/ppermute | solution.py:339
  24.3 7.9 %collective-permute-start.5 = (bf16[128,768]{1,0:T(8,128)(2,1)}, bf16[128,768]{1,0:T(8,128)(2,1)}, u32[]{:S(2)}, u32[]{:S(2)}) collective-permute-start(bf16[128,768]{1,0:T(8,128)(2,1)} %copy-done.2), channel_id=1, source_target_pairs={{0,6},{2,0},{4,2},{6,4},{1,7},{3,1},{5,3},{7,5},{8,14},{10,8},{12,... | collective-permute-start | bytes 589832 | tf_op jit(solution)/shard_map/ppermute | solution.py:339
  29.5 3.3 %copy-start.3 = (bf16[128,768]{1,0:T(8,128)(2,1)S(1)}, bf16[128,768]{1,0:T(8,128)(2,1)}, u32[]{:S(2)}) copy-start(bf16[128,768]{1,0:T(8,128)(2,1)} %copy-done.2) | copy-start | bytes 589828
  32.2 2.4 %collective-permute-start.7 = (bf16[512,768]{1,0:T(8,128)(2,1)S(1)}, bf16[512,768]{1,0:T(8,128)(2,1)S(1)}, u32[]{:S(2)}, u32[]{:S(2)}) collective-permute-start(bf16[512,768]{1,0:T(8,128)(2,1)S(1)} %collective-permute-done.1.refs_0_), channel_id=1, source_target_pairs={{0,1},{1,0},{2,3},{3,2},{4,5},{5,4},{6,7},{7,6},{8,9},{9,8},{10,11... | collective-permute-start | bytes 2359304 | tf_op jit(solution)/shard_map/ppermute | solution.py:339
  32.3 3.4 %collective-permute-start.8 = (bf16[512,768]{1,0:T(8,128)(2,1)S(1)}, bf16[512,768]{1,0:T(8,128)(2,1)S(1)}, u32[]{:S(2)}, u32[]{:S(2)}) collective-permute-start(bf16[512,768]{1,0:T(8,128)(2,1)S(1)} %collective-permute-done.2.refs_2_), channel_id=1, source_target_pairs={{0,1},{1,0},{2,3},{3,2},{4,5},{5,4},{6,7},{7,6},{8,9},{9,8},{10,11... | collective-permute-start | bytes 2359304 | tf_op jit(solution)/shard_map/ppermute | solution.py:339
  34.0 3.2 %collective-permute-start.6 = (bf16[512,768]{1,0:T(8,128)(2,1)S(1)}, bf16[512,768]{1,0:T(8,128)(2,1)S(1)}, u32[]{:S(2)}, u32[]{:S(2)}) collective-permute-start(bf16[512,768]{1,0:T(8,128)(2,1)S(1)} %join.1.refs_0_), channel_id=1, source_target_pairs={{0,1},{1,0},{2,3},{3,2},{4,5},{5,4},{6,7},{7,6},{8,9},{9,8},{10,11... | collective-permute-start | bytes 2359304 | tf_op jit(solution)/shard_map/ppermute | solution.py:339
  38.1 1.3 %collective-permute-start.9 = (f32[32,128]{1,0:T(8,128)S(1)}, f32[32,128]{1,0:T(8,128)S(1)}, u32[]{:S(2)}, u32[]{:S(2)}) collective-permute-start(f32[32,128]{1,0:T(8,128)S(1)} %get-tuple-element.51.a_ref), channel_id=1, source_target_pairs={{0,1},{1,0},{2,3},{3,2},{4,5},{5,4},{6,7},{7,6},{8,9},{9,8},{10,11... | collective-permute-start | bytes 49160 | tf_op jit(solution)/shard_map/ppermute | solution.py:339
  52.8 18.5 %copy-start.1 = (f32[32,768]{1,0:T(8,128)S(1)}, f32[32,768]{1,0:T(8,128)}, u32[]{:S(2)}) copy-start(f32[32,768]{1,0:T(8,128)} %cur_ref.1) | copy-start | bytes 294916
  90.3 1.3 %collective-permute-start.10 = (f32[32,128]{1,0:T(8,128)S(1)}, f32[32,128]{1,0:T(8,128)S(1)}, u32[]{:S(2)}, u32[]{:S(2)}) collective-permute-start(f32[32,128]{1,0:T(8,128)S(1)} %get-tuple-element.62.a_ref), channel_id=1, source_target_pairs={{0,1},{1,0},{2,3},{3,2},{4,5},{5,4},{6,7},{7,6},{8,9},{9,8},{10,11... | collective-permute-start | bytes 49160 | tf_op jit(solution)/shard_map/ppermute | solution.py:339
